TPU v7x, 32 devices: a whole 2x2x4 slice. The times are simulated.
32 devices in a mesh: dp: 16 (over z, y, x), tensor: 2 (over core).
Axes of the slice: x: 2, y: 2, z: 4, core: 2. Of those that a mesh axis runs over, the one named last changes fastest.
Arguments:
- features: bfloat16 [16384, 2048], P('dp'), may hold values from -24 to 24
- keep_mask: int32 [16384], P('dp'), may hold values from 0 to 1, as said below
- proj_up: float32 [2048, 4096], P('dp', 'tensor'), may hold values from -0.125 to 0.125
- proj_down: float32 [256, 4096], P('dp', 'tensor'), may hold values from -0.09375 to 0.09375
- proj_norm: float32 [2, 4096], P(None, 'tensor'), may hold values from -1 to 1.4, as said below
- pred_up: float32 [256, 4096], P('dp', 'tensor'), may hold values from -0.375 to 0.375
- pred_down: float32 [256, 4096], P('dp', 'tensor'), may hold values from -0.09375 to 0.09375
- pred_norm: float32 [2, 4096], P(None, 'tensor'), may hold values from -1 to 1.4, as said below
- moment_proj_up: float32 [2048, 4096], P('dp', 'tensor'), may hold values from -0.00015258789 to 0.00015258789
- moment_proj_down: float32 [256, 4096], P('dp', 'tensor'), may hold values from -0.0008544922 to 0.0008544922
- moment_proj_norm: float32 [2, 4096], P(None, 'tensor'), may hold values from -0.00015258789 to 0.00015258789
- moment_pred_up: float32 [256, 4096], P('dp', 'tensor'), may hold values from -0.00024414062 to 0.00024414062
- moment_pred_down: float32 [256, 4096], P('dp', 'tensor'), may hold values from -0.0012207031 to 0.0012207031
- moment_pred_norm: float32 [2, 4096], P(None, 'tensor'), may hold values from -0.000328125 to 0.000328125
- target_up: float32 [2048, 4096], P('dp', 'tensor'), may hold values from -0.125 to 0.125
- target_down: float32 [256, 4096], P('dp', 'tensor'), may hold values from -0.09375 to 0.09375
- target_norm: float32 [2, 4096], P(None, 'tensor'), may hold values from -1 to 1.4, as said below
Outputs:
- loss: float32 [], replicated
- input_grad: float32 [16384, 2048], P('dp', 'tensor')
- proj_up_grad: float32 [2048, 4096], P('dp', 'tensor')
- proj_up_moment: float32 [2048, 4096], P('dp', 'tensor')
- proj_up_next: float32 [2048, 4096], P('dp', 'tensor')
- proj_down_grad: float32 [256, 4096], P('dp', 'tensor')
- proj_down_moment: float32 [256, 4096], P('dp', 'tensor')
- proj_down_next: float32 [256, 4096], P('dp', 'tensor')
- proj_norm_grad: float32 [2, 4096], P(None, 'tensor')
- proj_norm_moment: float32 [2, 4096], P(None, 'tensor')
- proj_norm_next: float32 [2, 4096], P(None, 'tensor')
- pred_up_grad: float32 [256, 4096], P('dp', 'tensor')
- pred_up_moment: float32 [256, 4096], P('dp', 'tensor')
- pred_up_next: float32 [256, 4096], P('dp', 'tensor')
- pred_down_grad: float32 [256, 4096], P('dp', 'tensor')
- pred_down_moment: float32 [256, 4096], P('dp', 'tensor')
- pred_down_next: float32 [256, 4096], P('dp', 'tensor')
- pred_norm_grad: float32 [2, 4096], P(None, 'tensor')
- pred_norm_moment: float32 [2, 4096], P(None, 'tensor')
- pred_norm_next: float32 [2, 4096], P(None, 'tensor')
- target_up_next: float32 [2048, 4096], P('dp', 'tensor')
- target_down_next: float32 [256, 4096], P('dp', 'tensor')
- target_norm_next: float32 [2, 4096], P(None, 'tensor')
Inputs may be any that keep to these rules, and one draw needn't show every extreme that they name: `keep_mask`: 1 marks a view whose loss term counts; the last view always counts. `proj_norm`: row 0 positive. `pred_norm`: row 0 positive. `target_norm`: row 0 positive.
All inputs are finite; a program needn't handle non-finite values.
Results may differ from a plain program's by a relative error of at most 0.022.
Values may be sent and summed in bfloat16 or wider, within the bound.
A program may use at most 192 MiB of HBM per device.

v0:
```python
import math

import jax
import jax.numpy as jnp
from jax import lax
from jax.sharding import PartitionSpec as P

NORM_EPS = 1e-05
UNIT_EPS = 1e-06
RATE_PROJ_UP = 9.0
RATE_PROJ_DOWN = 1.2
RATE_PROJ_NORM = 40.0
RATE_PRED_UP = 18.0
RATE_PRED_DOWN = 0.9
RATE_PRED_NORM = 30.0


def across(matrix, weight):
    return lax.dot_general(
        matrix, weight, (((1,), (1,)), ((), ())), preferred_element_type=jnp.float32
    )


def outer_sum(first_op, second_op):
    return lax.dot_general(
        first_op, second_op, (((0,), (0,)), ((), ())), preferred_element_type=jnp.float32
    )


def standard(hidden, col_sum, col_square, total_views):
    middle_mean = col_sum / total_views
    inverse = lax.rsqrt(col_square / total_views - middle_mean * middle_mean + NORM_EPS)
    return ((hidden - middle_mean) * inverse, inverse)


def norm_back(grad_out, scaled, inverse, params, sum_grad, sum_cross, total_views):
    return (
        params[0]
        * inverse
        * (grad_out - sum_grad / total_views - scaled * (sum_cross / total_views))
    )


def unit_rows(values):
    return values * lax.rsqrt(jnp.sum(values * values, 1, keepdims=True) + UNIT_EPS)


def partner(values):
    width = values.shape[1]
    return values.reshape(-1, 2, width)[:, ::-1, :].reshape(-1, width)


def nesterov(weight, moment, grad, rate):
    fresh = 0.5 * moment + grad
    return (fresh, weight - rate * (grad + 0.5 * fresh))


def body(
    features,
    keep_mask,
    proj_up,
    proj_down,
    proj_norm,
    pred_up,
    pred_down,
    pred_norm,
    moment_proj_up,
    moment_proj_down,
    moment_proj_norm,
    moment_pred_up,
    moment_pred_down,
    moment_pred_norm,
    target_up,
    target_down,
    target_norm,
):
    total_views = float(features.shape[0] * lax.axis_size("dp"))
    up_full, down_full, pup_full, pdown_full, tup_full, tdown_full = (
        lax.all_gather(proj_up.astype(jnp.bfloat16), "dp", axis=0, tiled=True),
        lax.all_gather(proj_down.astype(jnp.bfloat16), "dp", axis=0, tiled=True),
        lax.all_gather(pred_up.astype(jnp.bfloat16), "dp", axis=0, tiled=True),
        lax.all_gather(pred_down.astype(jnp.bfloat16), "dp", axis=0, tiled=True),
        lax.all_gather(target_up.astype(jnp.bfloat16), "dp", axis=0, tiled=True),
        lax.all_gather(target_down.astype(jnp.bfloat16), "dp", axis=0, tiled=True),
    )
    keep_float = keep_mask.astype(jnp.float32)
    hidden1 = jnp.dot(features, up_full, preferred_element_type=jnp.float32)
    target_hidden = jnp.dot(features, tup_full, preferred_element_type=jnp.float32)
    sum_one, square_one, sum_target, square_target, count = lax.psum(
        (
            jnp.sum(hidden1, 0),
            jnp.sum(hidden1 * hidden1, 0),
            jnp.sum(target_hidden, 0),
            jnp.sum(target_hidden * target_hidden, 0),
            jnp.sum(keep_float),
        ),
        "dp",
    )
    scaled1, inverse1 = standard(hidden1, sum_one, square_one, total_views)
    action1, gelu_back1 = jax.vjp(jax.nn.gelu, scaled1 * proj_norm[0] + proj_norm[1])
    action1 = action1.astype(jnp.bfloat16)
    target_scaled, target_inverse = standard(target_hidden, sum_target, square_target, total_views)
    target_action = jax.nn.gelu(target_scaled * target_norm[0] + target_norm[1]).astype(
        jnp.bfloat16
    )
    middle, target_out = (
        lax.psum(across(action1, down_full).astype(jnp.bfloat16), "tensor").astype(jnp.float32),
        lax.psum(across(target_action, tdown_full).astype(jnp.bfloat16), "tensor").astype(
            jnp.float32
        ),
    )
    middle_low = middle.astype(jnp.bfloat16)
    hidden2 = jnp.dot(middle_low, pup_full, preferred_element_type=jnp.float32)
    sum_two, square_two = lax.psum((jnp.sum(hidden2, 0), jnp.sum(hidden2 * hidden2, 0)), "dp")
    scaled2, inverse2 = standard(hidden2, sum_two, square_two, total_views)
    action2, gelu_back2 = jax.vjp(jax.nn.gelu, scaled2 * pred_norm[0] + pred_norm[1])
    action2 = action2.astype(jnp.bfloat16)
    query = lax.psum(across(action2, pdown_full).astype(jnp.bfloat16), "tensor").astype(jnp.float32)
    goal = partner(unit_rows(target_out))

    def loss_terms(values):
        return jnp.sum(keep_float * (2.0 - 2.0 * jnp.sum(unit_rows(values) * goal, 1)))

    local_loss, loss_back = jax.vjp(loss_terms, query)
    loss_total = lax.psum(local_loss, "dp")
    (grad_query,) = loss_back(1.0 / count)
    grad_query = grad_query.astype(jnp.bfloat16)
    grad_pred_down = outer_sum(grad_query, action2)
    (grad_norm2,) = gelu_back2(jnp.dot(grad_query, pdown_full, preferred_element_type=jnp.float32))
    back_sum2, back_cross2 = lax.psum(
        (jnp.sum(grad_norm2, 0), jnp.sum(grad_norm2 * scaled2, 0)), "dp"
    )
    grad_hidden2 = norm_back(
        grad_norm2, scaled2, inverse2, pred_norm, back_sum2, back_cross2, total_views
    ).astype(jnp.bfloat16)
    grad_pred_norm = jnp.stack([back_cross2, back_sum2])
    grad_pred_up = outer_sum(middle_low, grad_hidden2)
    grad_middle = lax.psum(across(grad_hidden2, pup_full).astype(jnp.bfloat16), "tensor")
    grad_proj_down = outer_sum(grad_middle, action1)
    (grad_norm1,) = gelu_back1(jnp.dot(grad_middle, down_full, preferred_element_type=jnp.float32))
    back_sum1, back_cross1 = lax.psum(
        (jnp.sum(grad_norm1, 0), jnp.sum(grad_norm1 * scaled1, 0)), "dp"
    )
    grad_hidden1 = norm_back(
        grad_norm1, scaled1, inverse1, proj_norm, back_sum1, back_cross1, total_views
    ).astype(jnp.bfloat16)
    grad_proj_norm = jnp.stack([back_cross1, back_sum1])
    grad_proj_up = outer_sum(features, grad_hidden1)
    input_grad = lax.psum_scatter(
        across(grad_hidden1, up_full).astype(jnp.bfloat16),
        "tensor",
        scatter_dimension=1,
        tiled=True,
    ).astype(jnp.float32)
    shard_proj_up, shard_proj_down, shard_pred_up, shard_pred_down = (
        lax.psum_scatter(grad_proj_up, "dp", scatter_dimension=0, tiled=True),
        lax.psum_scatter(grad_proj_down, "dp", scatter_dimension=0, tiled=True),
        lax.psum_scatter(grad_pred_up, "dp", scatter_dimension=0, tiled=True),
        lax.psum_scatter(grad_pred_down, "dp", scatter_dimension=0, tiled=True),
    )
    loss = loss_total / count
    scale = math.sqrt(total_views)
    mom_pu, next_pu = nesterov(proj_up, moment_proj_up, shard_proj_up, RATE_PROJ_UP * scale)
    mom_pd, next_pd = nesterov(proj_down, moment_proj_down, shard_proj_down, RATE_PROJ_DOWN * scale)
    mom_pn, next_pn = nesterov(proj_norm, moment_proj_norm, grad_proj_norm, RATE_PROJ_NORM * scale)
    mom_qu, next_qu = nesterov(pred_up, moment_pred_up, shard_pred_up, RATE_PRED_UP * scale)
    mom_qd, next_qd = nesterov(pred_down, moment_pred_down, shard_pred_down, RATE_PRED_DOWN * scale)
    mom_qn, next_qn = nesterov(pred_norm, moment_pred_norm, grad_pred_norm, RATE_PRED_NORM * scale)
    target_up_next = 0.5 * target_up + 0.5 * next_pu
    target_down_next = 0.5 * target_down + 0.5 * next_pd
    target_norm_next = 0.5 * target_norm + 0.5 * next_pn
    return (
        loss,
        input_grad,
        shard_proj_up,
        mom_pu,
        next_pu,
        shard_proj_down,
        mom_pd,
        next_pd,
        grad_proj_norm,
        mom_pn,
        next_pn,
        shard_pred_up,
        mom_qu,
        next_qu,
        shard_pred_down,
        mom_qd,
        next_qd,
        grad_pred_norm,
        mom_qn,
        next_qn,
        target_up_next,
        target_down_next,
        target_norm_next,
    )


def solution(mesh):
    placed = (
        P("dp", None),
        P("dp"),
        P("dp", "tensor"),
        P("dp", "tensor"),
        P(None, "tensor"),
        P("dp", "tensor"),
        P("dp", "tensor"),
        P(None, "tensor"),
        P("dp", "tensor"),
        P("dp", "tensor"),
        P(None, "tensor"),
        P("dp", "tensor"),
        P("dp", "tensor"),
        P(None, "tensor"),
        P("dp", "tensor"),
        P("dp", "tensor"),
        P(None, "tensor"),
    )
    return jax.shard_map(
        body,
        mesh=mesh,
        in_specs=placed,
        out_specs=(
            P(),
            P("dp", "tensor"),
            P("dp", "tensor"),
            P("dp", "tensor"),
            P("dp", "tensor"),
            P("dp", "tensor"),
            P("dp", "tensor"),
            P("dp", "tensor"),
            P(None, "tensor"),
            P(None, "tensor"),
            P(None, "tensor"),
            P("dp", "tensor"),
            P("dp", "tensor"),
            P("dp", "tensor"),
            P("dp", "tensor"),
            P("dp", "tensor"),
            P("dp", "tensor"),
            P(None, "tensor"),
            P(None, "tensor"),
            P(None, "tensor"),
            P("dp", "tensor"),
            P("dp", "tensor"),
            P(None, "tensor"),
        ),
        check_vma=False,
    )
```

profile of v0, /device:TPU:0, one launch (start us, length us, event | category | flops | bytes accessed | tf_op | source)
XLA Modules:
  0.0 1274.9 jit_solution(8194916152034224531)
XLA Ops:
  7.2 2.1 convert_element_type.66
  11.0 2.1 convert_element_type.75
  15.6 111.3 %all-gather.7.cloned.1.call-done = bf16[2048,2048]{1,0:T(8,128)(2,1)} async-done(((bf16[128,2048]{1,0:T(8,128)(2,1)}), bf16[2048,2048]{1,0:T(8,128)(2,1)}) %all-gather.7.cloned.1.call-update) | async-done | bytes 8388624 | tf_op jit(solution)/shard_map/all_gather | solution.py:79
  126.9 14.4 %fusion.40 = (f32[2048]{0:T(1024)S(1)}, f32[2048]{0:T(1024)S(1)}, f32[1024,2048]{1,0:T(8,128)}) fusion(bf16[1024,2048]{1,0:T(8,128)(2,1)} %param.17, bf16[2048,2048]{1,0:T(8,128)(2,1)} %all-gather.7.cloned.1.call-done), kind=kOutput, calls=%fused_computation.100 | convolution fusion | flops 8596221952 | bytes 20987904 | tf_op jit(solution)/shard_map/dot_general | solution.py:87
  141.3 74.6 %all-reduce.3 = (f32[2048]{0:T(1024)S(1)}, f32[2048]{0:T(1024)S(1)}) all-reduce(f32[2048]{0:T(1024)S(1)} %get-tuple-element.53, f32[2048]{0:T(1024)S(1)} %get-tuple-element.52), channel_id=1, replica_groups=mesh['dp'=16,'tensor'=2] {'dp'}, use_global_device_ids=true, to_apply=%region_3.0 | all-reduce | flops 4096 | bytes 32768 | tf_op jit(solution)/shard_map/psum | solution.py:89
  216.0 7.3 multiply_convert_fusion.3
  223.3 4.6 convolution_convert_fusion.3
  230.4 68.7 %all-gather.15.cloned.1.call-done = bf16[2048,2048]{1,0:T(8,128)(2,1)} async-done(((bf16[128,2048]{1,0:T(8,128)(2,1)}), bf16[2048,2048]{1,0:T(8,128)(2,1)}) %all-gather.15.cloned.1.call-update) | async-done | bytes 8388624 | tf_op jit(solution)/shard_map/all_gather | solution.py:83
  299.1 14.4 %fusion.41 = (f32[2048]{0:T(1024)S(1)}, f32[2048]{0:T(1024)S(1)}, f32[1024,2048]{1,0:T(8,128)}) fusion(bf16[1024,2048]{1,0:T(8,128)(2,1)} %param.17, bf16[2048,2048]{1,0:T(8,128)(2,1)} %all-gather.15.cloned.1.call-done), kind=kOutput, calls=%fused_computation.101 | convolution fusion | flops 8596221952 | bytes 20987904 | tf_op jit(solution)/shard_map/dot_general | solution.py:88
  313.5 42.3 %all-gather.11.cloned.1.call-done = bf16[256,2048]{1,0:T(8,128)(2,1)} async-done(((bf16[16,2048]{1,0:T(8,128)(2,1)}), bf16[256,2048]{1,0:T(8,128)(2,1)}) %all-gather.11.cloned.1.call-update) | async-done | bytes 1048592 | tf_op jit(solution)/shard_map/all_gather | solution.py:81
  355.8 20.3 %all-reduce.9.cloned.1.call-done = bf16[1024,256]{1,0:T(8,128)(2,1)} async-done(((bf16[1024,256]{1,0:T(8,128)(2,1)}), bf16[1024,256]{1,0:T(8,128)(2,1)}) %all-reduce.9.cloned.1.call-update) | async-done | bytes 524304 | tf_op jit(solution)/shard_map/psum | solution.py:107
  376.1 5.9 fusion.39
  382.0 78.7 %all-reduce.2 = (f32[2048]{0:T(1024)S(1)}, f32[2048]{0:T(1024)S(1)}, f32[2048]{0:T(1024)S(1)}, f32[2048]{0:T(1024)S(1)}, f32[]{:T(128)}) all-reduce(f32[2048]{0:T(1024)S(1)} %get-tuple-element.51, f32[2048]{0:T(1024)S(1)} %get-tuple-element.50, f32[2048]{0:T(1024)S(1)} %get-tuple-element.55, ...), channel_id=1, replica_groups=mesh['dp'=16,'tensor'=2] {'dp'}, use_global_device_ids=true, to_apply=%region_8.0 | all-reduce | flops 8193 | bytes 65544 | tf_op jit(solution)/shard_map/psum | solution.py:114
  460.8 7.3 multiply_convert_fusion.2
  468.1 4.6 convolution_convert_fusion.2
  472.7 21.7 %all-gather.17.cloned.1.call-done = bf16[256,2048]{1,0:T(8,128)(2,1)} async-done(((bf16[16,2048]{1,0:T(8,128)(2,1)}), bf16[256,2048]{1,0:T(8,128)(2,1)}) %all-gather.17.cloned.1.call-update) | async-done | bytes 1048592 | tf_op jit(solution)/shard_map/all_gather | solution.py:84
  494.3 8.3 fusion.22
  503.9 17.3 %all-reduce.13.cloned.1.call-done = (bf16[1024,256]{1,0:T(8,128)(2,1)}, bf16[1024,256]{1,0:T(8,128)(2,1)}) async-done(((bf16[1024,256]{1,0:T(8,128)(2,1)}, bf16[1024,256]{1,0:T(8,128)(2,1)}), (bf16[1024,256]{1,0:T(8,128)(2,1)}, bf16[1024,256]{1,0:T(8,128)(2,1)})) %all-reduce.13.cloned.1.call-update) | async-done | bytes 1048592 | tf_op jit(solution)/shard_map/psum | solution.py:118
  524.7 2.8 rev.3
  528.3 1.7 fusion.30
  530.0 12.9 %fusion.38 = (f32[2048]{0:T(1024)S(1)}, f32[2048]{0:T(1024)S(1)}, f32[1024,2048]{1,0:T(8,128)}) fusion(f32[2048]{0:T(1024)S(1)} %get-tuple-element.92, f32[1024,2048]{1,0:T(8,128)} %get-tuple-element.104, f32[2048]{0:T(1024)S(1)} %get-tuple-element.100, f32[2048]{0:T(1024)S(1)} %bitcast.46, f32[2048]{0:T(1024)S(1)} %bitcast.42, ...), kind=kOutput, calls=%fused_computation.98 | convolution fusion | flops 1130098688 | bytes 19460096 | tf_op jit(solution)/shard_map/dot_general | solution.py:129
  542.9 77.0 %all-reduce.1 = (f32[2048]{0:T(1024)S(1)}, f32[2048]{0:T(1024)S(1)}) all-reduce(f32[2048]{0:T(1024)S(1)} %get-tuple-element.49, f32[2048]{0:T(1024)S(1)} %get-tuple-element.48), channel_id=1, replica_groups=mesh['dp'=16,'tensor'=2] {'dp'}, use_global_device_ids=true, to_apply=%region_26.0 | all-reduce | flops 4096 | bytes 32768 | tf_op jit(solution)/shard_map/psum | solution.py:130
  620.6 7.1 multiply_convert_fusion.1
  627.7 1.9 copy-done
  629.7 2.1 convolution_convert_fusion.1
  631.8 5.2 fusion.45
  637.3 4.8 fusion.49
  642.8 3.7 all-reduce.11.cloned.1.call-done
  646.5 5.0 fusion.48
  651.6 11.4 fusion.37
  663.1 77.5 %all-reduce = (f32[]{:T(128)}, f32[2048]{0:T(1024)S(1)}, f32[2048]{0:T(1024)S(1)}) all-reduce(f32[]{:T(128)} %multiply_reduce_fusion.5, f32[2048]{0:T(1024)S(1)} %get-tuple-element.47, f32[2048]{0:T(1024)S(1)} %get-tuple-element.46), channel_id=1, replica_groups=mesh['dp'=16,'tensor'=2] {'dp'}, use_global_device_ids=true, to_apply=%region_19.0 | all-reduce | flops 4097 | bytes 32776 | tf_op jit(solution)/shard_map/psum | solution.py:125
  740.6 7.1 multiply_convert_fusion
  747.7 1.9 copy-done.1
  749.7 12.6 convolution_convert_fusion
  762.5 15.2 %convolution_bitcast_fusion = f32[2048,2048]{0,1:T(8,128)} fusion(bf16[1024,2048]{1,0:T(8,128)(2,1)} %copy-done.1, bf16[1024,2048]{1,0:T(8,128)(2,1)} %param.17), kind=kOutput, calls=%fused_computation.5 | convolution fusion | flops 8589934592 | bytes 25165824 | tf_op jit(solution)/shard_map/dot_general | solution.py:25
  780.9 2.5 copy.40
  787.6 1.7 multiply_subtract_fusion.1
  789.2 22.8 %reduce-scatter.12.cloned.1.call-done = f32[16,2048]{1,0:T(8,128)} async-done(((f32[256,2048]{1,0:T(8,128)}), f32[16,2048]{1,0:T(8,128)}) %reduce-scatter.12.cloned.1.call-update) | async-done | bytes 131088 | tf_op jit(solution)/shard_map/reduce_scatter | solution.py:158
  812.0 1.7 multiply_subtract_fusion.2
  813.7 78.7 %reduce-scatter.10.cloned.1.call-done = f32[16,2048]{1,0:T(8,128)} async-done(((f32[256,2048]{1,0:T(8,128)}), f32[16,2048]{1,0:T(8,128)}) %reduce-scatter.10.cloned.1.call-update) | async-done | bytes 131088 | tf_op jit(solution)/shard_map/reduce_scatter | solution.py:157
  892.4 1.8 add_multiply_fusion.1
  894.2 10.5 reduce-scatter.6.cloned.1.call-done
  904.7 4.1 convert_element_type.85
  908.8 345.8 %reduce-scatter.8.cloned.1.call-done = f32[128,2048]{0,1:T(8,128)} async-done(((f32[2048,2048]{0,1:T(8,128)}), f32[128,2048]{0,1:T(8,128)}) %reduce-scatter.8.cloned.1.call-update) | async-done | bytes 1048592 | tf_op jit(solution)/shard_map/reduce_scatter | solution.py:156
  1254.5 3.5 add_multiply_fusion
  1258.1 2.5 copy.46
  1260.6 2.5 copy.45
  1263.1 2.5 copy.44
  (102 shorter events, 20.5 us)
Async XLA Ops:
  7.2 119.7 %all-gather.7.cloned.1.call-start = ((), (), s32[]{:S(2)}) async-start(), calls=%async_computation.5 | async-start | bytes 8912896 | tf_op jit(solution)/shard_map/all_gather | solution.py:79
  9.3 214.0 %all-gather.9.cloned.1.call-start = ((), (), s32[]{:S(2)}) async-start(), calls=%async_computation.6 | async-start | bytes 1114112 | tf_op jit(solution)/shard_map/all_gather | solution.py:80
  11.0 288.1 %all-gather.15.cloned.1.call-start = ((), (), s32[]{:S(2)}) async-start(), calls=%async_computation.10 | async-start | bytes 8912896 | tf_op jit(solution)/shard_map/all_gather | solution.py:83
  13.1 342.7 %all-gather.11.cloned.1.call-start = ((), (), s32[]{:S(2)}) async-start(), calls=%async_computation.8 | async-start | bytes 1114112 | tf_op jit(solution)/shard_map/all_gather | solution.py:81
  14.7 361.4 %all-reduce.9.cloned.1.call-start = ((), (), s32[]{:S(2)}) async-start(), calls=%async_computation.7 | async-start | bytes 1048576 | tf_op jit(solution)/shard_map/psum | solution.py:107
  216.0 12.0 copy-start.7
  216.0 12.8 %copy-start.11 = (f32[16,2048]{1,0:T(8,128)S(1)}, f32[16,2048]{1,0:T(8,128)}, u32[]{:S(2)}) copy-start(f32[16,2048]{1,0:T(8,128)} %param.32) | copy-start | bytes 393220
  216.0 13.7 %copy-start.15 = (s32[1024]{0:T(1024)S(1)}, s32[1024]{0:T(1024)}, u32[]{:S(2)}) copy-start(s32[1024]{0:T(1024)} %param.18) | copy-start | bytes 12292
  216.0 14.3 %copy-start.12 = (f32[2,2048]{1,0:T(2,128)S(1)}, f32[2,2048]{1,0:T(2,128)}, u32[]{:S(2)}) copy-start(f32[2,2048]{1,0:T(2,128)} %param.24) | copy-start | bytes 49156
  216.0 14.4 %copy-start.14 = (f32[2,2048]{1,0:T(2,128)S(1)}, f32[2,2048]{1,0:T(2,128)}, u32[]{:S(2)}) copy-start(f32[2,2048]{1,0:T(2,128)} %param.33) | copy-start | bytes 49156
  227.9 240.1 %all-gather.13.cloned.1.call-start = ((), (), s32[]{:S(2)}) async-start(), calls=%async_computation.9 | async-start | bytes 1114112 | tf_op jit(solution)/shard_map/all_gather | solution.py:82
  228.7 265.7 %all-gather.17.cloned.1.call-start = ((), (), s32[]{:S(2)}) async-start(), calls=%async_computation.11 | async-start | bytes 1114112 | tf_op jit(solution)/shard_map/all_gather | solution.py:84
  229.4 291.9 %all-reduce.13.cloned.1.call-start = ((), (), s32[]{:S(2)}) async-start(), calls=%async_computation.18 | async-start | bytes 2097152 | tf_op jit(solution)/shard_map/psum | solution.py:118
  502.7 143.9 %all-reduce.11.cloned.1.call-start = ((), (), s32[]{:S(2)}) async-start(), calls=%async_computation.12 | async-start | bytes 1048576 | tf_op jit(solution)/shard_map/psum | solution.py:138
  620.0 0.6 copy-start.17
  620.0 7.8 copy-start.16
  620.6 9.1 copy-start.5
  627.7 1.9 copy-start
  629.7 2.2 copy-start.4
  629.7 7.6 copy-start.6
  631.8 155.8 %reduce-scatter.14.cloned.1.call-start = ((), (), s32[]{:S(2)}) async-start(), calls=%async_computation.17 | async-start | bytes 2228224 | tf_op jit(solution)/shard_map/reduce_scatter | solution.py:159
  637.0 14.6 %copy-start.20 = (bf16[256,2048]{1,0:T(8,128)(2,1)S(1)}, bf16[256,2048]{1,0:T(8,128)(2,1)}, u32[]{:S(2)}) copy-start(bf16[256,2048]{1,0:T(8,128)(2,1)} %all-gather.9.cloned.1.call-done) | copy-start | bytes 3145732
  637.0 175.0 %reduce-scatter.12.cloned.1.call-start = ((), (), s32[]{:S(2)}) async-start(), calls=%async_computation.16 | async-start | bytes 2228224 | tf_op jit(solution)/shard_map/reduce_scatter | solution.py:158
  642.1 250.3 %reduce-scatter.10.cloned.1.call-start = ((), (), s32[]{:S(2)}) async-start(), calls=%async_computation.15 | async-start | bytes 2228224 | tf_op jit(solution)/shard_map/reduce_scatter | solution.py:157
  646.5 5.1 copy-start.21
  651.6 253.1 %reduce-scatter.6.cloned.1.call-start = ((), (), s32[]{:S(2)}) async-start(), calls=%async_computation.13 | async-start | bytes 6291456 | tf_op jit(solution)/shard_map/reduce_scatter | solution.py:149
  740.6 7.1 copy-start.18
  740.6 7.1 copy-start.19
  747.7 1.9 copy-start.1
  762.3 492.3 %reduce-scatter.8.cloned.1.call-start = ((), (), s32[]{:S(2)}) async-start(), calls=%async_computation.14 | async-start | bytes 17825792 | tf_op jit(solution)/shard_map/reduce_scatter | solution.py:156
  777.7 1.2 copy-start.3
  777.7 5.7 copy-start.13
  777.7 9.8 copy-start.8
  777.8 34.3 %copy-start.9 = (f32[16,2048]{1,0:T(8,128)S(1)}, f32[16,2048]{1,0:T(8,128)}, u32[]{:S(2)}) copy-start(f32[16,2048]{1,0:T(8,128)} %param.22) | copy-start | bytes 393220
  777.8 114.7 %copy-start.10 = (f32[16,2048]{1,0:T(8,128)S(1)}, f32[16,2048]{1,0:T(8,128)}, u32[]{:S(2)}) copy-start(f32[16,2048]{1,0:T(8,128)} %param.20) | copy-start | bytes 393220
  1254.5 11.1 copy-start.2
Sparse Core Ops, SparseCore 0:
  11.4 115.5 all-gather.6
  130.3 53.7 all-gather.8
  187.4 111.6 all-gather.14
  302.3 53.4 all-gather.10
  358.6 17.5 all-reduce.8
  379.7 56.7 all-gather.12
  440.2 54.0 all-gather.16
  502.8 18.4 all-reduce.12
  631.9 14.5 all-reduce.10
  649.3 81.7 reduce-scatter.13
  734.0 77.9 reduce-scatter.11
  814.8 77.5 reduce-scatter.9
  895.4 9.2 reduce-scatter.5
  906.9 347.6 reduce-scatter.7
where the time goes:
time: 1290 us; the launch traced here: 1270 us
  waiting for transfers between devices  743 us (58%)
  blocking collectives  308 us (24%)
  matrix products  121 us (9%)
  other arithmetic  58.8 us (5%)
  local copies, waits for them, and re-layouts  24 us (2%)
  between operations  17.7 us (1%)
    reduce_scatter x1, waiting for transfers between devices, body(): lax.psum_scatter(grad_proj_up, 'dp', scatter_dimension=0, tiled=True)  346 us
    all_gather x1, waiting for transfers between devices, body(): lax.all_gather(proj_up.astype(jnp.bfloat16), 'dp', axis=0, tiled=True)  111 us
    psum x1, blocking collectives, body(): lax.psum((jnp.sum(hidden2, 0), jnp.sum(hidden2 * hidden2, 0)), 'dp')  78.7 us
    reduce_scatter x1, waiting for transfers between devices, body(): lax.psum_scatter(grad_proj_down, 'dp', scatter_dimension=0, tiled=True)  78.7 us
    psum x1, blocking collectives, body(): loss_total = lax.psum(local_loss, 'dp')  77.5 us
    psum x1, blocking collectives, body(): lax.psum((jnp.sum(grad_norm2, 0), jnp.sum(grad_norm2 * scaled2, 0)), 'dp')  77 us
    psum x1, blocking collectives, body(): lax.psum((jnp.sum(hidden1, 0), jnp.sum(hidden1 * hidden1, 0), jnp.sum(tar...  74.6 us
    all_gather x1, waiting for transfers between devices, body(): lax.all_gather(target_up.astype(jnp.bfloat16), 'dp', axis=0, tiled=True)  68.7 us
  transfers between devices with their start and end apart: 14, of which 11 were waited for; matrix products, arithmetic and copies ran while one was open for 11% of the time, Pallas kernels for 0%

commit v1 on v0

--- a/solution.py
+++ b/solution.py
@@ -75,27 +75,34 @@
     target_norm,
 ):
     total_views = float(features.shape[0] * lax.axis_size("dp"))
-    up_full, down_full, pup_full, pdown_full, tup_full, tdown_full = (
-        lax.all_gather(proj_up.astype(jnp.bfloat16), "dp", axis=0, tiled=True),
-        lax.all_gather(proj_down.astype(jnp.bfloat16), "dp", axis=0, tiled=True),
-        lax.all_gather(pred_up.astype(jnp.bfloat16), "dp", axis=0, tiled=True),
-        lax.all_gather(pred_down.astype(jnp.bfloat16), "dp", axis=0, tiled=True),
-        lax.all_gather(target_up.astype(jnp.bfloat16), "dp", axis=0, tiled=True),
-        lax.all_gather(target_down.astype(jnp.bfloat16), "dp", axis=0, tiled=True),
+    width = proj_up.shape[1]
+
+    def gathered(parts):
+        low = jnp.stack([part.astype(jnp.bfloat16) for part in parts])
+        full = lax.all_gather(low, "dp", axis=1, tiled=True)
+        return tuple(full[i] for i in range(len(parts)))
+
+    (up_full, tup_full) = gathered((proj_up, target_up))
+    (down_full, pup_full, pdown_full, tdown_full) = gathered(
+        (proj_down, pred_up, pred_down, target_down)
     )
     keep_float = keep_mask.astype(jnp.float32)
     hidden1 = jnp.dot(features, up_full, preferred_element_type=jnp.float32)
     target_hidden = jnp.dot(features, tup_full, preferred_element_type=jnp.float32)
-    sum_one, square_one, sum_target, square_target, count = lax.psum(
-        (
-            jnp.sum(hidden1, 0),
-            jnp.sum(hidden1 * hidden1, 0),
-            jnp.sum(target_hidden, 0),
-            jnp.sum(target_hidden * target_hidden, 0),
-            jnp.sum(keep_float),
+    sums = lax.psum(
+        jnp.stack(
+            [
+                jnp.sum(hidden1, 0),
+                jnp.sum(hidden1 * hidden1, 0),
+                jnp.sum(target_hidden, 0),
+                jnp.sum(target_hidden * target_hidden, 0),
+                jnp.full((width,), jnp.sum(keep_float)),
+            ]
         ),
         "dp",
     )
+    sum_one, square_one, sum_target, square_target = sums[0], sums[1], sums[2], sums[3]
+    count = sums[4, 0]
     scaled1, inverse1 = standard(hidden1, sum_one, square_one, total_views)
     action1, gelu_back1 = jax.vjp(jax.nn.gelu, scaled1 * proj_norm[0] + proj_norm[1])
     action1 = action1.astype(jnp.bfloat16)
@@ -111,7 +118,9 @@
     )
     middle_low = middle.astype(jnp.bfloat16)
     hidden2 = jnp.dot(middle_low, pup_full, preferred_element_type=jnp.float32)
-    sum_two, square_two = lax.psum((jnp.sum(hidden2, 0), jnp.sum(hidden2 * hidden2, 0)), "dp")
+    sum_two, square_two = lax.psum(
+        jnp.stack([jnp.sum(hidden2, 0), jnp.sum(hidden2 * hidden2, 0)]), "dp"
+    )
     scaled2, inverse2 = standard(hidden2, sum_two, square_two, total_views)
     action2, gelu_back2 = jax.vjp(jax.nn.gelu, scaled2 * pred_norm[0] + pred_norm[1])
     action2 = action2.astype(jnp.bfloat16)
@@ -122,14 +131,21 @@
         return jnp.sum(keep_float * (2.0 - 2.0 * jnp.sum(unit_rows(values) * goal, 1)))
 
     local_loss, loss_back = jax.vjp(loss_terms, query)
-    loss_total = lax.psum(local_loss, "dp")
     (grad_query,) = loss_back(1.0 / count)
     grad_query = grad_query.astype(jnp.bfloat16)
     grad_pred_down = outer_sum(grad_query, action2)
     (grad_norm2,) = gelu_back2(jnp.dot(grad_query, pdown_full, preferred_element_type=jnp.float32))
-    back_sum2, back_cross2 = lax.psum(
-        (jnp.sum(grad_norm2, 0), jnp.sum(grad_norm2 * scaled2, 0)), "dp"
-    )
+    back_sum2, back_cross2, loss_row = lax.psum(
+        jnp.stack(
+            [
+                jnp.sum(grad_norm2, 0),
+                jnp.sum(grad_norm2 * scaled2, 0),
+                jnp.full((width,), local_loss),
+            ]
+        ),
+        "dp",
+    )
+    loss_total = loss_row[0]
     grad_hidden2 = norm_back(
         grad_norm2, scaled2, inverse2, pred_norm, back_sum2, back_cross2, total_views
     ).astype(jnp.bfloat16)
@@ -139,7 +155,7 @@
     grad_proj_down = outer_sum(grad_middle, action1)
     (grad_norm1,) = gelu_back1(jnp.dot(grad_middle, down_full, preferred_element_type=jnp.float32))
     back_sum1, back_cross1 = lax.psum(
-        (jnp.sum(grad_norm1, 0), jnp.sum(grad_norm1 * scaled1, 0)), "dp"
+        jnp.stack([jnp.sum(grad_norm1, 0), jnp.sum(grad_norm1 * scaled1, 0)]), "dp"
     )
     grad_hidden1 = norm_back(
         grad_norm1, scaled1, inverse1, proj_norm, back_sum1, back_cross1, total_views
@@ -152,12 +168,16 @@
         scatter_dimension=1,
         tiled=True,
     ).astype(jnp.float32)
-    shard_proj_up, shard_proj_down, shard_pred_up, shard_pred_down = (
-        lax.psum_scatter(grad_proj_up, "dp", scatter_dimension=0, tiled=True),
-        lax.psum_scatter(grad_proj_down, "dp", scatter_dimension=0, tiled=True),
-        lax.psum_scatter(grad_pred_up, "dp", scatter_dimension=0, tiled=True),
-        lax.psum_scatter(grad_pred_down, "dp", scatter_dimension=0, tiled=True),
-    )
+    shard_proj_up = lax.psum_scatter(
+        grad_proj_up.astype(jnp.bfloat16), "dp", scatter_dimension=0, tiled=True
+    ).astype(jnp.float32)
+    small = lax.psum_scatter(
+        jnp.stack([grad_proj_down, grad_pred_up, grad_pred_down]).astype(jnp.bfloat16),
+        "dp",
+        scatter_dimension=1,
+        tiled=True,
+    ).astype(jnp.float32)
+    shard_proj_down, shard_pred_up, shard_pred_down = small[0], small[1], small[2]
     loss = loss_total / count
     scale = math.sqrt(total_views)
     mom_pu, next_pu = nesterov(proj_up, moment_proj_up, shard_proj_up, RATE_PROJ_UP * scale)

time: 1290 us -> 924 us (0.72)
  waiting for transfers between devices: 743 us -> 373 us
  local copies, waits for them, and re-layouts: 24 us -> 41.8 us
    reduce_scatter x4 -> x1, waiting for transfers between devices: 447 us -> 0.01 us  [body(): lax.psum_scatter(jnp.stack([grad_proj_down, grad_pred_up, grad_pred_down]...]
    unnamed x14 -> x9, waiting for transfers between devices: 0.26 us -> 156 us
    all_gather x6 -> x2, waiting for transfers between devices: 244 us -> 191 us  [gathered(): full = lax.all_gather(low, 'dp', axis=1, tiled=True)]
    unnamed x51 -> x45, local copies, waits for them, and re-layouts: 19 us -> 33.7 us
    psum x1, waiting for transfers between devices: 20.3 us -> 5.67 us  [body(): lax.psum(across(action1, down_full).astype(jnp.bfloat16), 'tensor')]
  transfers between devices with their start and end apart: 14 -> 8, of which waited for: 11 -> 5; matrix products, arithmetic and copies ran while one was open for 11% -> 14% of each run, Pallas kernels for 0% -> 0%
where the time goes in v1:
time: 924 us; the launch traced here: 913 us
  waiting for transfers between devices  373 us (40%)
  blocking collectives  306 us (33%)
  matrix products  115 us (12%)
  other arithmetic  57.9 us (6%)
  local copies, waits for them, and re-layouts  41.8 us (5%)
  between operations  18.1 us (2%)
    all_gather x2, waiting for transfers between devices, gathered(): full = lax.all_gather(low, 'dp', axis=1, tiled=True)  191 us
    unnamed x9, waiting for transfers between devices  156 us
    psum x1, blocking collectives, body(): lax.psum(jnp.stack([jnp.sum(grad_norm1, 0), jnp.sum(grad_norm1 * scaled1,...  77.5 us
    psum x1, blocking collectives, body(): lax.psum(jnp.stack([jnp.sum(hidden2, 0), jnp.sum(hidden2 * hidden2, 0)]),...  77 us
    psum x1, blocking collectives, body(): lax.psum(jnp.stack([jnp.sum(grad_norm2, 0), jnp.sum(grad_norm2 * scaled2,...  77 us
    psum x1, blocking collectives, body(): lax.psum(jnp.stack([jnp.sum(hidden1, 0), jnp.sum(hidden1 * hidden1, 0), j...  74.8 us
    unnamed x45, local copies, waits for them, and re-layouts  33.7 us
    dot_general x5, matrix products, across(): lax.dot_general(matrix, weight, (((1,), (1,)), ((), ())), preferred_eleme...  32.4 us
  transfers between devices with their start and end apart: 8, of which 5 were waited for; matrix products, arithmetic and copies ran while one was open for 14% of the time, Pallas kernels for 0%

profile of v1, /device:TPU:0, one launch (start us, length us, event | category | flops | bytes accessed | tf_op | source)
XLA Modules:
  0.0 913.4 jit_solution(7391022365718388882)
XLA Ops:
  7.2 1.7 convert_bitcast_fusion.1
  12.9 1.3 convert_reduce_fusion
  15.0 190.8 %all-gather.3.cloned.1.call-done = bf16[2,2048,2048]{2,1,0:T(8,128)(2,1)} async-done(((bf16[2,128,2048]{2,1,0:T(8,128)(2,1)}), bf16[2,2048,2048]{2,1,0:T(8,128)(2,1)}) %all-gather.3.cloned.1.call-update) | async-done | bytes 16777232 | tf_op jit(solution)/shard_map/all_gather | solution.py:82
  205.8 14.6 %multiply_reduce_fusion.2 = (f32[2048]{0:T(1024)S(1)}, f32[2048]{0:T(1024)S(1)}, f32[2048,1024]{0,1:T(8,128)}) fusion(bf16[1024,2048]{1,0:T(8,128)(2,1)} %param.17, bf16[2,2048,2048]{2,1,0:T(8,128)(2,1)} %all-gather.3.cloned.1.call-done), kind=kOutput, calls=%fused_computation.45 | convolution fusion | flops 8596221952 | bytes 20987904 | tf_op jit(solution)/shard_map/dot_general | solution.py:91
  220.4 11.0 %multiply_reduce_fusion.3 = (f32[2048]{0:T(1024)S(1)}, f32[2048]{0:T(1024)S(1)}, f32[2048,1024]{0,1:T(8,128)}) fusion(bf16[1024,2048]{1,0:T(8,128)(2,1)S(1)} %copy-done.16, bf16[2,2048,2048]{2,1,0:T(8,128)(2,1)S(1)} %copy-done.15), kind=kOutput, calls=%fused_computation.46 | convolution fusion | flops 8596221952 | bytes 20987904 | tf_op jit(solution)/shard_map/dot_general | solution.py:90
  232.1 74.8 %psum.56 = f32[5,2048]{1,0:T(8,128)S(1)} all-reduce(f32[5,2048]{1,0:T(8,128)S(1)} %stack.95), channel_id=1, replica_groups=mesh['dp'=16,'tensor'=2] {'dp'}, use_global_device_ids=true, to_apply=%region_5.0 | all-reduce | flops 10240 | bytes 81920 | tf_op jit(solution)/shard_map/psum | solution.py:92
  307.0 7.2 multiply_convert_fusion.2
  314.3 4.6 convolution_convert_fusion.5
  319.4 8.6 fusion.34
  327.9 5.7 all-reduce.5.cloned.1.call-done
  333.6 5.9 fusion.53
  339.5 77.0 %psum.59 = f32[2,2048]{1,0:T(2,128)S(1)} all-reduce(f32[2,2048]{1,0:T(2,128)S(1)} %pad_maximum_fusion.3), channel_id=1, replica_groups=mesh['dp'=16,'tensor'=2] {'dp'}, use_global_device_ids=true, to_apply=%region_11.0 | all-reduce | flops 4096 | bytes 32768 | tf_op jit(solution)/shard_map/psum | solution.py:121
  416.6 5.9 multiply_convert_fusion.1
  422.5 1.9 copy-done
  424.4 3.3 convolution_convert_fusion.4
  429.2 14.2 %all-reduce.9.cloned.1.call-done = (bf16[1024,256]{1,0:T(8,128)(2,1)}, bf16[1024,256]{1,0:T(8,128)(2,1)}) async-done(((bf16[1024,256]{1,0:T(8,128)(2,1)}, bf16[1024,256]{1,0:T(8,128)(2,1)}), (bf16[1024,256]{1,0:T(8,128)(2,1)}, bf16[1024,256]{1,0:T(8,128)(2,1)})) %all-reduce.9.cloned.1.call-update) | async-done | bytes 1048592 | tf_op jit(solution)/shard_map/psum | solution.py:127
  444.7 1.3 fusion.37
  447.9 2.8 rev.3
  451.4 1.8 fusion.42
  454.6 12.4 %fusion.52 = (f32[2048]{0:T(1024)S(1)}, f32[2048]{0:T(1024)S(1)}, f32[1024,2048]{1,0:T(8,128)}) fusion(f32[2048]{0:T(1024)S(1)} %bitcast.134, f32[1024,2048]{1,0:T(8,128)} %get-tuple-element.134, f32[2048]{0:T(1024)S(1)} %bitcast.137, f32[2048]{0:T(1024)S(1)} %bitcast.149, f32[2048]{0:T(1024)S(1)} %bitcast.147, ...), kind=kOutput, calls=%fused_computation.140 | convolution fusion | flops 1130098688 | bytes 19460096 | tf_op jit(solution)/shard_map/dot_general | solution.py:137
  467.1 77.0 %psum.61 = f32[3,2048]{1,0:T(4,128)S(1)} all-reduce(f32[3,2048]{1,0:T(4,128)S(1)} %maximum_maximum_fusion), channel_id=1, replica_groups=mesh['dp'=16,'tensor'=2] {'dp'}, use_global_device_ids=true, to_apply=%region_19.0 | all-reduce | flops 6144 | bytes 49152 | tf_op jit(solution)/shard_map/psum | solution.py:138
  544.7 7.1 multiply_convert_fusion
  551.8 2.0 copy-done.1
  553.8 3.4 convolution_convert_fusion.3
  557.5 3.6 fusion.32
  561.1 4.6 fusion.33
  565.7 6.2 all-reduce.7.cloned.1.call-done
  572.0 3.7 fusion.31
  575.6 3.2 pad_maximum_fusion
  578.9 11.9 %fusion.51 = (f32[2048]{0:T(1024)S(1)}, f32[2048]{0:T(1024)S(1)}, f32[1024,2048]{1,0:T(8,128)}) fusion(f32[2048]{0:T(1024)S(1)} %bitcast.140, f32[2048,1024]{0,1:T(8,128)} %get-tuple-element.132, f32[2048]{0:T(1024)S(1)} %bitcast.143, f32[2048]{0:T(1024)S(1)} %bitcast.160, f32[2048]{0:T(1024)S(1)} %bitcast.158, bf16[1024,256]{1,0:T(8,128)(2,1)S(1)} %copy-done.17, ...), kind=kOutput, calls=%fused_computation.139 | convolution fusion | flops 1128263680 | bytes 18399232 | tf_op jit(solution)/shard_map/dot_general | solution.py:156
  590.9 77.5 %psum.63 = f32[2,2048]{1,0:T(2,128)S(1)} all-reduce(f32[2,2048]{1,0:T(2,128)S(1)} %pad_maximum_fusion.4), channel_id=1, replica_groups=mesh['dp'=16,'tensor'=2] {'dp'}, use_global_device_ids=true, to_apply=%region_23.0 | all-reduce | flops 4096 | bytes 32768 | tf_op jit(solution)/shard_map/psum | solution.py:157
  669.0 7.0 fusion.25
  676.0 1.9 copy-done.2
  678.0 12.6 %fusion.30 = bf16[1024,2048]{1,0:T(8,128)(2,1)} fusion(bf16[1024,2048]{1,0:T(8,128)(2,1)S(1)} %fusion.25, bf16[2,2048,2048]{2,1,0:T(8,128)(2,1)} %all-gather.3.cloned.1.call-done), kind=kOutput, calls=%fused_computation.50 | convolution fusion | flops 8592031744 | bytes 16777216 | tf_op jit(solution)/shard_map/dot_general | solution.py:19
  690.9 14.7 %convert_bitcast_fusion = bf16[2048,2048]{0,1:T(8,128)(2,1)} fusion(bf16[1024,2048]{1,0:T(8,128)(2,1)} %copy-done.2, bf16[1024,2048]{1,0:T(8,128)(2,1)} %param.17), kind=kOutput, calls=%fused_computation.36 | convolution fusion | flops 8594128896 | bytes 16777216 | tf_op jit(solution)/shard_map/dot_general | solution.py:25
  705.6 12.3 %copy.54 = bf16[2048,2048]{1,0:T(8,128)(2,1)} copy(bf16[2048,2048]{0,1:T(8,128)(2,1)} %convert_bitcast_fusion) | data formatting | bytes 16777216
  719.5 1.3 copy.49
  720.8 2.6 copy.47
  725.9 1.4 multiply_subtract_fusion.4
  727.3 1.4 add_multiply_fusion.2
  729.7 2.2 multiply_subtract_fusion.1
  731.9 4.1 convert_element_type.98
  736.0 155.8 %reduce-scatter.10.cloned.1.call-done = bf16[128,2048]{1,0:T(8,128)(2,1)} async-done(((bf16[2048,2048]{1,0:T(8,128)(2,1)}), bf16[128,2048]{1,0:T(8,128)(2,1)}) %reduce-scatter.10.cloned.1.call-update) | async-done | bytes 524304
  891.8 1.3 copy.55
  894.3 3.1 add_multiply_fusion
  897.4 2.5 copy.53
  900.0 2.5 copy.52
  902.5 2.5 copy.51
  (81 shorter events, 18.9 us)
Async XLA Ops:
  7.2 198.6 %all-gather.3.cloned.1.call-start = ((), (), s32[]{:S(2)}) async-start(), calls=%async_computation.3 | async-start | bytes 17825792 | tf_op jit(solution)/shard_map/all_gather | solution.py:82
  10.0 304.2 %all-gather.5.cloned.1.call-start = ((), (), s32[]{:S(2)}) async-start(), calls=%async_computation.4 | async-start | bytes 4456448 | tf_op jit(solution)/shard_map/all_gather | solution.py:82
  12.8 320.8 %all-reduce.5.cloned.1.call-start = ((), (), s32[]{:S(2)}) async-start(), calls=%async_computation.5 | async-start | bytes 1048576 | tf_op jit(solution)/shard_map/psum | solution.py:114
  205.8 14.6 %copy-start.15 = (bf16[2,2048,2048]{2,1,0:T(8,128)(2,1)S(1)}, bf16[2,2048,2048]{2,1,0:T(8,128)(2,1)}, u32[]{:S(2)}) copy-start(bf16[2,2048,2048]{2,1,0:T(8,128)(2,1)} %all-gather.3.cloned.1.call-done) | copy-start | bytes 50331652
  205.8 14.6 %copy-start.16 = (bf16[1024,2048]{1,0:T(8,128)(2,1)S(1)}, bf16[1024,2048]{1,0:T(8,128)(2,1)}, u32[]{:S(2)}) copy-start(bf16[1024,2048]{1,0:T(8,128)(2,1)} %param.17) | copy-start | bytes 12582916
  220.4 86.6 %copy-start.13 = (f32[2,2048]{1,0:T(2,128)S(1)}, f32[2,2048]{1,0:T(2,128)}, u32[]{:S(2)}) copy-start(f32[2,2048]{1,0:T(2,128)} %param.21) | copy-start | bytes 49156
  318.9 124.6 %all-reduce.9.cloned.1.call-start = ((), (), s32[]{:S(2)}) async-start(), calls=%async_computation.10 | async-start | bytes 2097152 | tf_op jit(solution)/shard_map/psum | solution.py:127
  327.9 88.6 %copy-start.12 = (f32[2,2048]{1,0:T(2,128)S(1)}, f32[2,2048]{1,0:T(2,128)}, u32[]{:S(2)}) copy-start(f32[2,2048]{1,0:T(2,128)} %param.24) | copy-start | bytes 49156
  422.5 1.9 copy-start
  424.4 4.8 copy-start.14
  427.8 144.2 %all-reduce.7.cloned.1.call-start = ((), (), s32[]{:S(2)}) async-start(), calls=%async_computation.6 | async-start | bytes 1048576 | tf_op jit(solution)/shard_map/psum | solution.py:154
  544.1 0.6 copy-start.11
  551.8 2.0 copy-start.1
  553.8 3.7 copy-start.7
  553.8 7.3 copy-start.6
  557.2 171.5 %reduce-scatter.8.cloned.1.call-start = ((), (), s32[]{:S(2)}) async-start(), calls=%async_computation.8 | async-start | bytes 3342336 | tf_op jit(solution)/shard_map/reduce_scatter | solution.py:174
  572.0 6.9 copy-start.17
  578.9 153.1 %reduce-scatter.6.cloned.1.call-start = ((), (), s32[]{:S(2)}) async-start(), calls=%async_computation.7 | async-start | bytes 6291456 | tf_op jit(solution)/shard_map/reduce_scatter | solution.py:165
  676.0 1.9 copy-start.2
  690.6 201.2 %reduce-scatter.10.cloned.1.call-start = ((), (), s32[]{:S(2)}) async-start(), calls=%async_computation.9 | async-start | bytes 8912896
  717.9 1.2 copy-start.3
  717.9 1.6 copy-start.4
  717.9 11.8 %copy-start.8 = (f32[16,2048]{1,0:T(8,128)S(1)}, f32[16,2048]{1,0:T(8,128)}, u32[]{:S(2)}) copy-start(f32[16,2048]{1,0:T(8,128)} %param.32) | copy-start | bytes 393220
  717.9 11.8 %copy-start.9 = (f32[16,2048]{1,0:T(8,128)S(1)}, f32[16,2048]{1,0:T(8,128)}, u32[]{:S(2)}) copy-start(f32[16,2048]{1,0:T(8,128)} %param.23) | copy-start | bytes 393220
  717.9 11.8 %copy-start.10 = (f32[16,2048]{1,0:T(8,128)S(1)}, f32[16,2048]{1,0:T(8,128)}, u32[]{:S(2)}) copy-start(f32[16,2048]{1,0:T(8,128)} %param.22) | copy-start | bytes 393220
  720.8 173.5 %copy-start.5 = (f32[128,2048]{0,1:T(8,128)S(1)}, f32[128,2048]{0,1:T(8,128)}, u32[]{:S(2)}) copy-start(f32[128,2048]{0,1:T(8,128)} %copy.49) | copy-start | bytes 3145732
Sparse Core Ops, SparseCore 0:
  11.4 194.3 all-gather.2
  209.1 75.3 all-gather.4
  319.0 14.5 all-reduce.4
  427.9 15.5 all-reduce.8
  557.3 14.5 all-reduce.6
  579.0 85.6 reduce-scatter.7
  690.7 7.8 reduce-scatter.5
  718.1 173.6 reduce-scatter.9

commit v2 on v1

v2 whole, which is shorter than its diff:
```python
import functools
import math

import jax
import jax.numpy as jnp
from jax import lax
from jax.experimental import pallas as pl
from jax.experimental.pallas import tpu as pltpu
from jax.sharding import PartitionSpec as P

NORM_EPS = 1e-05
UNIT_EPS = 1e-06
RATE_PROJ_UP = 9.0
RATE_PROJ_DOWN = 1.2
RATE_PROJ_NORM = 40.0
RATE_PRED_UP = 18.0
RATE_PRED_DOWN = 0.9
RATE_PRED_NORM = 30.0


def across(matrix, weight):
    return lax.dot_general(
        matrix, weight, (((1,), (1,)), ((), ())), preferred_element_type=jnp.float32
    )


def outer_sum(first_op, second_op):
    return lax.dot_general(
        first_op, second_op, (((0,), (0,)), ((), ())), preferred_element_type=jnp.float32
    )


def standard(hidden, col_sum, col_square, total_views):
    middle_mean = col_sum / total_views
    inverse = lax.rsqrt(col_square / total_views - middle_mean * middle_mean + NORM_EPS)
    return ((hidden - middle_mean) * inverse, inverse)


def norm_back(grad_out, scaled, inverse, params, sum_grad, sum_cross, total_views):
    return (
        params[0]
        * inverse
        * (grad_out - sum_grad / total_views - scaled * (sum_cross / total_views))
    )


def unit_rows(values):
    return values * lax.rsqrt(jnp.sum(values * values, 1, keepdims=True) + UNIT_EPS)


def partner(values):
    width = values.shape[1]
    return values.reshape(-1, 2, width)[:, ::-1, :].reshape(-1, width)


def nesterov(weight, moment, grad, rate):
    fresh = 0.5 * moment + grad
    return (fresh, weight - rate * (grad + 0.5 * fresh))


def finish(
    total_views,
    args,
    loss,
    input_grad,
    shard_proj_up,
    shard_proj_down,
    grad_proj_norm,
    shard_pred_up,
    shard_pred_down,
    grad_pred_norm,
):
    (proj_up, proj_down, proj_norm, pred_up, pred_down, pred_norm) = args[2:8]
    (
        moment_proj_up,
        moment_proj_down,
        moment_proj_norm,
        moment_pred_up,
        moment_pred_down,
        moment_pred_norm,
        target_up,
        target_down,
        target_norm,
    ) = args[8:]
    scale = math.sqrt(total_views)
    mom_pu, next_pu = nesterov(proj_up, moment_proj_up, shard_proj_up, RATE_PROJ_UP * scale)
    mom_pd, next_pd = nesterov(proj_down, moment_proj_down, shard_proj_down, RATE_PROJ_DOWN * scale)
    mom_pn, next_pn = nesterov(proj_norm, moment_proj_norm, grad_proj_norm, RATE_PROJ_NORM * scale)
    mom_qu, next_qu = nesterov(pred_up, moment_pred_up, shard_pred_up, RATE_PRED_UP * scale)
    mom_qd, next_qd = nesterov(pred_down, moment_pred_down, shard_pred_down, RATE_PRED_DOWN * scale)
    mom_qn, next_qn = nesterov(pred_norm, moment_pred_norm, grad_pred_norm, RATE_PRED_NORM * scale)
    target_up_next = 0.5 * target_up + 0.5 * next_pu
    target_down_next = 0.5 * target_down + 0.5 * next_pd
    target_norm_next = 0.5 * target_norm + 0.5 * next_pn
    return (
        loss,
        input_grad,
        shard_proj_up,
        mom_pu,
        next_pu,
        shard_proj_down,
        mom_pd,
        next_pd,
        grad_proj_norm,
        mom_pn,
        next_pn,
        shard_pred_up,
        mom_qu,
        next_qu,
        shard_pred_down,
        mom_qd,
        next_qd,
        grad_pred_norm,
        mom_qn,
        next_qn,
        target_up_next,
        target_down_next,
        target_norm_next,
    )


def plain_body(
    features,
    keep_mask,
    proj_up,
    proj_down,
    proj_norm,
    pred_up,
    pred_down,
    pred_norm,
    moment_proj_up,
    moment_proj_down,
    moment_proj_norm,
    moment_pred_up,
    moment_pred_down,
    moment_pred_norm,
    target_up,
    target_down,
    target_norm,
):
    total_views = float(features.shape[0] * lax.axis_size("dp"))
    width = proj_up.shape[1]

    def gathered(parts):
        low = jnp.stack([part.astype(jnp.bfloat16) for part in parts])
        full = lax.all_gather(low, "dp", axis=1, tiled=True)
        return tuple(full[i] for i in range(len(parts)))

    (up_full, tup_full) = gathered((proj_up, target_up))
    (down_full, pup_full, pdown_full, tdown_full) = gathered(
        (proj_down, pred_up, pred_down, target_down)
    )
    keep_float = keep_mask.astype(jnp.float32)
    hidden1 = jnp.dot(features, up_full, preferred_element_type=jnp.float32)
    target_hidden = jnp.dot(features, tup_full, preferred_element_type=jnp.float32)
    sums = lax.psum(
        jnp.stack(
            [
                jnp.sum(hidden1, 0),
                jnp.sum(hidden1 * hidden1, 0),
                jnp.sum(target_hidden, 0),
                jnp.sum(target_hidden * target_hidden, 0),
                jnp.full((width,), jnp.sum(keep_float)),
            ]
        ),
        "dp",
    )
    sum_one, square_one, sum_target, square_target = sums[0], sums[1], sums[2], sums[3]
    count = sums[4, 0]
    scaled1, inverse1 = standard(hidden1, sum_one, square_one, total_views)
    action1, gelu_back1 = jax.vjp(jax.nn.gelu, scaled1 * proj_norm[0] + proj_norm[1])
    action1 = action1.astype(jnp.bfloat16)
    target_scaled, target_inverse = standard(target_hidden, sum_target, square_target, total_views)
    target_action = jax.nn.gelu(target_scaled * target_norm[0] + target_norm[1]).astype(
        jnp.bfloat16
    )
    middle, target_out = (
        lax.psum(across(action1, down_full).astype(jnp.bfloat16), "tensor").astype(jnp.float32),
        lax.psum(across(target_action, tdown_full).astype(jnp.bfloat16), "tensor").astype(
            jnp.float32
        ),
    )
    middle_low = middle.astype(jnp.bfloat16)
    hidden2 = jnp.dot(middle_low, pup_full, preferred_element_type=jnp.float32)
    sum_two, square_two = lax.psum(
        jnp.stack([jnp.sum(hidden2, 0), jnp.sum(hidden2 * hidden2, 0)]), "dp"
    )
    scaled2, inverse2 = standard(hidden2, sum_two, square_two, total_views)
    action2, gelu_back2 = jax.vjp(jax.nn.gelu, scaled2 * pred_norm[0] + pred_norm[1])
    action2 = action2.astype(jnp.bfloat16)
    query = lax.psum(across(action2, pdown_full).astype(jnp.bfloat16), "tensor").astype(jnp.float32)
    goal = partner(unit_rows(target_out))

    def loss_terms(values):
        return jnp.sum(keep_float * (2.0 - 2.0 * jnp.sum(unit_rows(values) * goal, 1)))

    local_loss, loss_back = jax.vjp(loss_terms, query)
    (grad_query,) = loss_back(1.0 / count)
    grad_query = grad_query.astype(jnp.bfloat16)
    grad_pred_down = outer_sum(grad_query, action2)
    (grad_norm2,) = gelu_back2(jnp.dot(grad_query, pdown_full, preferred_element_type=jnp.float32))
    back_sum2, back_cross2, loss_row = lax.psum(
        jnp.stack(
            [
                jnp.sum(grad_norm2, 0),
                jnp.sum(grad_norm2 * scaled2, 0),
                jnp.full((width,), local_loss),
            ]
        ),
        "dp",
    )
    loss_total = loss_row[0]
    grad_hidden2 = norm_back(
        grad_norm2, scaled2, inverse2, pred_norm, back_sum2, back_cross2, total_views
    ).astype(jnp.bfloat16)
    grad_pred_norm = jnp.stack([back_cross2, back_sum2])
    grad_pred_up = outer_sum(middle_low, grad_hidden2)
    grad_middle = lax.psum(across(grad_hidden2, pup_full).astype(jnp.bfloat16), "tensor")
    grad_proj_down = outer_sum(grad_middle, action1)
    (grad_norm1,) = gelu_back1(jnp.dot(grad_middle, down_full, preferred_element_type=jnp.float32))
    back_sum1, back_cross1 = lax.psum(
        jnp.stack([jnp.sum(grad_norm1, 0), jnp.sum(grad_norm1 * scaled1, 0)]), "dp"
    )
    grad_hidden1 = norm_back(
        grad_norm1, scaled1, inverse1, proj_norm, back_sum1, back_cross1, total_views
    ).astype(jnp.bfloat16)
    grad_proj_norm = jnp.stack([back_cross1, back_sum1])
    grad_proj_up = outer_sum(features, grad_hidden1)
    input_grad = lax.psum_scatter(
        across(grad_hidden1, up_full).astype(jnp.bfloat16),
        "tensor",
        scatter_dimension=1,
        tiled=True,
    ).astype(jnp.float32)
    shard_proj_up = lax.psum_scatter(
        grad_proj_up.astype(jnp.bfloat16), "dp", scatter_dimension=0, tiled=True
    ).astype(jnp.float32)
    small = lax.psum_scatter(
        jnp.stack([grad_proj_down, grad_pred_up, grad_pred_down]).astype(jnp.bfloat16),
        "dp",
        scatter_dimension=1,
        tiled=True,
    ).astype(jnp.float32)
    shard_proj_down, shard_pred_up, shard_pred_down = small[0], small[1], small[2]
    loss = loss_total / count
    return finish(
        total_views,
        (
            features,
            keep_mask,
            proj_up,
            proj_down,
            proj_norm,
            pred_up,
            pred_down,
            pred_norm,
            moment_proj_up,
            moment_proj_down,
            moment_proj_norm,
            moment_pred_up,
            moment_pred_down,
            moment_pred_norm,
            target_up,
            target_down,
            target_norm,
        ),
        loss,
        input_grad,
        shard_proj_up,
        shard_proj_down,
        grad_proj_norm,
        shard_pred_up,
        shard_pred_down,
        grad_pred_norm,
    )


MESH = pl.DeviceIdType.MESH
GRIDS = {16: (4, 2, 2)}
TILE = 256
GELU_A = math.sqrt(2.0 / math.pi)
GELU_B = 0.044715
ALONG_LAST = (0, ((0, 2, 1), (0, 1, 2)))
ACROSS_FIRST = (1, ((2, 1, 0), (1, 2, 0)))
Z_AHEAD = 2
VMEM_LIMIT = 63 * 1024 * 1024


def loop(count, step):
    def one(i, carry):
        step(i)
        return carry

    lax.fori_loop(0, count, one, 0)


def nt_dot(first_op, second_op):
    return lax.dot_general(
        first_op, second_op, (((1,), (1,)), ((), ())), preferred_element_type=jnp.float32
    )


def tn_dot(first_op, second_op):
    return lax.dot_general(
        first_op, second_op, (((0,), (0,)), ((), ())), preferred_element_type=jnp.float32
    )


def gelu_tanh(value):
    return jnp.tanh(GELU_A * (value + GELU_B * value * value * value))


def step_kernel(
    grid,
    total_views,
    x_hbm,
    pu_hbm,
    tu_hbm,
    pd_hbm,
    qu_hbm,
    qd_hbm,
    td_hbm,
    proj_norm,
    pred_norm,
    target_norm,
    keep,
    ig_hbm,
    gu_out,
    gs_out,
    proj_stat,
    pred_stat,
    loss_out,
    feats,
    up,
    tup,
    small,
    act1,
    hat1,
    act2,
    hat2,
    wide,
    tact,
    acc,
    ex,
    exr,
    sr1,
    sr2,
    sr3,
    inv1,
    inv2,
    pa,
    pb,
    qa,
    qb,
    load_sem,
    ag_s,
    ag_r,
    ps_s,
    ps_r,
    qs_s,
    qs_r,
    ex_s,
    ex_r,
    rs_s,
    rs_r,
    ss_s,
    ss_r,
    ig_s,
    ig_r,
    ready,
):
    n0, n1, n2 = grid
    plane = n1 * n2
    views, width = wide.shape
    rows = up.shape[3]
    small_rows = small.shape[4]
    blocks = views // rows
    chunk = width // 4
    half = width // 2
    dp = lax.axis_index("dp")
    core = lax.axis_index("tensor")
    me = (dp // plane, (dp // n2) % n1, dp % n2)
    mp = dp % plane
    other = (dp, 1 - core)

    def place(index):
        return ((index[0] * n1 + index[1]) * n2 + index[2], core)

    def moved(axis, k):
        target = list(me)
        target[axis] = (me[axis] + k) % grid[axis]
        return tuple(target)

    barrier = pltpu.get_barrier_semaphore()
    greet = [place(moved(0, k)) for k in range(1, n0)]
    greet += [(me[0] * plane + (mp + k) % plane, core) for k in range(1, plane)]
    greet.append(other)
    for device in greet:
        pl.semaphore_signal(barrier, inc=1, device_id=device, device_id_type=MESH)

    loads = [
        pltpu.make_async_copy(src, wide.at[pl.ds(start, src.shape[0])], load_sem.at[i])
        for i, (src, start) in enumerate(
            (
                (pd_hbm, 2 * rows),
                (qu_hbm, 2 * rows + small_rows),
                (qd_hbm, 2 * rows + 2 * small_rows),
                (td_hbm, 2 * rows + 3 * small_rows),
                (pu_hbm, 0),
                (tu_hbm, rows),
            )
        )
    ]
    loads.append(pltpu.make_async_copy(x_hbm, feats, load_sem.at[6]))
    for load in loads:
        load.start()
    for load in loads[:4]:
        load.wait()
    for w in range(4):
        small[w, me[0], me[1], me[2]] = wide[
            pl.ds(2 * rows + w * small_rows, small_rows), :
        ].astype(jnp.bfloat16)
    loads[4].wait()
    up[me[0], me[1], me[2]] = wide[pl.ds(0, rows), :].astype(jnp.bfloat16)
    loads[5].wait()
    tup[me[0], me[1], me[2]] = wide[pl.ds(rows, rows), :].astype(jnp.bfloat16)
    pl.semaphore_wait(barrier, len(greet))

    base = (0, n0 - 1, n0 - 1 + n1 - 1)
    chunks = [("small", 0, ALONG_LAST)]
    chunks += [("up", i, ALONG_LAST) for i in range(4)]
    chunks += [("small", 1, ACROSS_FIRST)]
    chunks += [("target", i, ALONG_LAST) for i in range(4)]

    def gather_copies(c, lane, phase):
        kind, index, (_, orders) = chunks[c]
        order = orders[lane]
        axis = order[phase]
        sel = [slice(None) if b in order[:phase] else me[b] for b in range(3)]
        if kind == "small":
            ref = small.at[
                pl.ds(2 * index, 2), sel[0], sel[1], sel[2], :, pl.ds(lane * half, half)
            ]
        else:
            buffer = up if kind == "up" else tup
            ref = buffer.at[
                sel[0], sel[1], sel[2], :, pl.ds(index * chunk + lane * TILE, TILE)
            ]
        return [
            pltpu.make_async_remote_copy(
                src_ref=ref,
                dst_ref=ref,
                send_sem=ag_s.at[c, lane, base[axis] + k - 1],
                recv_sem=ag_r.at[c, lane, base[axis] + k - 1],
                device_id=place(moved(axis, k)),
                device_id_type=MESH,
            )
            for k in range(1, grid[axis])
        ]

    def gather_start(c, phase):
        for lane in range(2):
            if phase:
                for copy in gather_copies(c, lane, phase - 1):
                    copy.wait_recv()
            for copy in gather_copies(c, lane, phase):
                copy.start()

    def gather_end(c):
        for lane in range(2):
            for copy in gather_copies(c, lane, 2):
                copy.wait_recv()

    def sum_copies(buffers, i, stage):
        first, second, send, recv = buffers
        if stage == 0:
            ref = first.at[i, mp]
            return [
                pltpu.make_async_remote_copy(
                    src_ref=ref,
                    dst_ref=ref,
                    send_sem=send.at[i, k - 1],
                    recv_sem=recv.at[i, k - 1],
                    device_id=(me[0] * plane + (mp + k) % plane, core),
                    device_id_type=MESH,
                )
                for k in range(1, plane)
            ]
        ref = second.at[i, me[0]]
        return [
            pltpu.make_async_remote_copy(
                src_ref=ref,
                dst_ref=ref,
                send_sem=send.at[i, plane - 1 + k - 1],
                recv_sem=recv.at[i, plane - 1 + k - 1],
                device_id=place(moved(0, k)),
                device_id_type=MESH,
            )
            for k in range(1, n0)
        ]

    narrow_sum = (pa, pb, ps_s, ps_r)
    whole_sum = (qa, qb, qs_s, qs_r)

    def sum_start(buffers, i):
        for copy in sum_copies(buffers, i, 0):
            copy.start()

    def sum_middle(buffers, i):
        for copy in sum_copies(buffers, i, 0):
            copy.wait()
        first, second = buffers[:2]
        total = first[i, 0]
        for j in range(1, plane):
            total = total + first[i, j]
        second[i, me[0]] = total
        for copy in sum_copies(buffers, i, 1):
            copy.start()

    def sum_end(buffers, i):
        for copy in sum_copies(buffers, i, 1):
            copy.wait()
        second = buffers[1]
        total = second[i, 0]
        for j in range(1, n0):
            total = total + second[i, j]
        return total

    def swap(i):
        return pltpu.make_async_remote_copy(
            src_ref=ex.at[i],
            dst_ref=exr.at[i],
            send_sem=ex_s.at[i],
            recv_sem=ex_r.at[i],
            device_id=other,
            device_id_type=MESH,
        )

    def swap_end(i):
        swap(i).wait()

        def add(b):
            part = pl.ds(pl.multiple_of(b * rows, rows), rows)
            ex[i, part, :] = (
                ex[i, part, :].astype(jnp.float32) + exr[i, part, :].astype(jnp.float32)
            ).astype(jnp.bfloat16)

        loop(blocks, add)

    def weight(w, columns):
        return small[w, :, :, :, :, columns].reshape(plane * n0 * small_rows, columns.size)

    def columns_at(start, size):
        return pl.ds(pl.multiple_of(start, TILE), size)

    def hidden_chunk(weights, i, slot):
        def one(lane):
            columns = columns_at(i * chunk + lane * TILE, TILE)
            matrix = weights[:, :, :, :, columns].reshape(n0 * plane * rows, TILE)
            values = jnp.dot(feats[...], matrix, preferred_element_type=jnp.float32)
            wide[:, columns] = values
            spot = columns_at(lane * TILE, TILE)
            pa[slot, mp, 0:1, spot] = jnp.sum(values, 0, keepdims=True)
            pa[slot, mp, 1:2, spot] = jnp.sum(values * values, 0, keepdims=True)

        loop(2, one)
        pa[slot, mp, 2:4, :] = jnp.broadcast_to(jnp.sum(keep[...], 0, keepdims=True), (2, chunk))

    def spread(total):
        mean = total[0:1] / total_views
        return mean, lax.rsqrt(total[1:2] / total_views - mean * mean + NORM_EPS)

    def act_tiles(start, count, mean, inverse, norm, act_ref, hat_ref, act_start):
        for n in range(count):
            columns = pl.ds(start + n * TILE, TILE)
            targets = pl.ds(act_start + n * TILE, TILE)
            here = slice(n * TILE, (n + 1) * TILE)
            mean_n, inverse_n = mean[:, here], inverse[:, here]
            gain, shift = norm[0:1, columns], norm[1:2, columns]

            def one(b):
                part = pl.ds(pl.multiple_of(b * rows, rows), rows)
                hat = (wide[part, columns] - mean_n) * inverse_n
                value = hat * gain + shift
                action = 0.5 * value * (1.0 + gelu_tanh(value))
                act_ref[b // 2, b % 2, :, targets] = action.astype(jnp.bfloat16)
                if hat_ref is not None:
                    hat_ref[b // 2, b % 2, :, targets] = hat.astype(jnp.bfloat16)

            loop(blocks, one)

    def act_chunk(slot, i, norm, act_ref, hat_ref, inv_ref, w, act_start):
        total = sum_end(narrow_sum, slot)
        mean, inverse = spread(total)
        if inv_ref is not None:
            inv_ref[:, pl.ds(i * chunk, chunk)] = inverse
        act_tiles(i * chunk, chunk // TILE, mean, inverse, norm, act_ref, hat_ref, act_start)
        action = act_ref[:, :, :, pl.ds(act_start, chunk)].reshape(views, chunk)
        product = nt_dot(action, weight(w, pl.ds(i * chunk, chunk)))
        if i == 0:
            acc[...] = product
        else:
            acc[...] += product
        return total

    count = [None]

    def online_middle():
        ex[0] = acc[...].astype(jnp.bfloat16)
        swap(0).start()
        swap_end(0)

        def one(n):
            columns = columns_at(n * TILE, TILE)
            values = jnp.dot(ex[0], weight(1, columns), preferred_element_type=jnp.float32)
            wide[:, columns] = values
            qa[0, mp, 0:1, columns] = jnp.sum(values, 0, keepdims=True)
            qa[0, mp, 1:2, columns] = jnp.sum(values * values, 0, keepdims=True)

        loop(width // TILE, one)
        qa[0, mp, 2:4, :] = jnp.zeros((2, width), jnp.float32)
        sum_start(whole_sum, 0)

    def online_query():
        total = sum_end(whole_sum, 0)
        mean, inverse = spread(total)
        inv2[...] = inverse
        act_tiles(0, width // TILE, mean, inverse, pred_norm, act2, hat2, 0)
        ex[1] = nt_dot(
            act2[...].reshape(views, width), weight(2, pl.ds(0, width))
        ).astype(jnp.bfloat16)
        swap(1).start()

    def compute(c):
        if c == 1:
            loads[6].wait()
        if 1 <= c <= 4:
            i = c - 1
            if i:
                sum_middle(narrow_sum, i - 1)
            hidden_chunk(up, i, i)
            sum_start(narrow_sum, i)
            if i:
                total = act_chunk(i - 1, i - 1, proj_norm, act1, hat1, inv1, 0, (i - 1) * chunk)
                if i == 1:
                    count[0] = total[2:3, 0:1]
        if c == 5:
            sum_middle(narrow_sum, 3)
            act_chunk(3, 3, proj_norm, act1, hat1, inv1, 0, 3 * chunk)
            online_middle()
        if c == 6:
            sum_middle(whole_sum, 0)
            online_query()
        if 6 <= c <= 9:
            i = c - 6
            if i:
                sum_middle(narrow_sum, 4 + i - 1)
            hidden_chunk(tup, i, 4 + i)
            sum_start(narrow_sum, 4 + i)
            if i:
                act_chunk(4 + i - 1, i - 1, target_norm, tact, None, None, 3, 0)
            if c == 6:
                swap_end(1)

    total_chunks = len(chunks)
    for c in range(Z_AHEAD):
        gather_start(c, 0)
    for tick in range(total_chunks + 2):
        if tick < total_chunks:
            gather_start(tick, 1)
        if tick + Z_AHEAD < total_chunks:
            gather_start(tick + Z_AHEAD, 0)
        if 1 <= tick <= total_chunks:
            gather_start(tick - 1, 2)
        if tick >= 2:
            gather_end(tick - 2)
            compute(tick - 2)
    for c in range(total_chunks):
        for lane in range(2):
            for phase in range(3):
                for copy in gather_copies(c, lane, phase):
                    copy.wait_send()
    sum_middle(narrow_sum, 7)
    act_chunk(7, 3, target_norm, tact, None, None, 3, 0)
    ex[2] = acc[...].astype(jnp.bfloat16)
    swap(2).start()
    swap(2).wait()

    scale = -2.0 / count[0]

    def unit_scale(values):
        return lax.rsqrt(jnp.sum(values * values, 1, keepdims=True) + UNIT_EPS)

    even = (lax.broadcasted_iota(jnp.int32, (rows, acc.shape[1]), 0) % 2) == 0

    def loss_tile(b, carry):
        part = pl.ds(pl.multiple_of(b * rows, rows), rows)
        query = ex[1, part, :].astype(jnp.float32)
        target = ex[2, part, :].astype(jnp.float32) + exr[2, part, :].astype(jnp.float32)
        target = target * unit_scale(target)
        goal = jnp.where(even, pltpu.roll(target, rows - 1, 0), pltpu.roll(target, 1, 0))
        back = unit_scale(query)
        unit = query * back
        cosine = jnp.sum(unit * goal, 1, keepdims=True)
        kept = keep[part, :]
        ex[1, part, :] = ((scale * kept * back) * (goal - cosine * unit)).astype(jnp.bfloat16)
        return carry + kept * (2.0 - 2.0 * cosine)

    loss_rows = lax.fori_loop(0, blocks, loss_tile, jnp.zeros((rows, 1), jnp.float32))
    local_loss = jnp.sum(loss_rows, 0, keepdims=True)

    def back_norm(i, w, grads, hat_ref, norm, extra):
        def one(n):
            columns = columns_at(n * TILE, TILE)
            wide[:, columns] = jnp.dot(
                ex[grads], weight(w, columns), preferred_element_type=jnp.float32
            )
            gain, shift = norm[0:1, columns], norm[1:2, columns]

            def tile(b, carry):
                part = pl.ds(pl.multiple_of(b * rows, rows), rows)
                hat = hat_ref[b // 2, b % 2, :, columns].astype(jnp.float32)
                value = hat * gain + shift
                bent = gelu_tanh(value)
                slope = 0.5 * (1.0 + bent) + (0.5 * GELU_A) * value * (1.0 - bent * bent) * (
                    1.0 + (3.0 * GELU_B) * value * value
                )
                grad = wide[part, columns] * slope
                wide[part, columns] = grad
                cross = grad * hat
                return (
                    carry[0] + jnp.sum(grad.reshape(rows // 8, 8, TILE), 0),
                    carry[1] + jnp.sum(cross.reshape(rows // 8, 8, TILE), 0),
                )

            zero = jnp.zeros((8, TILE), jnp.float32)
            sums = lax.fori_loop(0, blocks, tile, (zero, zero))
            qa[i, mp, 0:1, columns] = jnp.sum(sums[0], 0, keepdims=True)
            qa[i, mp, 1:2, columns] = jnp.sum(sums[1], 0, keepdims=True)

        loop(width // TILE, one)
        qa[i, mp, 2:4, :] = jnp.broadcast_to(extra, (2, width))
        sum_start(whole_sum, i)

    def grad_hidden(stat, hat_ref, norm, inv_ref, columns):
        gain = norm[0:1, columns] * inv_ref[:, columns]
        shift = stat[0:1, columns] / total_views
        slope = stat[1:2, columns] / total_views

        def tile(b):
            part = pl.ds(pl.multiple_of(b * rows, rows), rows)
            hat = hat_ref[b // 2, b % 2, :, columns].astype(jnp.float32)
            hat_ref[b // 2, b % 2, :, columns] = (
                gain * (wide[part, columns] - shift - hat * slope)
            ).astype(jnp.bfloat16)

        loop(blocks, tile)

    def small_grad(w, grads, act_ref):
        def one(n):
            columns = columns_at(n * TILE, TILE)
            right = act_ref[:, :, :, columns].reshape(views, TILE)
            value = tn_dot(ex[grads], right).astype(jnp.bfloat16)
            small[w, :, :, :, :, columns] = value.reshape(n0, n1, n2, small_rows, TILE)

        loop(width // TILE, one)

    def reduce_copies(kind, g, lane, phase):
        axis, second = ((1, 2), (2, 1))[lane]
        if kind == "up":
            columns = pl.ds(g * chunk + lane * TILE, TILE)
            send, recv = rs_s, rs_r
            source = lambda sel: tup.at[sel[0], sel[1], sel[2], :, columns]
            lands = (
                act2.at[:, :, :, columns],
                hat2.at[:, 0, :, columns],
                hat2.at[me[0], 1, :, columns],
            )
        else:
            columns = pl.ds(lane * half, half)
            send, recv = ss_s, ss_r
            source = lambda sel: small.at[3 - g, sel[0], sel[1], sel[2], :, columns]
            lands = (
                sr1.at[g, :, :, :, columns],
                sr2.at[g, :, :, columns],
                sr3.at[g, me[0], :, columns],
            )
        copies = []
        moves = range(1, n0) if phase == 2 else (1,)
        for k in moves:
            axis_now = (axis, second, 0)[phase]
            target = moved(axis_now, k)
            sel = [slice(None)] * 3
            if phase > 0:
                sel[axis] = me[axis]
            if phase > 1:
                sel[second] = me[second]
            sel[axis_now] = target[axis_now]
            copies.append(
                pltpu.make_async_remote_copy(
                    src_ref=source(sel),
                    dst_ref=lands[phase],
                    send_sem=send.at[g, lane, phase + k - 1],
                    recv_sem=recv.at[g, lane, phase + k - 1],
                    device_id=place(target),
                    device_id_type=MESH,
                )
            )
        return copies

    def reduce_step(kind, g, phase):
        for lane in range(2):
            if phase:
                for copy in reduce_copies(kind, g, lane, phase - 1):
                    copy.wait()
                reduce_add(kind, g, lane, phase)
            if phase < 3:
                for copy in reduce_copies(kind, g, lane, phase):
                    copy.start()

    def plus(first_op, second_op):
        return (first_op.astype(jnp.float32) + second_op.astype(jnp.float32)).astype(jnp.bfloat16)

    def reduce_add(kind, g, lane, phase):
        big = kind == "up"
        if big:
            columns = pl.ds(g * chunk + lane * TILE, TILE)
        else:
            columns = pl.ds(lane * half, half)
        if phase == 1:

            def add(j):
                z, i = j // 2, j % 2
                y, x = (me[1], i) if lane == 0 else (i, me[2])
                if big:
                    tup[z, y, x, :, columns] = plus(
                        tup[z, y, x, :, columns], act2[z, i, :, columns]
                    )
                else:
                    small[3 - g, z, y, x, :, columns] = plus(
                        small[3 - g, z, y, x, :, columns], sr1[g, z, i, :, columns]
                    )

            loop(n0 * 2, add)
        elif phase == 2:

            def add(z):
                if big:
                    tup[z, me[1], me[2], :, columns] = plus(
                        tup[z, me[1], me[2], :, columns], hat2[z, 0, :, columns]
                    )
                else:
                    small[3 - g, z, me[1], me[2], :, columns] = plus(
                        small[3 - g, z, me[1], me[2], :, columns], sr2[g, z, :, columns]
                    )

            loop(n0, add)
        else:
            if big:
                total = tup[me[0], me[1], me[2], :, columns].astype(jnp.float32)
                for k in range(1, n0):
                    total = total + hat2[(me[0] + k) % n0, 1, :, columns].astype(jnp.float32)
                gu_out[:, columns] = total
            else:
                total = small[3 - g, me[0], me[1], me[2], :, columns].astype(jnp.float32)
                for k in range(1, n0):
                    total = total + sr3[g, (me[0] + k) % n0, :, columns].astype(jnp.float32)
                gs_out[g, :, columns] = total

    back_norm(1, 2, 1, hat2, pred_norm, local_loss)
    small_grad(3, 1, act2)
    reduce_step("small", 0, 0)
    sum_middle(whole_sum, 1)
    pred_stat[...] = sum_end(whole_sum, 1)
    loss_out[...] = jnp.broadcast_to(pred_stat[2:3, 0:1] / count[0], loss_out.shape)
    loop(
        width // TILE,
        lambda n: grad_hidden(pred_stat, hat2, pred_norm, inv2, columns_at(n * TILE, TILE)),
    )
    ex[3] = nt_dot(hat2[...].reshape(views, width), weight(1, pl.ds(0, width))).astype(jnp.bfloat16)
    swap(3).start()
    small_grad(2, 0, hat2)
    reduce_step("small", 1, 0)
    reduce_step("small", 0, 1)
    swap_end(3)
    back_norm(2, 0, 3, hat1, proj_norm, jnp.zeros((1, 1), jnp.float32))
    small_grad(1, 3, act1)
    pl.semaphore_signal(ready, inc=1, device_id=other, device_id_type=MESH)
    reduce_step("small", 2, 0)
    reduce_step("small", 1, 1)
    reduce_step("small", 0, 2)
    sum_middle(whole_sum, 2)
    proj_stat[...] = sum_end(whole_sum, 2)

    def up_grad(g):
        for n in range(2):
            grad_hidden(proj_stat, hat1, proj_norm, inv1, pl.ds(g * chunk + n * TILE, TILE))
        columns = pl.ds(g * chunk, chunk)

        def one(z):
            left = feats[:, columns_at(z * plane * rows, plane * rows)]
            value = tn_dot(left, hat1[:, :, :, columns].reshape(views, chunk))
            tup[z, :, :, :, columns] = value.astype(jnp.bfloat16).reshape(n1, n2, rows, chunk)

        loop(n0, one)
        reduce_step("up", g, 0)

    parts = ig_s.shape[0]

    def input_copy(q):
        return pltpu.make_async_remote_copy(
            src_ref=act1.at[:, :, :, pl.ds(q * TILE, TILE)],
            dst_ref=act1.at[:, :, :, pl.ds((parts + q) * TILE, TILE)],
            send_sem=ig_s.at[q],
            recv_sem=ig_r.at[q],
            device_id=other,
            device_id_type=MESH,
        )

    def input_product(q, side):
        first = side * (n0 // 2) + q // n1
        matrix = up[first, q % n1].reshape(n2 * rows, width)
        return nt_dot(hat1[...].reshape(views, width), matrix)

    for g in range(4):
        up_grad(g)
        if g == 0:
            reduce_step("small", 2, 1)
            reduce_step("small", 1, 2)
        else:
            reduce_step("up", g - 1, 1)
        if g == 1:
            reduce_step("small", 0, 3)
            reduce_step("small", 2, 2)
        if g >= 2:
            reduce_step("up", g - 2, 2)
    pl.semaphore_wait(ready, 1)

    def send_part(q):
        act1[:, :, :, pl.ds(q * TILE, TILE)] = (
            input_product(q, 1 - core).astype(jnp.bfloat16).reshape(n0, 2, rows, TILE)
        )
        input_copy(q).start()

    def own_part(q):
        wide[:, pl.ds(q * TILE, TILE)] = input_product(q, core)

    for q in range(2):
        send_part(q)
    reduce_step("up", 3, 1)
    reduce_step("up", 2, 2)
    for q in range(2, parts):
        send_part(q)
    for q in range(parts):
        own_part(q)
    reduce_step("up", 3, 2)
    out_copies = []
    for q in range(parts):
        input_copy(q).wait()

        def add(b, q=q):
            part = pl.ds(pl.multiple_of(b * rows, rows), rows)
            wide[part, pl.ds(q * TILE, TILE)] += act1[
                b // 2, b % 2, :, pl.ds((parts + q) * TILE, TILE)
            ].astype(jnp.float32)

        loop(blocks, add)
    out_copy = pltpu.make_async_copy(
        wide.at[:, pl.ds(0, parts * TILE)], ig_hbm, load_sem.at[0]
    )
    out_copy.start()
    for g in (1, 2):
        reduce_step("small", g, 3)
    for g in range(4):
        reduce_step("up", g, 3)
    out_copy.wait()


def kernel_step(grid, total_views, features, keep, ups, downs, norms):
    n0, n1, n2 = grid
    plane = n1 * n2
    views, depth = features.shape
    rows, width = ups[0].shape
    small_rows = downs[0].shape[0]
    out = small_rows * n0 * plane
    parts = depth // 2 // TILE
    low, full = jnp.bfloat16, jnp.float32
    vm = pltpu.VMEM
    dma = pltpu.SemaphoreType.DMA
    anywhere = pl.BlockSpec(memory_space=pl.ANY)
    inside = pl.BlockSpec(memory_space=pltpu.VMEM)
    spread_shape = (n0, 2, rows, width)
    moves = n0 - 1 + n1 - 1 + n2 - 1
    sum_moves = plane - 1 + n0 - 1
    return pl.pallas_call(
        functools.partial(step_kernel, grid, total_views),
        out_shape=(
            jax.ShapeDtypeStruct((views, depth // 2), full),
            jax.ShapeDtypeStruct((rows, width), full),
            jax.ShapeDtypeStruct((3, small_rows, width), full),
            jax.ShapeDtypeStruct((4, width), full),
            jax.ShapeDtypeStruct((4, width), full),
            jax.ShapeDtypeStruct((8, 128), full),
        ),
        in_specs=[anywhere] * 7 + [inside] * 4,
        out_specs=(anywhere,) + (inside,) * 5,
        scratch_shapes=[
            vm((views, depth), low),
            vm((n0, n1, n2, rows, width), low),
            vm((n0, n1, n2, rows, width), low),
            vm((4, n0, n1, n2, small_rows, width), low),
            vm(spread_shape, low),
            vm(spread_shape, low),
            vm(spread_shape, low),
            vm(spread_shape, low),
            vm((views, width), full),
            vm((n0, 2, rows, width // 4), low),
            vm((views, out), full),
            vm((4, views, out), low),
            vm((4, views, out), low),
            vm((3, n0, 2, small_rows, width), low),
            vm((3, n0, small_rows, width), low),
            vm((3, n0, small_rows, width), low),
            vm((1, width), full),
            vm((1, width), full),
            vm((8, plane, 4, width // 4), full),
            vm((8, n0, 4, width // 4), full),
            vm((3, plane, 4, width), full),
            vm((3, n0, 4, width), full),
            dma((7,)),
            dma((10, 2, moves)),
            dma((10, 2, moves)),
            dma((8, sum_moves)),
            dma((8, sum_moves)),
            dma((3, sum_moves)),
            dma((3, sum_moves)),
            dma((4,)),
            dma((4,)),
            dma((4, 2, n0 + 1)),
            dma((4, 2, n0 + 1)),
            dma((3, 2, n0 + 1)),
            dma((3, 2, n0 + 1)),
            dma((parts,)),
            dma((parts,)),
            pltpu.SemaphoreType.REGULAR,
        ],
        compiler_params=pltpu.CompilerParams(
            collective_id=0, has_side_effects=True, vmem_limit_bytes=VMEM_LIMIT
        ),
    )(features, *ups, *downs, *norms, keep)


def step_body(grid, *args):
    (
        features,
        keep_mask,
        proj_up,
        proj_down,
        proj_norm,
        pred_up,
        pred_down,
        pred_norm,
        moment_proj_up,
        moment_proj_down,
        moment_proj_norm,
        moment_pred_up,
        moment_pred_down,
        moment_pred_norm,
        target_up,
        target_down,
        target_norm,
    ) = args
    if grid is None:
        return plain_body(*args)
    total_views = float(features.shape[0] * lax.axis_size("dp"))
    input_grad, shard_proj_up, shard_small, proj_stat, pred_stat, loss = kernel_step(
        grid,
        total_views,
        features,
        keep_mask.astype(jnp.float32).reshape(-1, 1),
        (proj_up, target_up),
        (proj_down, pred_up, pred_down, target_down),
        (proj_norm, pred_norm, target_norm),
    )
    shard_pred_down, shard_pred_up, shard_proj_down = shard_small[0], shard_small[1], shard_small[2]
    grad_proj_norm = proj_stat[1::-1]
    grad_pred_norm = pred_stat[1::-1]
    return finish(
        total_views,
        args,
        loss[0, 0],
        input_grad,
        shard_proj_up,
        shard_proj_down,
        grad_proj_norm,
        shard_pred_up,
        shard_pred_down,
        grad_pred_norm,
    )


def solution(mesh):
    placed = (
        P("dp", None),
        P("dp"),
        P("dp", "tensor"),
        P("dp", "tensor"),
        P(None, "tensor"),
        P("dp", "tensor"),
        P("dp", "tensor"),
        P(None, "tensor"),
        P("dp", "tensor"),
        P("dp", "tensor"),
        P(None, "tensor"),
        P("dp", "tensor"),
        P("dp", "tensor"),
        P(None, "tensor"),
        P("dp", "tensor"),
        P("dp", "tensor"),
        P(None, "tensor"),
    )
    return jax.shard_map(
        functools.partial(step_body, GRIDS.get(mesh.shape["dp"])),
        mesh=mesh,
        in_specs=placed,
        out_specs=(
            P(),
            P("dp", "tensor"),
            P("dp", "tensor"),
            P("dp", "tensor"),
            P("dp", "tensor"),
            P("dp", "tensor"),
            P("dp", "tensor"),
            P("dp", "tensor"),
            P(None, "tensor"),
            P(None, "tensor"),
            P(None, "tensor"),
            P("dp", "tensor"),
            P("dp", "tensor"),
            P("dp", "tensor"),
            P("dp", "tensor"),
            P("dp", "tensor"),
            P("dp", "tensor"),
            P(None, "tensor"),
            P(None, "tensor"),
            P(None, "tensor"),
            P("dp", "tensor"),
            P("dp", "tensor"),
            P(None, "tensor"),
        ),
        check_vma=False,
    )
```

time: 924 us -> 416 us (0.45); the launches traced: 913 us -> 416 us
  Pallas kernels: 0 us -> 399 us
  waiting for transfers between devices: 373 us -> 0 us
  blocking collectives: 306 us -> 0 us
  matrix products: 115 us -> 0 us
  other arithmetic: 57.9 us -> 6.82 us
  local copies, waits for them, and re-layouts: 41.8 us -> 9.13 us
  between operations: 18.1 us -> 0.9 us
    pallas_call x0 -> x1, Pallas kernels: none -> 399 us  [kernel_step(): pl.pallas_call(functools.partial(step_kernel, grid, total_views), out_sha...]
    psum x4 -> x0, blocking collectives: 306 us -> none  [the longest x1 77.5 us: body(): lax.psum(jnp.stack([jnp.sum(grad_norm1, 0), jnp.sum(grad_norm1 * scaled1,...]
    all_gather x2 -> x0, waiting for transfers between devices: 191 us -> none  [gathered(): full = lax.all_gather(low, 'dp', axis=1, tiled=True)]
    unnamed x9 -> x0, waiting for transfers between devices: 156 us -> none
    dot_general x14 -> x0, matrix products: 115 us -> none  [the longest x5 32.4 us: across(): lax.dot_general(matrix, weight, (((1,), (1,)), ((), ())), preferred_eleme...]
    convert_element_type x6 -> x1, other arithmetic: 32.2 us -> 0.69 us  [step_body(): keep_mask.astype(jnp.float32).reshape(-1, 1)]
    unnamed x45 -> x38, local copies, waits for them, and re-layouts: 33.7 us -> 5.95 us
    psum x3 -> x0, waiting for transfers between devices: 26.1 us -> none  [the longest x1 14.2 us: body(): lax.psum(across(action2, pdown_full).astype(jnp.bfloat16), 'tensor')]
  transfers between devices with their start and end apart: 8 -> 0, of which waited for: 5 -> 0; matrix products, arithmetic and copies ran while one was open for 14% -> 0% of each run, Pallas kernels for 0% -> 0%
where the time goes in v2:
time: 416 us
  Pallas kernels  399 us (96%)
  local copies, waits for them, and re-layouts  9.13 us (2%)
  other arithmetic  6.82 us (2%)
    pallas_call x1, Pallas kernels, kernel_step(): pl.pallas_call(functools.partial(step_kernel, grid, total_views), out_sha...  399 us

profile of v2, /device:TPU:0, one launch (start us, length us, event | category | flops | bytes accessed | tf_op | source)
XLA Modules:
  0.0 416.1 jit_solution(15418406042164033070)
XLA Ops:
  0.7 0.7 convert_element_type.3
  1.3 1.0 copy.40.keep
  2.4 399.3 %shard_map.344 = (f32[1024,1024]{1,0:T(8,128)}, f32[128,2048]{1,0:T(8,128)}, f32[3,16,2048]{2,1,0:T(8,128)}, f32[4,2048]{1,0:T(4,128)}, f32[4,2048]{1,0:T(4,128)}, /*index=5*/f32[8,128]{1,0:T(8,128)}) custom-call(bf16[1024,2048]{1,0:T(8,128)(2,1)} %x_hbm.1, f32[128,2048]{1,0:T(8,128)} %pu_hbm.1, f32[128,2048]{1,0:T(8,128)} %tu_hbm.1, f32[16,2048]{1,0:T(8,128)} %pd_hbm.1, ...), custom_call_target="tpu_custom_call" | custom-call | tf_op jit(solution)/shard_map/pallas_call | solution.py:995
  401.7 0.0 copy-start.1
  401.7 0.0 copy-start.2
  401.7 0.0 copy-start.3
  401.7 0.0 copy-start.4
  401.7 0.0 copy-start.5
  401.7 0.0 copy-start.6
  401.7 0.0 copy-start.7
  401.7 0.0 copy-start.8
  401.8 1.3 slice.18
  403.1 0.0 copy-start.17
  403.1 0.0 copy-start.16
  403.1 0.0 copy-start.9
  403.1 0.0 copy-start.10
  403.1 0.0 copy-start.11
  403.1 0.0 copy-start.14
  403.1 0.0 copy-start.15
  403.1 4.4 %add_multiply_fusion = (f32[128,2048]{1,0:T(8,128)}, f32[128,2048]{1,0:T(8,128)}, f32[128,2048]{1,0:T(8,128)}) fusion(f32[128,2048]{1,0:T(8,128)} %tu_hbm.1, f32[128,2048]{1,0:T(8,128)} %pu_hbm.1, f32[128,2048]{1,0:T(8,128)} %get-tuple-element.87, f32[128,2048]{1,0:T(8,128)} %param.25), kind=kLoop, calls=%fused_computation | loop fusion | flops 2097152 | bytes 7340032 | tf_op jit(solution)/shard_map/add | solution.py:92
  407.5 0.0 copy-done.1
  407.5 0.0 copy-done.2
  407.5 0.0 copy-done.3
  407.5 0.0 copy-done.4
  407.5 0.0 copy-done.5
  407.5 0.0 copy-done.6
  407.5 0.0 copy-done.7
  407.5 0.0 copy-done.8
  407.6 1.1 multiply_subtract_fusion.1
  408.6 0.0 copy-done.17
  408.6 0.4 rev.6
  409.1 0.0 copy-start.12
  409.1 0.0 copy-done.16
  409.1 0.4 rev.7
  409.5 0.0 copy-done.9
  409.5 0.0 copy-done.10
  409.5 0.0 copy-done.11
  409.6 0.0 copy-done.14
  409.6 0.0 copy-done.15
  409.6 0.0 copy-start.13
  409.6 0.7 add_multiply_fusion.2
  410.3 0.0 copy-start
  410.3 4.9 %copy.43 = f32[1024,1024]{1,0:T(8,128)} copy(f32[1024,1024]{1,0:T(8,128)} %get-tuple-element.86) | data formatting | bytes 8388608
  415.1 0.0 copy-done.12
  415.1 0.0 copy-done.13
  415.1 0.0 copy-done
  415.2 1.0 copy.44
  (2 shorter events, 0.0 us)
Async XLA Ops:
  401.7 5.8 %copy-start.1 = (f32[16,2048]{1,0:T(8,128)S(1)}, f32[16,2048]{1,0:T(8,128)}, u32[]{:S(2)}) copy-start(f32[16,2048]{1,0:T(8,128)} %pd_hbm.1) | copy-start | bytes 393220
  401.7 5.8 %copy-start.2 = (f32[16,2048]{1,0:T(8,128)S(1)}, f32[16,2048]{1,0:T(8,128)}, u32[]{:S(2)}) copy-start(f32[16,2048]{1,0:T(8,128)} %qu_hbm.1) | copy-start | bytes 393220
  401.7 5.8 %copy-start.3 = (f32[16,2048]{1,0:T(8,128)S(1)}, f32[16,2048]{1,0:T(8,128)}, u32[]{:S(2)}) copy-start(f32[16,2048]{1,0:T(8,128)} %qd_hbm.1) | copy-start | bytes 393220
  401.7 5.8 %copy-start.4 = (f32[16,2048]{1,0:T(8,128)S(1)}, f32[16,2048]{1,0:T(8,128)}, u32[]{:S(2)}) copy-start(f32[16,2048]{1,0:T(8,128)} %td_hbm.1) | copy-start | bytes 393220
  401.7 5.8 %copy-start.5 = (f32[3,16,2048]{2,1,0:T(8,128)S(1)}, f32[3,16,2048]{2,1,0:T(8,128)}, u32[]{:S(2)}) copy-start(f32[3,16,2048]{2,1,0:T(8,128)} %get-tuple-element.32) | copy-start | bytes 1179652
  401.7 5.8 %copy-start.6 = (f32[16,2048]{1,0:T(8,128)S(1)}, f32[16,2048]{1,0:T(8,128)}, u32[]{:S(2)}) copy-start(f32[16,2048]{1,0:T(8,128)} %param.29) | copy-start | bytes 393220
  401.7 5.8 %copy-start.7 = (f32[16,2048]{1,0:T(8,128)S(1)}, f32[16,2048]{1,0:T(8,128)}, u32[]{:S(2)}) copy-start(f32[16,2048]{1,0:T(8,128)} %param.28) | copy-start | bytes 393220
  401.7 5.8 %copy-start.8 = (f32[16,2048]{1,0:T(8,128)S(1)}, f32[16,2048]{1,0:T(8,128)}, u32[]{:S(2)}) copy-start(f32[16,2048]{1,0:T(8,128)} %param.26) | copy-start | bytes 393220
  403.1 5.6 %copy-start.17 = (f32[4,2048]{1,0:T(4,128)S(1)}, f32[4,2048]{1,0:T(4,128)}, u32[]{:S(2)}) copy-start(f32[4,2048]{1,0:T(4,128)} %get-tuple-element.33) | copy-start | bytes 98308
  403.1 6.0 %copy-start.16 = (f32[4,2048]{1,0:T(4,128)S(1)}, f32[4,2048]{1,0:T(4,128)}, u32[]{:S(2)}) copy-start(f32[4,2048]{1,0:T(4,128)} %get-tuple-element.34) | copy-start | bytes 98308
  403.1 6.5 %copy-start.9 = (f32[2,2048]{1,0:T(2,128)S(1)}, f32[2,2048]{1,0:T(2,128)}, u32[]{:S(2)}) copy-start(f32[2,2048]{1,0:T(2,128)} %proj_norm.1) | copy-start | bytes 49156
  403.1 6.5 %copy-start.10 = (f32[2,2048]{1,0:T(2,128)S(1)}, f32[2,2048]{1,0:T(2,128)}, u32[]{:S(2)}) copy-start(f32[2,2048]{1,0:T(2,128)} %pred_norm.1) | copy-start | bytes 49156
  403.1 6.5 %copy-start.11 = (f32[2,2048]{1,0:T(2,128)S(1)}, f32[2,2048]{1,0:T(2,128)}, u32[]{:S(2)}) copy-start(f32[2,2048]{1,0:T(2,128)} %target_norm.1) | copy-start | bytes 49156
  403.1 6.5 %copy-start.14 = (f32[2,2048]{1,0:T(2,128)S(1)}, f32[2,2048]{1,0:T(2,128)}, u32[]{:S(2)}) copy-start(f32[2,2048]{1,0:T(2,128)} %param.27) | copy-start | bytes 49156
  403.1 6.5 %copy-start.15 = (f32[2,2048]{1,0:T(2,128)S(1)}, f32[2,2048]{1,0:T(2,128)}, u32[]{:S(2)}) copy-start(f32[2,2048]{1,0:T(2,128)} %param.30) | copy-start | bytes 49156
  409.1 6.1 %copy-start.12 = (f32[2,2048]{1,0:T(2,128)}, f32[2,2048]{1,0:T(2,128)S(1)}, u32[]{:S(2)}) copy-start(f32[2,2048]{1,0:T(2,128)S(1)} %rev.6) | copy-start | bytes 49156
  409.6 5.6 %copy-start.13 = (f32[2,2048]{1,0:T(2,128)}, f32[2,2048]{1,0:T(2,128)S(1)}, u32[]{:S(2)}) copy-start(f32[2,2048]{1,0:T(2,128)S(1)} %rev.7) | copy-start | bytes 49156
  410.3 4.9 %copy-start = (f32[128,2048]{1,0:T(8,128)S(1)}, f32[128,2048]{1,0:T(8,128)}, u32[]{:S(2)}) copy-start(f32[128,2048]{1,0:T(8,128)} %get-tuple-element.87) | copy-start | bytes 3145732

commit v3 on v2

--- a/solution.py
+++ b/solution.py
@@ -280,9 +280,7 @@
 TILE = 256
 GELU_A = math.sqrt(2.0 / math.pi)
 GELU_B = 0.044715
-ALONG_LAST = (0, ((0, 2, 1), (0, 1, 2)))
-ACROSS_FIRST = (1, ((2, 1, 0), (1, 2, 0)))
-Z_AHEAD = 2
+LATE_PER_TICK = 2
 VMEM_LIMIT = 63 * 1024 * 1024
 
 
@@ -348,10 +346,13 @@
     sr3,
     inv1,
     inv2,
+    means,
     pa,
     pb,
     qa,
     qb,
+    ta,
+    tb,
     load_sem,
     ag_s,
     ag_r,
@@ -359,6 +360,8 @@
     ps_r,
     qs_s,
     qs_r,
+    ts_s,
+    ts_r,
     ex_s,
     ex_r,
     rs_s,
@@ -420,56 +423,104 @@
         small[w, me[0], me[1], me[2]] = wide[
             pl.ds(2 * rows + w * small_rows, small_rows), :
         ].astype(jnp.bfloat16)
-    loads[4].wait()
-    up[me[0], me[1], me[2]] = wide[pl.ds(0, rows), :].astype(jnp.bfloat16)
-    loads[5].wait()
-    tup[me[0], me[1], me[2]] = wide[pl.ds(rows, rows), :].astype(jnp.bfloat16)
     pl.semaphore_wait(barrier, len(greet))
 
-    base = (0, n0 - 1, n0 - 1 + n1 - 1)
-    chunks = [("small", 0, ALONG_LAST)]
-    chunks += [("up", i, ALONG_LAST) for i in range(4)]
-    chunks += [("small", 1, ACROSS_FIRST)]
-    chunks += [("target", i, ALONG_LAST) for i in range(4)]
-
-    def gather_copies(c, lane, phase):
-        kind, index, (_, orders) = chunks[c]
-        order = orders[lane]
-        axis = order[phase]
-        sel = [slice(None) if b in order[:phase] else me[b] for b in range(3)]
+    def take(load, buffer, start):
+        load.wait()
+        buffer[me[0], me[1], me[2]] = wide[pl.ds(start, rows), :].astype(jnp.bfloat16)
+
+    hops = n0 - 1
+    kinds = [("small", 0)] + [("up", i) for i in range(4)]
+    kinds += [("target", i) for i in (0, 1, 3)]
+    main = len(kinds)
+    kinds += [("target", 2), ("small", 1)]
+    late = [main + 1, main]
+
+    def piece(c, lane, sel):
+        kind, index = kinds[c]
         if kind == "small":
-            ref = small.at[
+            return small.at[
                 pl.ds(2 * index, 2), sel[0], sel[1], sel[2], :, pl.ds(lane * half, half)
             ]
-        else:
-            buffer = up if kind == "up" else tup
-            ref = buffer.at[
-                sel[0], sel[1], sel[2], :, pl.ds(index * chunk + lane * TILE, TILE)
-            ]
-        return [
-            pltpu.make_async_remote_copy(
-                src_ref=ref,
-                dst_ref=ref,
-                send_sem=ag_s.at[c, lane, base[axis] + k - 1],
-                recv_sem=ag_r.at[c, lane, base[axis] + k - 1],
-                device_id=place(moved(axis, k)),
-                device_id_type=MESH,
-            )
-            for k in range(1, grid[axis])
-        ]
-
-    def gather_start(c, phase):
+        buffer = up if kind == "up" else tup
+        return buffer.at[sel[0], sel[1], sel[2], :, pl.ds(index * chunk + lane * TILE, TILE)]
+
+    def gather_copy(c, lane, ref, sem, target):
+        return pltpu.make_async_remote_copy(
+            src_ref=ref,
+            dst_ref=ref,
+            send_sem=ag_s.at[c, lane, sem],
+            recv_sem=ag_r.at[c, lane, sem],
+            device_id=place(target),
+            device_id_type=MESH,
+        )
+
+    def inside_line(index):
+        return jnp.logical_and(index >= 0, index < n0)
+
+    def line_each(c, lane, hop, way, act):
+        sel = [None, slice(None), slice(None)] if c in late else [None, me[1], me[2]]
+        for bit, turn in enumerate((1, -1)):
+            block = me[0] - turn * (hop if way == "send" else hop + 1)
+            fits = inside_line(block)
+            if way == "send":
+                fits = jnp.logical_and(fits, inside_line(me[0] + turn))
+
+            @pl.when(fits)
+            def _(bit=bit, turn=turn, block=block):
+                ref = piece(c, lane, [block] + sel[1:])
+                target = (me[0] + (turn if way == "send" else -turn), me[1], me[2])
+                act(gather_copy(c, lane, ref, 2 * hop + bit, target))
+
+    def line_hop(c, lane, hop):
+        if hop:
+            line_each(c, lane, hop - 1, "recv", lambda copy: copy.wait_recv())
+        line_each(c, lane, hop, "send", lambda copy: copy.start())
+
+    def side_copy(c, lane, phase):
+        axis, second = ((2, 1), (1, 2))[lane]
+        sel = [me[0] if c in late else slice(None), me[1], me[2]]
+        if phase:
+            sel[axis] = slice(None)
+        return gather_copy(
+            c, lane, piece(c, lane, sel), 2 * hops + phase, moved((axis, second)[phase], 1)
+        )
+
+    def gather_line(c, hop):
+        for lane in range(2):
+            line_hop(c, lane, hop)
+
+    def gather_side(c, phase):
         for lane in range(2):
             if phase:
-                for copy in gather_copies(c, lane, phase - 1):
-                    copy.wait_recv()
-            for copy in gather_copies(c, lane, phase):
-                copy.start()
+                side_copy(c, lane, 0).wait_recv()
+            elif c not in late:
+                line_each(c, lane, hops - 1, "recv", lambda copy: copy.wait_recv())
+            side_copy(c, lane, phase).start()
 
     def gather_end(c):
         for lane in range(2):
-            for copy in gather_copies(c, lane, 2):
-                copy.wait_recv()
+            if c in late:
+                line_each(c, lane, hops - 1, "recv", lambda copy: copy.wait_recv())
+            else:
+                side_copy(c, lane, 1).wait_recv()
+
+    late_items = [(c, lane, hop) for hop in range(hops) for c in late for lane in range(2)]
+
+    def late_next():
+        if late_items:
+            c, lane, hop = late_items.pop(0)
+            if hop == 0:
+                side_copy(c, lane, 1).wait_recv()
+            line_hop(c, lane, hop)
+
+    def gather_sent():
+        for c in range(len(kinds)):
+            for lane in range(2):
+                for hop in range(hops):
+                    line_each(c, lane, hop, "send", lambda copy: copy.wait_send())
+                for phase in range(2):
+                    side_copy(c, lane, phase).wait_send()
 
     def sum_copies(buffers, i, stage):
         first, second, send, recv = buffers
@@ -501,6 +552,7 @@
 
     narrow_sum = (pa, pb, ps_s, ps_r)
     whole_sum = (qa, qb, qs_s, qs_r)
+    scalar_sum = (ta, tb, ts_s, ts_r)
 
     def sum_start(buffers, i):
         for copy in sum_copies(buffers, i, 0):
@@ -564,7 +616,6 @@
             pa[slot, mp, 1:2, spot] = jnp.sum(values * values, 0, keepdims=True)
 
         loop(2, one)
-        pa[slot, mp, 2:4, :] = jnp.broadcast_to(jnp.sum(keep[...], 0, keepdims=True), (2, chunk))
 
     def spread(total):
         mean = total[0:1] / total_views
@@ -603,90 +654,129 @@
             acc[...] += product
         return total
 
-    count = [None]
-
-    def online_middle():
-        ex[0] = acc[...].astype(jnp.bfloat16)
-        swap(0).start()
+    count = []
+
+    def middle_stats():
         swap_end(0)
 
         def one(n):
             columns = columns_at(n * TILE, TILE)
             values = jnp.dot(ex[0], weight(1, columns), preferred_element_type=jnp.float32)
-            wide[:, columns] = values
             qa[0, mp, 0:1, columns] = jnp.sum(values, 0, keepdims=True)
             qa[0, mp, 1:2, columns] = jnp.sum(values * values, 0, keepdims=True)
 
         loop(width // TILE, one)
-        qa[0, mp, 2:4, :] = jnp.zeros((2, width), jnp.float32)
         sum_start(whole_sum, 0)
 
     def online_query():
-        total = sum_end(whole_sum, 0)
-        mean, inverse = spread(total)
+        mean, inverse = spread(sum_end(whole_sum, 0))
         inv2[...] = inverse
-        act_tiles(0, width // TILE, mean, inverse, pred_norm, act2, hat2, 0)
+        means[...] = mean
+
+        def one(n):
+            columns = columns_at(n * TILE, TILE)
+            wide[:, pl.ds(3 * chunk, TILE)] = jnp.dot(
+                ex[0], weight(1, columns), preferred_element_type=jnp.float32
+            )
+            mean_n, inverse_n = means[:, columns], inv2[:, columns]
+            gain, shift = pred_norm[0:1, columns], pred_norm[1:2, columns]
+
+            def tile(b):
+                part = pl.ds(pl.multiple_of(b * rows, rows), rows)
+                hat = (wide[part, pl.ds(3 * chunk, TILE)] - mean_n) * inverse_n
+                value = hat * gain + shift
+                action = 0.5 * value * (1.0 + gelu_tanh(value))
+                act2[b // 2, b % 2, :, columns] = action.astype(jnp.bfloat16)
+                hat2[b // 2, b % 2, :, columns] = hat.astype(jnp.bfloat16)
+
+            loop(blocks, tile)
+
+        loop(width // TILE, one)
         ex[1] = nt_dot(
             act2[...].reshape(views, width), weight(2, pl.ds(0, width))
         ).astype(jnp.bfloat16)
         swap(1).start()
 
+    def early(c):
+        slot = c - 3
+        if 0 <= slot <= 3:
+            act_chunk(slot, slot, proj_norm, act1, hat1, inv1, 0, slot * chunk)
+        elif slot >= 4:
+            act_chunk(slot, slot - 4, target_norm, tact, None, None, 3, 0)
+        if slot == 3:
+            ex[0] = acc[...].astype(jnp.bfloat16)
+            swap(0).start()
+            middle_stats()
+        if slot == 5:
+            online_query()
+
+    def between(c):
+        if c >= 2:
+            sum_middle(narrow_sum, c - 2)
+        if c == 7:
+            sum_middle(whole_sum, 0)
+        if c == 3:
+            sum_middle(scalar_sum, 0)
+
     def compute(c):
-        if c == 1:
+        if c == 0:
             loads[6].wait()
-        if 1 <= c <= 4:
+            ta[0, mp] = jnp.broadcast_to(jnp.sum(keep[...], 0, keepdims=True), (8, 128))
+            sum_start(scalar_sum, 0)
+        else:
             i = c - 1
-            if i:
-                sum_middle(narrow_sum, i - 1)
-            hidden_chunk(up, i, i)
+            hidden_chunk(up if i < 4 else tup, i % 4, i)
             sum_start(narrow_sum, i)
-            if i:
-                total = act_chunk(i - 1, i - 1, proj_norm, act1, hat1, inv1, 0, (i - 1) * chunk)
-                if i == 1:
-                    count[0] = total[2:3, 0:1]
-        if c == 5:
-            sum_middle(narrow_sum, 3)
-            act_chunk(3, 3, proj_norm, act1, hat1, inv1, 0, 3 * chunk)
-            online_middle()
-        if c == 6:
-            sum_middle(whole_sum, 0)
-            online_query()
-        if 6 <= c <= 9:
-            i = c - 6
-            if i:
-                sum_middle(narrow_sum, 4 + i - 1)
-            hidden_chunk(tup, i, 4 + i)
-            sum_start(narrow_sum, 4 + i)
-            if i:
-                act_chunk(4 + i - 1, i - 1, target_norm, tact, None, None, 3, 0)
-            if c == 6:
-                swap_end(1)
-
-    total_chunks = len(chunks)
-    for c in range(Z_AHEAD):
-        gather_start(c, 0)
-    for tick in range(total_chunks + 2):
-        if tick < total_chunks:
-            gather_start(tick, 1)
-        if tick + Z_AHEAD < total_chunks:
-            gather_start(tick + Z_AHEAD, 0)
-        if 1 <= tick <= total_chunks:
-            gather_start(tick - 1, 2)
-        if tick >= 2:
+        if c == 4:
+            count.append(sum_end(scalar_sum, 0))
+
+    gather_line(0, 0)
+    gather_side(late[0], 0)
+    take(loads[5], tup, rows)
+    gather_side(late[1], 0)
+    take(loads[4], up, 0)
+    gather_line(1, 0)
+    gather_line(0, 1)
+    gather_line(2, 0)
+    gather_line(1, 1)
+    gather_line(0, 2)
+    for c in late:
+        gather_side(c, 1)
+    for tick in range(main + 2):
+        if tick < main:
+            gather_side(tick, 0)
+        for ahead, hop in ((1, 2), (2, 1), (3, 0)):
+            if tick + ahead < main:
+                gather_line(tick + ahead, hop)
+        if tick >= 1:
+            for _ in range(LATE_PER_TICK):
+                late_next()
+        if 1 <= tick <= main:
+            gather_side(tick - 1, 1)
+        if 2 <= tick <= main:
+            early(tick - 2)
+            between(tick - 2)
             gather_end(tick - 2)
             compute(tick - 2)
-    for c in range(total_chunks):
-        for lane in range(2):
-            for phase in range(3):
-                for copy in gather_copies(c, lane, phase):
-                    copy.wait_send()
+    gather_end(main + 1)
+    early(main - 1)
+    between(main - 1)
+    gather_end(main)
+    compute(main - 1)
+    early(main)
+    between(main)
+    gather_end(main - 1)
+    compute(main)
+    early(main + 1)
     sum_middle(narrow_sum, 7)
     act_chunk(7, 3, target_norm, tact, None, None, 3, 0)
     ex[2] = acc[...].astype(jnp.bfloat16)
     swap(2).start()
+    gather_sent()
+    swap_end(1)
     swap(2).wait()
 
-    scale = -2.0 / count[0]
+    scale = -2.0 / count[0][0:1, 0:1]
 
     def unit_scale(values):
         return lax.rsqrt(jnp.sum(values * values, 1, keepdims=True) + UNIT_EPS)
@@ -707,9 +797,10 @@
         return carry + kept * (2.0 - 2.0 * cosine)
 
     loss_rows = lax.fori_loop(0, blocks, loss_tile, jnp.zeros((rows, 1), jnp.float32))
-    local_loss = jnp.sum(loss_rows, 0, keepdims=True)
-
-    def back_norm(i, w, grads, hat_ref, norm, extra):
+    ta[1, mp] = jnp.broadcast_to(jnp.sum(loss_rows, 0, keepdims=True), (8, 128))
+    sum_start(scalar_sum, 1)
+
+    def back_norm(i, w, grads, hat_ref, norm):
         def one(n):
             columns = columns_at(n * TILE, TILE)
             wide[:, columns] = jnp.dot(
@@ -739,7 +830,6 @@
             qa[i, mp, 1:2, columns] = jnp.sum(sums[1], 0, keepdims=True)
 
         loop(width // TILE, one)
-        qa[i, mp, 2:4, :] = jnp.broadcast_to(extra, (2, width))
         sum_start(whole_sum, i)
 
     def grad_hidden(stat, hat_ref, norm, inv_ref, columns):
@@ -867,12 +957,11 @@
                     total = total + sr3[g, (me[0] + k) % n0, :, columns].astype(jnp.float32)
                 gs_out[g, :, columns] = total
 
-    back_norm(1, 2, 1, hat2, pred_norm, local_loss)
+    back_norm(1, 2, 1, hat2, pred_norm)
     small_grad(3, 1, act2)
     reduce_step("small", 0, 0)
     sum_middle(whole_sum, 1)
     pred_stat[...] = sum_end(whole_sum, 1)
-    loss_out[...] = jnp.broadcast_to(pred_stat[2:3, 0:1] / count[0], loss_out.shape)
     loop(
         width // TILE,
         lambda n: grad_hidden(pred_stat, hat2, pred_norm, inv2, columns_at(n * TILE, TILE)),
@@ -883,7 +972,8 @@
     reduce_step("small", 1, 0)
     reduce_step("small", 0, 1)
     swap_end(3)
-    back_norm(2, 0, 3, hat1, proj_norm, jnp.zeros((1, 1), jnp.float32))
+    back_norm(2, 0, 3, hat1, proj_norm)
+    sum_middle(scalar_sum, 1)
     small_grad(1, 3, act1)
     pl.semaphore_signal(ready, inc=1, device_id=other, device_id_type=MESH)
     reduce_step("small", 2, 0)
@@ -973,6 +1063,7 @@
         reduce_step("small", g, 3)
     for g in range(4):
         reduce_step("up", g, 3)
+    loss_out[...] = sum_end(scalar_sum, 1) / count[0]
     out_copy.wait()
 
 
@@ -990,7 +1081,7 @@
     anywhere = pl.BlockSpec(memory_space=pl.ANY)
     inside = pl.BlockSpec(memory_space=pltpu.VMEM)
     spread_shape = (n0, 2, rows, width)
-    moves = n0 - 1 + n1 - 1 + n2 - 1
+    moves = 2 * (n0 - 1) + 2
     sum_moves = plane - 1 + n0 - 1
     return pl.pallas_call(
         functools.partial(step_kernel, grid, total_views),
@@ -998,8 +1089,8 @@
             jax.ShapeDtypeStruct((views, depth // 2), full),
             jax.ShapeDtypeStruct((rows, width), full),
             jax.ShapeDtypeStruct((3, small_rows, width), full),
-            jax.ShapeDtypeStruct((4, width), full),
-            jax.ShapeDtypeStruct((4, width), full),
+            jax.ShapeDtypeStruct((2, width), full),
+            jax.ShapeDtypeStruct((2, width), full),
             jax.ShapeDtypeStruct((8, 128), full),
         ),
         in_specs=[anywhere] * 7 + [inside] * 4,
@@ -1023,10 +1114,13 @@
             vm((3, n0, small_rows, width), low),
             vm((1, width), full),
             vm((1, width), full),
-            vm((8, plane, 4, width // 4), full),
-            vm((8, n0, 4, width // 4), full),
-            vm((3, plane, 4, width), full),
-            vm((3, n0, 4, width), full),
+            vm((1, width), full),
+            vm((8, plane, 2, width // 4), full),
+            vm((8, n0, 2, width // 4), full),
+            vm((3, plane, 2, width), full),
+            vm((3, n0, 2, width), full),
+            vm((2, plane, 8, 128), full),
+            vm((2, n0, 8, 128), full),
             dma((7,)),
             dma((10, 2, moves)),
             dma((10, 2, moves)),
@@ -1034,6 +1128,8 @@
             dma((8, sum_moves)),
             dma((3, sum_moves)),
             dma((3, sum_moves)),
+            dma((2, sum_moves)),
+            dma((2, sum_moves)),
             dma((4,)),
             dma((4,)),
             dma((4, 2, n0 + 1)),
@@ -1083,8 +1179,8 @@
         (proj_norm, pred_norm, target_norm),
     )
     shard_pred_down, shard_pred_up, shard_proj_down = shard_small[0], shard_small[1], shard_small[2]
-    grad_proj_norm = proj_stat[1::-1]
-    grad_pred_norm = pred_stat[1::-1]
+    grad_proj_norm = proj_stat[::-1]
+    grad_pred_norm = pred_stat[::-1]
     return finish(
         total_views,
         args,

time: 416 us -> 352 us (0.85)
  Pallas kernels: 399 us -> 335 us
    pallas_call x1, Pallas kernels: 399 us -> 335 us  [kernel_step(): pl.pallas_call(functools.partial(step_kernel, grid, total_views), out_sha...]
where the time goes in v3:
time: 352 us; the launch traced here: 351 us
  Pallas kernels  335 us (95%)
  local copies, waits for them, and re-layouts  9.08 us (3%)
  other arithmetic  6.82 us (2%)
    pallas_call x1, Pallas kernels, kernel_step(): pl.pallas_call(functools.partial(step_kernel, grid, total_views), out_sha...  335 us

profile of v3, /device:TPU:0, one launch (start us, length us, event | category | flops | bytes accessed | tf_op | source)
XLA Modules:
  0.0 351.3 jit_solution(1980082260768409907)
XLA Ops:
  0.7 0.7 convert_element_type.3
  1.3 1.0 copy.40.keep
  2.4 334.5 %shard_map.344 = (f32[1024,1024]{1,0:T(8,128)}, f32[128,2048]{1,0:T(8,128)}, f32[3,16,2048]{2,1,0:T(8,128)}, f32[2,2048]{1,0:T(2,128)}, f32[2,2048]{1,0:T(2,128)}, /*index=5*/f32[8,128]{1,0:T(8,128)}) custom-call(bf16[1024,2048]{1,0:T(8,128)(2,1)} %x_hbm.1, f32[128,2048]{1,0:T(8,128)} %pu_hbm.1, f32[128,2048]{1,0:T(8,128)} %tu_hbm.1, f32[16,2048]{1,0:T(8,128)} %pd_hbm.1, ...), custom_call_target="tpu_custom_call" | custom-call | tf_op jit(solution)/shard_map/pallas_call | solution.py:1086
  336.9 0.0 copy-start.1
  336.9 0.0 copy-start.2
  336.9 0.0 copy-start.3
  337.0 0.0 copy-start.4
  337.0 0.0 copy-start.5
  337.0 0.0 copy-start.6
  337.0 0.0 copy-start.7
  337.0 0.0 copy-start.8
  337.0 1.3 slice.12
  338.3 0.0 copy-start.17
  338.3 0.0 copy-start.16
  338.3 0.0 copy-start.9
  338.3 0.0 copy-start.10
  338.3 0.0 copy-start.11
  338.4 0.0 copy-start.14
  338.4 0.0 copy-start.15
  338.4 4.4 %add_multiply_fusion = (f32[128,2048]{1,0:T(8,128)}, f32[128,2048]{1,0:T(8,128)}, f32[128,2048]{1,0:T(8,128)}) fusion(f32[128,2048]{1,0:T(8,128)} %tu_hbm.1, f32[128,2048]{1,0:T(8,128)} %pu_hbm.1, f32[128,2048]{1,0:T(8,128)} %get-tuple-element.87, f32[128,2048]{1,0:T(8,128)} %param.25), kind=kLoop, calls=%fused_computation | loop fusion | flops 2097152 | bytes 7340032 | tf_op jit(solution)/shard_map/add | solution.py:92
  342.8 0.0 copy-done.1
  342.8 0.0 copy-done.2
  342.8 0.0 copy-done.3
  342.8 0.0 copy-done.4
  342.8 0.0 copy-done.5
  342.8 0.0 copy-done.6
  342.8 0.0 copy-done.7
  342.8 0.0 copy-done.8
  342.8 1.1 multiply_subtract_fusion.1
  343.9 0.0 copy-done.17
  343.9 0.4 rev.6
  344.3 0.0 copy-start.12
  344.3 0.0 copy-done.16
  344.3 0.4 rev.7
  344.7 0.0 copy-done.9
  344.7 0.0 copy-done.10
  344.8 0.0 copy-done.11
  344.8 0.0 copy-done.14
  344.8 0.0 copy-done.15
  344.8 0.0 copy-start.13
  344.8 0.7 add_multiply_fusion.2
  345.5 0.0 copy-start
  345.5 4.9 %copy.43 = f32[1024,1024]{1,0:T(8,128)} copy(f32[1024,1024]{1,0:T(8,128)} %get-tuple-element.86) | data formatting | bytes 8388608
  350.4 0.0 copy-done.12
  350.4 0.0 copy-done.13
  350.4 0.0 copy-done
  350.4 1.0 copy.44
Async XLA Ops:
  336.9 5.8 %copy-start.1 = (f32[16,2048]{1,0:T(8,128)S(1)}, f32[16,2048]{1,0:T(8,128)}, u32[]{:S(2)}) copy-start(f32[16,2048]{1,0:T(8,128)} %pd_hbm.1) | copy-start | bytes 393220
  336.9 5.8 %copy-start.2 = (f32[16,2048]{1,0:T(8,128)S(1)}, f32[16,2048]{1,0:T(8,128)}, u32[]{:S(2)}) copy-start(f32[16,2048]{1,0:T(8,128)} %qu_hbm.1) | copy-start | bytes 393220
  336.9 5.8 %copy-start.3 = (f32[16,2048]{1,0:T(8,128)S(1)}, f32[16,2048]{1,0:T(8,128)}, u32[]{:S(2)}) copy-start(f32[16,2048]{1,0:T(8,128)} %qd_hbm.1) | copy-start | bytes 393220
  337.0 5.8 %copy-start.4 = (f32[16,2048]{1,0:T(8,128)S(1)}, f32[16,2048]{1,0:T(8,128)}, u32[]{:S(2)}) copy-start(f32[16,2048]{1,0:T(8,128)} %td_hbm.1) | copy-start | bytes 393220
  337.0 5.8 %copy-start.5 = (f32[3,16,2048]{2,1,0:T(8,128)S(1)}, f32[3,16,2048]{2,1,0:T(8,128)}, u32[]{:S(2)}) copy-start(f32[3,16,2048]{2,1,0:T(8,128)} %get-tuple-element.32) | copy-start | bytes 1179652
  337.0 5.8 %copy-start.6 = (f32[16,2048]{1,0:T(8,128)S(1)}, f32[16,2048]{1,0:T(8,128)}, u32[]{:S(2)}) copy-start(f32[16,2048]{1,0:T(8,128)} %param.29) | copy-start | bytes 393220
  337.0 5.8 %copy-start.7 = (f32[16,2048]{1,0:T(8,128)S(1)}, f32[16,2048]{1,0:T(8,128)}, u32[]{:S(2)}) copy-start(f32[16,2048]{1,0:T(8,128)} %param.28) | copy-start | bytes 393220
  337.0 5.8 %copy-start.8 = (f32[16,2048]{1,0:T(8,128)S(1)}, f32[16,2048]{1,0:T(8,128)}, u32[]{:S(2)}) copy-start(f32[16,2048]{1,0:T(8,128)} %param.26) | copy-start | bytes 393220
  338.3 5.6 %copy-start.17 = (f32[2,2048]{1,0:T(2,128)S(1)}, f32[2,2048]{1,0:T(2,128)}, u32[]{:S(2)}) copy-start(f32[2,2048]{1,0:T(2,128)} %get-tuple-element.33) | copy-start | bytes 49156
  338.3 6.0 %copy-start.16 = (f32[2,2048]{1,0:T(2,128)S(1)}, f32[2,2048]{1,0:T(2,128)}, u32[]{:S(2)}) copy-start(f32[2,2048]{1,0:T(2,128)} %get-tuple-element.34) | copy-start | bytes 49156
  338.3 6.4 %copy-start.9 = (f32[2,2048]{1,0:T(2,128)S(1)}, f32[2,2048]{1,0:T(2,128)}, u32[]{:S(2)}) copy-start(f32[2,2048]{1,0:T(2,128)} %proj_norm.1) | copy-start | bytes 49156
  338.3 6.4 %copy-start.10 = (f32[2,2048]{1,0:T(2,128)S(1)}, f32[2,2048]{1,0:T(2,128)}, u32[]{:S(2)}) copy-start(f32[2,2048]{1,0:T(2,128)} %pred_norm.1) | copy-start | bytes 49156
  338.3 6.4 %copy-start.11 = (f32[2,2048]{1,0:T(2,128)S(1)}, f32[2,2048]{1,0:T(2,128)}, u32[]{:S(2)}) copy-start(f32[2,2048]{1,0:T(2,128)} %target_norm.1) | copy-start | bytes 49156
  338.4 6.4 %copy-start.14 = (f32[2,2048]{1,0:T(2,128)S(1)}, f32[2,2048]{1,0:T(2,128)}, u32[]{:S(2)}) copy-start(f32[2,2048]{1,0:T(2,128)} %param.27) | copy-start | bytes 49156
  338.4 6.4 %copy-start.15 = (f32[2,2048]{1,0:T(2,128)S(1)}, f32[2,2048]{1,0:T(2,128)}, u32[]{:S(2)}) copy-start(f32[2,2048]{1,0:T(2,128)} %param.30) | copy-start | bytes 49156
  344.3 6.1 %copy-start.12 = (f32[2,2048]{1,0:T(2,128)}, f32[2,2048]{1,0:T(2,128)S(1)}, u32[]{:S(2)}) copy-start(f32[2,2048]{1,0:T(2,128)S(1)} %rev.6) | copy-start | bytes 49156
  344.8 5.6 %copy-start.13 = (f32[2,2048]{1,0:T(2,128)}, f32[2,2048]{1,0:T(2,128)S(1)}, u32[]{:S(2)}) copy-start(f32[2,2048]{1,0:T(2,128)S(1)} %rev.7) | copy-start | bytes 49156
  345.5 4.9 %copy-start = (f32[128,2048]{1,0:T(8,128)S(1)}, f32[128,2048]{1,0:T(8,128)}, u32[]{:S(2)}) copy-start(f32[128,2048]{1,0:T(8,128)} %get-tuple-element.87) | copy-start | bytes 3145732

commit v4 on v3

--- a/solution.py
+++ b/solution.py
@@ -304,8 +304,15 @@
     )
 
 
-def gelu_tanh(value):
-    return jnp.tanh(GELU_A * (value + GELU_B * value * value * value))
+def gelu_parts(value):
+    square = value * value
+    gate = 0.5 + 0.5 * jnp.tanh(value * (GELU_A + (GELU_A * GELU_B) * square))
+    return gate, square
+
+
+def gelu_slope(value, gate, square):
+    bend = value * (2.0 * GELU_A + (6.0 * GELU_A * GELU_B) * square)
+    return gate * (1.0 + (1.0 - gate) * bend)
 
 
 def step_kernel(
@@ -324,7 +331,9 @@
     keep,
     ig_hbm,
     gu_out,
-    gs_out,
+    qd_out,
+    qu_out,
+    pd_out,
     proj_stat,
     pred_stat,
     loss_out,
@@ -341,6 +350,7 @@
     acc,
     ex,
     exr,
+    slope1,
     sr1,
     sr2,
     sr3,
@@ -415,22 +425,25 @@
         )
     ]
     loads.append(pltpu.make_async_copy(x_hbm, feats, load_sem.at[6]))
-    for load in loads:
-        load.start()
-    for load in loads[:4]:
-        load.wait()
-    for w in range(4):
-        small[w, me[0], me[1], me[2]] = wide[
-            pl.ds(2 * rows + w * small_rows, small_rows), :
-        ].astype(jnp.bfloat16)
-    pl.semaphore_wait(barrier, len(greet))
+    for i in (4, 0, 1, 2, 3, 5, 6):
+        loads[i].start()
 
     def take(load, buffer, start):
         load.wait()
         buffer[me[0], me[1], me[2]] = wide[pl.ds(start, rows), :].astype(jnp.bfloat16)
 
+    def take_small():
+        for w, load in enumerate(loads[:4]):
+            load.wait()
+            small[w, me[0], me[1], me[2]] = wide[
+                pl.ds(2 * rows + w * small_rows, small_rows), :
+            ].astype(jnp.bfloat16)
+
+    take(loads[4], up, 0)
+    pl.semaphore_wait(barrier, len(greet))
+
     hops = n0 - 1
-    kinds = [("small", 0)] + [("up", i) for i in range(4)]
+    kinds = [("up", i) for i in range(4)] + [("small", 0)]
     kinds += [("target", i) for i in (0, 1, 3)]
     main = len(kinds)
     kinds += [("target", 2), ("small", 1)]
@@ -551,7 +564,7 @@
         ]
 
     narrow_sum = (pa, pb, ps_s, ps_r)
-    whole_sum = (qa, qb, qs_s, qs_r)
+    half_sum = (qa, qb, qs_s, qs_r)
     scalar_sum = (ta, tb, ts_s, ts_r)
 
     def sum_start(buffers, i):
@@ -581,7 +594,7 @@
     def swap(i):
         return pltpu.make_async_remote_copy(
             src_ref=ex.at[i],
-            dst_ref=exr.at[i],
+            dst_ref=exr.at[i % 2],
             send_sem=ex_s.at[i],
             recv_sem=ex_r.at[i],
             device_id=other,
@@ -594,7 +607,7 @@
         def add(b):
             part = pl.ds(pl.multiple_of(b * rows, rows), rows)
             ex[i, part, :] = (
-                ex[i, part, :].astype(jnp.float32) + exr[i, part, :].astype(jnp.float32)
+                ex[i, part, :].astype(jnp.float32) + exr[i % 2, part, :].astype(jnp.float32)
             ).astype(jnp.bfloat16)
 
         loop(blocks, add)
@@ -621,61 +634,82 @@
         mean = total[0:1] / total_views
         return mean, lax.rsqrt(total[1:2] / total_views - mean * mean + NORM_EPS)
 
-    def act_tiles(start, count, mean, inverse, norm, act_ref, hat_ref, act_start):
-        for n in range(count):
-            columns = pl.ds(start + n * TILE, TILE)
-            targets = pl.ds(act_start + n * TILE, TILE)
+    def act_tile(start, mean, inverse, norm, act_ref, hat_ref, act_start):
+        columns = pl.ds(start, TILE)
+        targets = pl.ds(act_start, TILE)
+        gain, shift = norm[0:1, columns], norm[1:2, columns]
+
+        def one(b):
+            part = pl.ds(pl.multiple_of(b * rows, rows), rows)
+            hat = (wide[part, columns] - mean) * inverse
+            value = hat * gain + shift
+            gate, square = gelu_parts(value)
+            act_ref[b // 2, b % 2, :, targets] = (value * gate).astype(jnp.bfloat16)
+            if hat_ref is not None:
+                hat_ref[b // 2, b % 2, :, targets] = hat.astype(jnp.bfloat16)
+                slope1[b // 2, b % 2, :, targets] = gelu_slope(value, gate, square).astype(
+                    jnp.bfloat16
+                )
+
+        loop(blocks, one)
+
+    def act_online(i):
+        mean, inverse = spread(sum_end(narrow_sum, i))
+        inv1[:, pl.ds(i * chunk, chunk)] = inverse
+        for n in range(chunk // TILE):
+            start = i * chunk + n * TILE
             here = slice(n * TILE, (n + 1) * TILE)
-            mean_n, inverse_n = mean[:, here], inverse[:, here]
-            gain, shift = norm[0:1, columns], norm[1:2, columns]
-
-            def one(b):
-                part = pl.ds(pl.multiple_of(b * rows, rows), rows)
-                hat = (wide[part, columns] - mean_n) * inverse_n
-                value = hat * gain + shift
-                action = 0.5 * value * (1.0 + gelu_tanh(value))
-                act_ref[b // 2, b % 2, :, targets] = action.astype(jnp.bfloat16)
-                if hat_ref is not None:
-                    hat_ref[b // 2, b % 2, :, targets] = hat.astype(jnp.bfloat16)
-
-            loop(blocks, one)
-
-    def act_chunk(slot, i, norm, act_ref, hat_ref, inv_ref, w, act_start):
-        total = sum_end(narrow_sum, slot)
-        mean, inverse = spread(total)
-        if inv_ref is not None:
-            inv_ref[:, pl.ds(i * chunk, chunk)] = inverse
-        act_tiles(i * chunk, chunk // TILE, mean, inverse, norm, act_ref, hat_ref, act_start)
-        action = act_ref[:, :, :, pl.ds(act_start, chunk)].reshape(views, chunk)
-        product = nt_dot(action, weight(w, pl.ds(i * chunk, chunk)))
-        if i == 0:
-            acc[...] = product
-        else:
-            acc[...] += product
-        return total
+            act_tile(start, mean[:, here], inverse[:, here], proj_norm, act1, hat1, start)
+
+    def act_target(i):
+        mean, inverse = spread(sum_end(narrow_sum, 4 + i))
+        for n in range(chunk // TILE):
+            start = i * chunk + n * TILE
+            here = slice(n * TILE, (n + 1) * TILE)
+            act_tile(start, mean[:, here], inverse[:, here], target_norm, tact, None, 0)
+            product = nt_dot(tact[...].reshape(views, TILE), weight(3, pl.ds(start, TILE)))
+            if start == 0:
+                acc[...] = product
+            else:
+                acc[...] += product
 
     count = []
 
-    def middle_stats():
+    def sum_rows(i, columns, first_row, second_row):
+        qa[i, mp, 0:1, columns] = first_row
+        qa[i, mp, 1:2, columns] = second_row
+
+    def online_middle():
+        ex[0] = nt_dot(act1[...].reshape(views, width), weight(0, pl.ds(0, width))).astype(
+            jnp.bfloat16
+        )
+        swap(0).start()
         swap_end(0)
+        for side in range(2):
+
+            def one(n):
+                columns = columns_at(side * half + n * TILE, TILE)
+                values = jnp.dot(ex[0], weight(1, columns), preferred_element_type=jnp.float32)
+                sum_rows(
+                    side,
+                    columns_at(n * TILE, TILE),
+                    jnp.sum(values, 0, keepdims=True),
+                    jnp.sum(values * values, 0, keepdims=True),
+                )
+
+            loop(half // TILE, one)
+            sum_start(half_sum, side)
+
+    def online_query():
+        for side in range(2):
+            mean, inverse = spread(sum_end(half_sum, side))
+            inv2[:, pl.ds(side * half, half)] = inverse
+            means[:, pl.ds(side * half, half)] = mean
+        spare = pl.ds(3 * chunk, TILE)
 
         def one(n):
             columns = columns_at(n * TILE, TILE)
-            values = jnp.dot(ex[0], weight(1, columns), preferred_element_type=jnp.float32)
-            qa[0, mp, 0:1, columns] = jnp.sum(values, 0, keepdims=True)
-            qa[0, mp, 1:2, columns] = jnp.sum(values * values, 0, keepdims=True)
-
-        loop(width // TILE, one)
-        sum_start(whole_sum, 0)
-
-    def online_query():
-        mean, inverse = spread(sum_end(whole_sum, 0))
-        inv2[...] = inverse
-        means[...] = mean
-
-        def one(n):
-            columns = columns_at(n * TILE, TILE)
-            wide[:, pl.ds(3 * chunk, TILE)] = jnp.dot(
+            wide[:, spare] = jnp.dot(
                 ex[0], weight(1, columns), preferred_element_type=jnp.float32
             )
             mean_n, inverse_n = means[:, columns], inv2[:, columns]
@@ -683,10 +717,10 @@
 
             def tile(b):
                 part = pl.ds(pl.multiple_of(b * rows, rows), rows)
-                hat = (wide[part, pl.ds(3 * chunk, TILE)] - mean_n) * inverse_n
+                hat = (wide[part, spare] - mean_n) * inverse_n
                 value = hat * gain + shift
-                action = 0.5 * value * (1.0 + gelu_tanh(value))
-                act2[b // 2, b % 2, :, columns] = action.astype(jnp.bfloat16)
+                gate, _ = gelu_parts(value)
+                act2[b // 2, b % 2, :, columns] = (value * gate).astype(jnp.bfloat16)
                 hat2[b // 2, b % 2, :, columns] = hat.astype(jnp.bfloat16)
 
             loop(blocks, tile)
@@ -697,44 +731,42 @@
         ).astype(jnp.bfloat16)
         swap(1).start()
 
-    def early(c):
-        slot = c - 3
-        if 0 <= slot <= 3:
-            act_chunk(slot, slot, proj_norm, act1, hat1, inv1, 0, slot * chunk)
-        elif slot >= 4:
-            act_chunk(slot, slot - 4, target_norm, tact, None, None, 3, 0)
-        if slot == 3:
-            ex[0] = acc[...].astype(jnp.bfloat16)
-            swap(0).start()
-            middle_stats()
-        if slot == 5:
-            online_query()
-
-    def between(c):
-        if c >= 2:
-            sum_middle(narrow_sum, c - 2)
-        if c == 7:
-            sum_middle(whole_sum, 0)
-        if c == 3:
+    def forward(tick):
+        gather_side(tick, 0)
+        for ahead, hop in ((1, 2), (2, 1), (3, 0)):
+            if tick + ahead < main:
+                gather_line(tick + ahead, hop)
+        if tick >= 1:
+            for _ in range(LATE_PER_TICK):
+                late_next()
+            gather_side(tick - 1, 1)
+
+    def hidden(slot):
+        hidden_chunk(up if slot < 4 else tup, slot % 4, slot)
+        sum_start(narrow_sum, slot)
+
+    def after(tick):
+        if tick == 2:
+            loads[6].wait()
+            kept = jnp.sum(jnp.sum(keep[...], 0, keepdims=True), 1, keepdims=True)
+            ta[0, mp] = jnp.broadcast_to(kept, (8, 128))
+            sum_start(scalar_sum, 0)
+        if tick <= 5:
+            hidden(tick - 2)
+        if tick == 4:
             sum_middle(scalar_sum, 0)
-
-    def compute(c):
-        if c == 0:
-            loads[6].wait()
-            ta[0, mp] = jnp.broadcast_to(jnp.sum(keep[...], 0, keepdims=True), (8, 128))
-            sum_start(scalar_sum, 0)
-        else:
-            i = c - 1
-            hidden_chunk(up if i < 4 else tup, i % 4, i)
-            sum_start(narrow_sum, i)
-        if c == 4:
+        if 3 <= tick <= 6:
+            sum_middle(narrow_sum, tick - 3)
+        if tick >= 4:
+            act_online(tick - 4)
+        if tick == 6:
             count.append(sum_end(scalar_sum, 0))
 
     gather_line(0, 0)
+    take_small()
     gather_side(late[0], 0)
     take(loads[5], tup, rows)
     gather_side(late[1], 0)
-    take(loads[4], up, 0)
     gather_line(1, 0)
     gather_line(0, 1)
     gather_line(2, 0)
@@ -742,38 +774,39 @@
     gather_line(0, 2)
     for c in late:
         gather_side(c, 1)
-    for tick in range(main + 2):
-        if tick < main:
-            gather_side(tick, 0)
-        for ahead, hop in ((1, 2), (2, 1), (3, 0)):
-            if tick + ahead < main:
-                gather_line(tick + ahead, hop)
-        if tick >= 1:
-            for _ in range(LATE_PER_TICK):
-                late_next()
-        if 1 <= tick <= main:
-            gather_side(tick - 1, 1)
-        if 2 <= tick <= main:
-            early(tick - 2)
-            between(tick - 2)
+    for tick in range(main - 1):
+        forward(tick)
+        if tick >= 2:
             gather_end(tick - 2)
-            compute(tick - 2)
+            after(tick)
+    forward(main - 1)
+    after(main - 1)
+    online_middle()
+    gather_side(main - 1, 1)
+    gather_end(main - 3)
+    hidden(4)
+    gather_end(main)
+    hidden(6)
+    sum_middle(half_sum, 0)
+    sum_middle(half_sum, 1)
+    sum_middle(narrow_sum, 4)
+    gather_end(main - 2)
+    hidden(5)
     gather_end(main + 1)
-    early(main - 1)
-    between(main - 1)
-    gather_end(main)
-    compute(main - 1)
-    early(main)
-    between(main)
+    online_query()
+    act_target(0)
+    sum_middle(narrow_sum, 6)
+    sum_middle(narrow_sum, 5)
     gather_end(main - 1)
-    compute(main)
-    early(main + 1)
+    hidden(7)
+    swap_end(1)
+    act_target(1)
+    act_target(2)
     sum_middle(narrow_sum, 7)
-    act_chunk(7, 3, target_norm, tact, None, None, 3, 0)
+    act_target(3)
     ex[2] = acc[...].astype(jnp.bfloat16)
     swap(2).start()
     gather_sent()
-    swap_end(1)
     swap(2).wait()
 
     scale = -2.0 / count[0][0:1, 0:1]
@@ -782,17 +815,19 @@
         return lax.rsqrt(jnp.sum(values * values, 1, keepdims=True) + UNIT_EPS)
 
     even = (lax.broadcasted_iota(jnp.int32, (rows, acc.shape[1]), 0) % 2) == 0
+
+    spot = lax.broadcasted_iota(jnp.int32, (rows, blocks), 1)
 
     def loss_tile(b, carry):
         part = pl.ds(pl.multiple_of(b * rows, rows), rows)
         query = ex[1, part, :].astype(jnp.float32)
-        target = ex[2, part, :].astype(jnp.float32) + exr[2, part, :].astype(jnp.float32)
+        target = ex[2, part, :].astype(jnp.float32) + exr[0, part, :].astype(jnp.float32)
         target = target * unit_scale(target)
         goal = jnp.where(even, pltpu.roll(target, rows - 1, 0), pltpu.roll(target, 1, 0))
         back = unit_scale(query)
         unit = query * back
         cosine = jnp.sum(unit * goal, 1, keepdims=True)
-        kept = keep[part, :]
+        kept = jnp.sum(jnp.where(spot == b, keep[...], 0.0), 1, keepdims=True)
         ex[1, part, :] = ((scale * kept * back) * (goal - cosine * unit)).astype(jnp.bfloat16)
         return carry + kept * (2.0 - 2.0 * cosine)
 
@@ -800,7 +835,7 @@
     ta[1, mp] = jnp.broadcast_to(jnp.sum(loss_rows, 0, keepdims=True), (8, 128))
     sum_start(scalar_sum, 1)
 
-    def back_norm(i, w, grads, hat_ref, norm):
+    def back_norm(i, first, last, w, grads, hat_ref, norm, slope_ref):
         def one(n):
             columns = columns_at(n * TILE, TILE)
             wide[:, columns] = jnp.dot(
@@ -811,11 +846,11 @@
             def tile(b, carry):
                 part = pl.ds(pl.multiple_of(b * rows, rows), rows)
                 hat = hat_ref[b // 2, b % 2, :, columns].astype(jnp.float32)
-                value = hat * gain + shift
-                bent = gelu_tanh(value)
-                slope = 0.5 * (1.0 + bent) + (0.5 * GELU_A) * value * (1.0 - bent * bent) * (
-                    1.0 + (3.0 * GELU_B) * value * value
-                )
+                if slope_ref is None:
+                    value = hat * gain + shift
+                    slope = gelu_slope(value, *gelu_parts(value))
+                else:
+                    slope = slope_ref[b // 2, b % 2, :, columns].astype(jnp.float32)
                 grad = wide[part, columns] * slope
                 wide[part, columns] = grad
                 cross = grad * hat
@@ -826,11 +861,16 @@
 
             zero = jnp.zeros((8, TILE), jnp.float32)
             sums = lax.fori_loop(0, blocks, tile, (zero, zero))
-            qa[i, mp, 0:1, columns] = jnp.sum(sums[0], 0, keepdims=True)
-            qa[i, mp, 1:2, columns] = jnp.sum(sums[1], 0, keepdims=True)
-
-        loop(width // TILE, one)
-        sum_start(whole_sum, i)
+            sum_rows(
+                i,
+                columns_at((n % side_tiles) * TILE, TILE),
+                jnp.sum(sums[0], 0, keepdims=True),
+                jnp.sum(sums[1], 0, keepdims=True),
+            )
+
+        loop(last - first, lambda n: one(first + n))
+
+    side_tiles = half // TILE
 
     def grad_hidden(stat, hat_ref, norm, inv_ref, columns):
         gain = norm[0:1, columns] * inv_ref[:, columns]
@@ -855,43 +895,67 @@
 
         loop(width // TILE, one)
 
+    def plus(*terms):
+        total = terms[0].astype(jnp.float32)
+        for term in terms[1:]:
+            total = total + term.astype(jnp.float32)
+        return total
+
+    def low_plus(*terms):
+        return plus(*terms).astype(jnp.bfloat16)
+
+    up_parts = [("line", 0, TILE // 2)]
+    up_parts += [("side", TILE + g * chunk, TILE) for g in range(3)]
+    up_parts += [("side", TILE + 3 * chunk, TILE // 2)]
+
     def reduce_copies(kind, g, lane, phase):
         axis, second = ((1, 2), (2, 1))[lane]
-        if kind == "up":
-            columns = pl.ds(g * chunk + lane * TILE, TILE)
-            send, recv = rs_s, rs_r
-            source = lambda sel: tup.at[sel[0], sel[1], sel[2], :, columns]
-            lands = (
-                act2.at[:, :, :, columns],
-                hat2.at[:, 0, :, columns],
-                hat2.at[me[0], 1, :, columns],
-            )
-        else:
-            columns = pl.ds(lane * half, half)
-            send, recv = ss_s, ss_r
-            source = lambda sel: small.at[3 - g, sel[0], sel[1], sel[2], :, columns]
-            lands = (
-                sr1.at[g, :, :, :, columns],
-                sr2.at[g, :, :, columns],
-                sr3.at[g, me[0], :, columns],
-            )
+        style = up_parts[g][0] if kind == "up" else "side"
+        order = (0, axis, second) if style == "line" else (axis, second, 0)
+        sems = ((0, 3, 4) if style == "line" else (0, 1, 2))[phase]
+        send, recv = (rs_s, rs_r) if kind == "up" else (ss_s, ss_r)
+        axis_now = order[phase]
         copies = []
-        moves = range(1, n0) if phase == 2 else (1,)
-        for k in moves:
-            axis_now = (axis, second, 0)[phase]
+        for k in range(1, grid[axis_now]):
             target = moved(axis_now, k)
             sel = [slice(None)] * 3
-            if phase > 0:
-                sel[axis] = me[axis]
-            if phase > 1:
-                sel[second] = me[second]
+            for done in order[:phase]:
+                sel[done] = me[done]
             sel[axis_now] = target[axis_now]
+            if kind == "small":
+                columns = pl.ds(lane * half, half)
+                source = small.at[3 - g, sel[0], sel[1], sel[2], :, columns]
+                if phase == 0:
+                    land = sr1.at[g, :, :, :, columns]
+                elif phase == 1:
+                    land = sr2.at[g, :, :, columns]
+                else:
+                    land = sr3.at[g, me[0], :, columns]
+            else:
+                _, start, size = up_parts[g]
+                columns = pl.ds(start + lane * size, size)
+                source = tup.at[sel[0], sel[1], sel[2], :, columns]
+                if style == "line":
+                    if phase == 0:
+                        land = (act2 if k < 3 else hat2).at[
+                            pl.ds(2 * ((k - 1) % 2), 2), :, :, columns
+                        ]
+                    elif phase == 1:
+                        land = hat2.at[2, :, :, columns]
+                    else:
+                        land = hat2.at[3, 0, :, columns]
+                elif phase == 0:
+                    land = act2.at[:, :, :, columns]
+                elif phase == 1:
+                    land = hat2.at[:, 0, :, columns]
+                else:
+                    land = hat2.at[me[0], 1, :, columns]
             copies.append(
                 pltpu.make_async_remote_copy(
-                    src_ref=source(sel),
-                    dst_ref=lands[phase],
-                    send_sem=send.at[g, lane, phase + k - 1],
-                    recv_sem=recv.at[g, lane, phase + k - 1],
+                    src_ref=source,
+                    dst_ref=land,
+                    send_sem=send.at[g, lane, sems + k - 1],
+                    recv_sem=recv.at[g, lane, sems + k - 1],
                     device_id=place(target),
                     device_id_type=MESH,
                 )
@@ -903,94 +967,165 @@
             if phase:
                 for copy in reduce_copies(kind, g, lane, phase - 1):
                     copy.wait()
-                reduce_add(kind, g, lane, phase)
+                if kind == "small":
+                    small_add(g, lane, phase)
+                elif up_parts[g][0] == "line":
+                    line_add(g, lane, phase)
+                else:
+                    side_add(g, lane, phase)
             if phase < 3:
                 for copy in reduce_copies(kind, g, lane, phase):
                     copy.start()
 
-    def plus(first_op, second_op):
-        return (first_op.astype(jnp.float32) + second_op.astype(jnp.float32)).astype(jnp.bfloat16)
-
-    def reduce_add(kind, g, lane, phase):
-        big = kind == "up"
-        if big:
-            columns = pl.ds(g * chunk + lane * TILE, TILE)
-        else:
-            columns = pl.ds(lane * half, half)
+    def plane_spot(lane, i):
+        return (me[1], i) if lane == 0 else (i, me[2])
+
+    def small_add(g, lane, phase):
+        columns = pl.ds(lane * half, half)
+        w = 3 - g
         if phase == 1:
 
             def add(j):
                 z, i = j // 2, j % 2
-                y, x = (me[1], i) if lane == 0 else (i, me[2])
-                if big:
-                    tup[z, y, x, :, columns] = plus(
-                        tup[z, y, x, :, columns], act2[z, i, :, columns]
-                    )
-                else:
-                    small[3 - g, z, y, x, :, columns] = plus(
-                        small[3 - g, z, y, x, :, columns], sr1[g, z, i, :, columns]
-                    )
+                y, x = plane_spot(lane, i)
+                small[w, z, y, x, :, columns] = low_plus(
+                    small[w, z, y, x, :, columns], sr1[g, z, i, :, columns]
+                )
 
             loop(n0 * 2, add)
         elif phase == 2:
 
             def add(z):
-                if big:
-                    tup[z, me[1], me[2], :, columns] = plus(
-                        tup[z, me[1], me[2], :, columns], hat2[z, 0, :, columns]
-                    )
-                else:
-                    small[3 - g, z, me[1], me[2], :, columns] = plus(
-                        small[3 - g, z, me[1], me[2], :, columns], sr2[g, z, :, columns]
-                    )
+                small[w, z, me[1], me[2], :, columns] = low_plus(
+                    small[w, z, me[1], me[2], :, columns], sr2[g, z, :, columns]
+                )
 
             loop(n0, add)
         else:
-            if big:
-                total = tup[me[0], me[1], me[2], :, columns].astype(jnp.float32)
-                for k in range(1, n0):
-                    total = total + hat2[(me[0] + k) % n0, 1, :, columns].astype(jnp.float32)
-                gu_out[:, columns] = total
-            else:
-                total = small[3 - g, me[0], me[1], me[2], :, columns].astype(jnp.float32)
-                for k in range(1, n0):
-                    total = total + sr3[g, (me[0] + k) % n0, :, columns].astype(jnp.float32)
-                gs_out[g, :, columns] = total
-
-    back_norm(1, 2, 1, hat2, pred_norm)
+            (qd_out, qu_out, pd_out)[g][:, columns] = low_plus(
+                small[w, me[0], me[1], me[2], :, columns],
+                *[sr3[g, (me[0] + k) % n0, :, columns] for k in range(1, n0)],
+            )
+
+    def side_add(g, lane, phase):
+        _, start, size = up_parts[g]
+        columns = pl.ds(start + lane * size, size)
+        if phase == 1:
+
+            def add(j):
+                z, i = j // 2, j % 2
+                y, x = plane_spot(lane, i)
+                tup[z, y, x, :, columns] = low_plus(
+                    tup[z, y, x, :, columns], act2[z, i, :, columns]
+                )
+
+            loop(n0 * 2, add)
+        elif phase == 2:
+
+            def add(z):
+                tup[z, me[1], me[2], :, columns] = low_plus(
+                    tup[z, me[1], me[2], :, columns], hat2[z, 0, :, columns]
+                )
+
+            loop(n0, add)
+        else:
+            gu_out[:, columns] = low_plus(
+                tup[me[0], me[1], me[2], :, columns],
+                *[hat2[(me[0] + k) % n0, 1, :, columns] for k in range(1, n0)],
+            )
+
+    def line_add(g, lane, phase):
+        _, start, size = up_parts[g]
+        columns = pl.ds(start + lane * size, size)
+        z = me[0]
+        if phase == 1:
+
+            def add(j):
+                y, x = j // 2, j % 2
+                tup[z, y, x, :, columns] = low_plus(
+                    tup[z, y, x, :, columns],
+                    act2[y, x, :, columns],
+                    act2[2 + y, x, :, columns],
+                    hat2[y, x, :, columns],
+                )
+
+            loop(plane, add)
+        elif phase == 2:
+
+            def add(i):
+                y, x = plane_spot(lane, i)
+                tup[z, y, x, :, columns] = low_plus(
+                    tup[z, y, x, :, columns], hat2[2, i, :, columns]
+                )
+
+            loop(2, add)
+        else:
+            gu_out[:, columns] = low_plus(
+                tup[z, me[1], me[2], :, columns], hat2[3, 0, :, columns]
+            )
+
+    def pred_half(side):
+        pred_stat[:, pl.ds(side * half, half)] = sum_end(half_sum, 2 + side)
+
+        def one(n):
+            columns = columns_at(side * half + n * TILE, TILE)
+            grad_hidden(pred_stat, hat2, pred_norm, inv2, columns)
+
+        loop(side_tiles, one)
+        columns = pl.ds(side * half, half)
+        product = nt_dot(hat2[:, :, :, columns].reshape(views, half), weight(1, columns))
+        if side == 0:
+            acc[...] = product
+        else:
+            acc[...] += product
+
+    middle_tile = side_tiles + side_tiles // 2
+    pred_args = (2, 1, hat2, pred_norm, None)
+    back_norm(2, 0, side_tiles, *pred_args)
+    sum_start(half_sum, 2)
+    back_norm(3, side_tiles, middle_tile, *pred_args)
+    sum_middle(half_sum, 2)
+    back_norm(3, middle_tile, 2 * side_tiles, *pred_args)
+    sum_start(half_sum, 3)
     small_grad(3, 1, act2)
+    sum_middle(half_sum, 3)
     reduce_step("small", 0, 0)
-    sum_middle(whole_sum, 1)
-    pred_stat[...] = sum_end(whole_sum, 1)
-    loop(
-        width // TILE,
-        lambda n: grad_hidden(pred_stat, hat2, pred_norm, inv2, columns_at(n * TILE, TILE)),
-    )
-    ex[3] = nt_dot(hat2[...].reshape(views, width), weight(1, pl.ds(0, width))).astype(jnp.bfloat16)
+    pred_half(0)
+    pred_half(1)
+    ex[3] = acc[...].astype(jnp.bfloat16)
     swap(3).start()
     small_grad(2, 0, hat2)
     reduce_step("small", 1, 0)
     reduce_step("small", 0, 1)
     swap_end(3)
-    back_norm(2, 0, 3, hat1, proj_norm)
-    sum_middle(scalar_sum, 1)
+    proj_args = (0, 3, hat1, proj_norm, slope1)
+    back_norm(4, 0, side_tiles, *proj_args)
+    sum_start(half_sum, 4)
+    back_norm(5, side_tiles, middle_tile, *proj_args)
+    sum_middle(half_sum, 4)
+    reduce_step("small", 1, 1)
+    reduce_step("small", 0, 2)
+    back_norm(5, middle_tile, 2 * side_tiles, *proj_args)
+    sum_start(half_sum, 5)
     small_grad(1, 3, act1)
     pl.semaphore_signal(ready, inc=1, device_id=other, device_id_type=MESH)
-    reduce_step("small", 2, 0)
-    reduce_step("small", 1, 1)
-    reduce_step("small", 0, 2)
-    sum_middle(whole_sum, 2)
-    proj_stat[...] = sum_end(whole_sum, 2)
+    sum_middle(half_sum, 5)
+    sum_middle(scalar_sum, 1)
+    proj_stat[:, pl.ds(0, half)] = sum_end(half_sum, 4)
+
+    def up_hidden(g):
+        _, start, size = up_parts[g]
+        for n in range(2 * size // TILE):
+            grad_hidden(proj_stat, hat1, proj_norm, inv1, pl.ds(start + n * TILE, TILE))
 
     def up_grad(g):
-        for n in range(2):
-            grad_hidden(proj_stat, hat1, proj_norm, inv1, pl.ds(g * chunk + n * TILE, TILE))
-        columns = pl.ds(g * chunk, chunk)
+        _, start, size = up_parts[g]
+        columns = pl.ds(start, 2 * size)
 
         def one(z):
             left = feats[:, columns_at(z * plane * rows, plane * rows)]
-            value = tn_dot(left, hat1[:, :, :, columns].reshape(views, chunk))
-            tup[z, :, :, :, columns] = value.astype(jnp.bfloat16).reshape(n1, n2, rows, chunk)
+            value = tn_dot(left, hat1[:, :, :, columns].reshape(views, 2 * size))
+            tup[z, :, :, :, columns] = value.astype(jnp.bfloat16).reshape(n1, n2, rows, 2 * size)
 
         loop(n0, one)
         reduce_step("up", g, 0)
@@ -1012,20 +1147,6 @@
         matrix = up[first, q % n1].reshape(n2 * rows, width)
         return nt_dot(hat1[...].reshape(views, width), matrix)
 
-    for g in range(4):
-        up_grad(g)
-        if g == 0:
-            reduce_step("small", 2, 1)
-            reduce_step("small", 1, 2)
-        else:
-            reduce_step("up", g - 1, 1)
-        if g == 1:
-            reduce_step("small", 0, 3)
-            reduce_step("small", 2, 2)
-        if g >= 2:
-            reduce_step("up", g - 2, 2)
-    pl.semaphore_wait(ready, 1)
-
     def send_part(q):
         act1[:, :, :, pl.ds(q * TILE, TILE)] = (
             input_product(q, 1 - core).astype(jnp.bfloat16).reshape(n0, 2, rows, TILE)
@@ -1035,35 +1156,60 @@
     def own_part(q):
         wide[:, pl.ds(q * TILE, TILE)] = input_product(q, core)
 
-    for q in range(2):
-        send_part(q)
+    up_hidden(0)
+    up_grad(0)
+    reduce_step("small", 2, 0)
+    up_hidden(1)
+    up_grad(1)
+    proj_stat[:, pl.ds(half, half)] = sum_end(half_sum, 5)
+    for g in (2, 3, 4):
+        up_hidden(g)
+    up_grad(2)
+    reduce_step("small", 1, 2)
+    reduce_step("small", 0, 3)
+    pl.semaphore_wait(ready, 1)
+    send_part(0)
+    reduce_step("up", 1, 1)
+    up_grad(3)
+    reduce_step("small", 2, 1)
+    send_part(1)
+    send_part(2)
+    reduce_step("up", 0, 1)
+    reduce_step("up", 2, 1)
+    up_grad(4)
+    reduce_step("up", 1, 2)
+    reduce_step("small", 2, 2)
+    reduce_step("small", 1, 3)
+    send_part(3)
+    own_part(0)
+    reduce_step("up", 0, 2)
     reduce_step("up", 3, 1)
     reduce_step("up", 2, 2)
-    for q in range(2, parts):
-        send_part(q)
-    for q in range(parts):
-        own_part(q)
+    own_part(1)
+    own_part(2)
+    reduce_step("up", 4, 1)
     reduce_step("up", 3, 2)
-    out_copies = []
+    own_part(3)
     for q in range(parts):
         input_copy(q).wait()
 
         def add(b, q=q):
             part = pl.ds(pl.multiple_of(b * rows, rows), rows)
-            wide[part, pl.ds(q * TILE, TILE)] += act1[
-                b // 2, b % 2, :, pl.ds((parts + q) * TILE, TILE)
-            ].astype(jnp.float32)
+            theirs = act1[b // 2, b % 2, :, pl.ds((parts + q) * TILE, TILE)]
+            act1[b // 2, b % 2, :, pl.ds(q * TILE, TILE)] = low_plus(
+                wide[part, pl.ds(q * TILE, TILE)], theirs
+            )
 
         loop(blocks, add)
     out_copy = pltpu.make_async_copy(
-        wide.at[:, pl.ds(0, parts * TILE)], ig_hbm, load_sem.at[0]
+        act1.at[:, :, :, pl.ds(0, parts * TILE)], ig_hbm, load_sem.at[0]
     )
     out_copy.start()
-    for g in (1, 2):
-        reduce_step("small", g, 3)
-    for g in range(4):
+    reduce_step("up", 4, 2)
+    reduce_step("small", 2, 3)
+    loss_out[...] = sum_end(scalar_sum, 1) / count[0]
+    for g in range(5):
         reduce_step("up", g, 3)
-    loss_out[...] = sum_end(scalar_sum, 1) / count[0]
     out_copy.wait()
 
 
@@ -1086,15 +1232,17 @@
     return pl.pallas_call(
         functools.partial(step_kernel, grid, total_views),
         out_shape=(
-            jax.ShapeDtypeStruct((views, depth // 2), full),
-            jax.ShapeDtypeStruct((rows, width), full),
-            jax.ShapeDtypeStruct((3, small_rows, width), full),
+            jax.ShapeDtypeStruct((n0, 2, rows, depth // 2), low),
+            jax.ShapeDtypeStruct((rows, width), low),
+            jax.ShapeDtypeStruct((small_rows, width), low),
+            jax.ShapeDtypeStruct((small_rows, width), low),
+            jax.ShapeDtypeStruct((small_rows, width), low),
             jax.ShapeDtypeStruct((2, width), full),
             jax.ShapeDtypeStruct((2, width), full),
             jax.ShapeDtypeStruct((8, 128), full),
         ),
         in_specs=[anywhere] * 7 + [inside] * 4,
-        out_specs=(anywhere,) + (inside,) * 5,
+        out_specs=(anywhere,) + (inside,) * 7,
         scratch_shapes=[
             vm((views, depth), low),
             vm((n0, n1, n2, rows, width), low),
@@ -1105,10 +1253,11 @@
             vm(spread_shape, low),
             vm(spread_shape, low),
             vm((views, width), full),
-            vm((n0, 2, rows, width // 4), low),
+            vm((n0, 2, rows, TILE), low),
             vm((views, out), full),
             vm((4, views, out), low),
-            vm((4, views, out), low),
+            vm((2, views, out), low),
+            vm(spread_shape, low),
             vm((3, n0, 2, small_rows, width), low),
             vm((3, n0, small_rows, width), low),
             vm((3, n0, small_rows, width), low),
@@ -1117,8 +1266,8 @@
             vm((1, width), full),
             vm((8, plane, 2, width // 4), full),
             vm((8, n0, 2, width // 4), full),
-            vm((3, plane, 2, width), full),
-            vm((3, n0, 2, width), full),
+            vm((6, plane, 2, width // 2), full),
+            vm((6, n0, 2, width // 2), full),
             vm((2, plane, 8, 128), full),
             vm((2, n0, 8, 128), full),
             dma((7,)),
@@ -1126,14 +1275,14 @@
             dma((10, 2, moves)),
             dma((8, sum_moves)),
             dma((8, sum_moves)),
-            dma((3, sum_moves)),
-            dma((3, sum_moves)),
+            dma((6, sum_moves)),
+            dma((6, sum_moves)),
             dma((2, sum_moves)),
             dma((2, sum_moves)),
             dma((4,)),
             dma((4,)),
-            dma((4, 2, n0 + 1)),
-            dma((4, 2, n0 + 1)),
+            dma((5, 2, n0 + 1)),
+            dma((5, 2, n0 + 1)),
             dma((3, 2, n0 + 1)),
             dma((3, 2, n0 + 1)),
             dma((parts,)),
@@ -1169,16 +1318,19 @@
     if grid is None:
         return plain_body(*args)
     total_views = float(features.shape[0] * lax.axis_size("dp"))
-    input_grad, shard_proj_up, shard_small, proj_stat, pred_stat, loss = kernel_step(
+    (input_grad, *shards, proj_stat, pred_stat, loss) = kernel_step(
         grid,
         total_views,
         features,
-        keep_mask.astype(jnp.float32).reshape(-1, 1),
+        keep_mask.astype(jnp.float32).reshape(-1, proj_up.shape[0]).T,
         (proj_up, target_up),
         (proj_down, pred_up, pred_down, target_down),
         (proj_norm, pred_norm, target_norm),
     )
-    shard_pred_down, shard_pred_up, shard_proj_down = shard_small[0], shard_small[1], shard_small[2]
+    shard_proj_up, shard_pred_down, shard_pred_up, shard_proj_down = (
+        shard.astype(jnp.float32) for shard in shards
+    )
+    input_grad = input_grad.astype(jnp.float32).reshape(features.shape[0], -1)
     grad_proj_norm = proj_stat[::-1]
     grad_pred_norm = pred_stat[::-1]
     return finish(

time: 352 us -> 339 us (0.963)
  Pallas kernels: 335 us -> 325 us
  local copies, waits for them, and re-layouts: 9.08 us -> 2.99 us
    pallas_call x1, Pallas kernels: 335 us -> 325 us  [kernel_step(): pl.pallas_call(functools.partial(step_kernel, grid, total_views), out_sha...]
    unnamed x38 -> x46, local copies, waits for them, and re-layouts: 5.95 us -> 0.12 us
    reshape x0 -> x2, other arithmetic: none -> 4.76 us  [the longest x1 4.07 us: step_body(): input_grad = input_grad.astype(jnp.float32).reshape(features.shape[0], -1)]
where the time goes in v4:
time: 339 us; the launch traced here: 338 us
  Pallas kernels  325 us (96%)
  other arithmetic  9.44 us (3%)
    pallas_call x1, Pallas kernels, kernel_step(): pl.pallas_call(functools.partial(step_kernel, grid, total_views), out_sha...  325 us

profile of v4, /device:TPU:0, one launch (start us, length us, event | category | flops | bytes accessed | tf_op | source)
XLA Modules:
  0.0 338.3 jit_solution(9655977024139593877)
XLA Ops:
  0.7 0.7 convert_bitcast_fusion
  1.3 0.7 copy.40
  2.1 324.9 %shard_map.344 = (bf16[4,2,128,1024]{3,2,1,0:T(8,128)(2,1)}, bf16[128,2048]{1,0:T(8,128)(2,1)}, bf16[16,2048]{1,0:T(8,128)(2,1)}, bf16[16,2048]{1,0:T(8,128)(2,1...) custom-call(bf16[1024,2048]{1,0:T(8,128)(2,1)} %x_hbm.1, ...), custom_call_target="tpu_custom_call" | custom-call | tf_op jit(solution)/shard_map/pallas_call | solution.py:1232
  327.0 0.0 copy-start
  327.0 0.0 copy-start.1
  327.0 0.0 copy-start.2
  327.0 0.0 copy-start.3
  327.0 1.3 slice.3
  328.4 4.1 %bitcast_convert_fusion = f32[1024,1024]{1,0:T(8,128)} fusion(bf16[4,2,128,1024]{3,2,1,0:T(8,128)(2,1)} %get-tuple-element.32), kind=kLoop, calls=%fused_computation | loop fusion | flops 1048576 | bytes 6291456 | tf_op jit(solution)/shard_map/reshape | solution.py:1333
  332.4 0.0 copy-start.10
  332.5 0.0 copy-start.17
  332.5 0.0 copy-start.18
  332.5 0.0 copy-done
  332.5 0.0 copy-done.1
  332.5 0.0 copy-done.2
  332.5 0.0 copy-done.3
  332.5 0.0 copy-start.22
  332.5 0.0 copy-start.21
  332.5 0.0 copy-start.11
  332.6 0.0 copy-start.12
  332.6 0.0 copy-start.13
  332.6 0.0 copy-start.19
  332.6 0.0 copy-start.20
  332.6 0.0 copy-start.4
  332.6 0.0 copy-start.8
  332.6 0.0 copy-start.16
  332.6 2.3 add_multiply_fusion
  335.0 0.0 copy-done.5
  335.0 0.0 copy-done.6
  335.0 0.0 copy-done.7
  335.0 0.0 copy-done.9
  335.0 0.0 copy-done.10
  335.0 0.0 copy-done.17
  335.0 0.0 copy-done.18
  335.0 0.9 add_multiply_fusion.1
  335.9 0.0 copy-done.22
  335.9 0.4 rev.6
  336.3 0.0 copy-start.14
  336.3 0.0 copy-done.21
  336.4 0.4 rev.7
  336.8 0.0 copy-done.11
  336.8 0.0 copy-done.12
  336.8 0.0 copy-done.13
  336.8 0.0 copy-start.15
  336.8 0.7 add_multiply_fusion.2
  337.5 0.0 copy-done.4
  337.5 0.8 multiply_subtract_fusion.2
  338.3 0.0 copy-done.15
  (9 shorter events, 0.0 us)
Async XLA Ops:
  327.0 5.5 %copy-start = (f32[128,2048]{1,0:T(8,128)S(1)}, f32[128,2048]{1,0:T(8,128)}, u32[]{:S(2)}) copy-start(f32[128,2048]{1,0:T(8,128)} %pu_hbm.1) | copy-start | bytes 3145732
  327.0 5.5 %copy-start.1 = (f32[128,2048]{1,0:T(8,128)S(1)}, f32[128,2048]{1,0:T(8,128)}, u32[]{:S(2)}) copy-start(f32[128,2048]{1,0:T(8,128)} %tu_hbm.1) | copy-start | bytes 3145732
  327.0 5.5 %copy-start.2 = (f32[128,2048]{1,0:T(8,128)S(1)}, f32[128,2048]{1,0:T(8,128)}, u32[]{:S(2)}) copy-start(f32[128,2048]{1,0:T(8,128)} %param.25) | copy-start | bytes 3145732
  327.0 5.5 %copy-start.3 = (bf16[128,2048]{1,0:T(8,128)(2,1)S(1)}, bf16[128,2048]{1,0:T(8,128)(2,1)}, u32[]{:S(2)}) copy-start(bf16[128,2048]{1,0:T(8,128)(2,1)} %get-tuple-element.33) | copy-start | bytes 1572868
  332.4 2.5 copy-start.5
  332.4 2.5 copy-start.6
  332.4 2.5 copy-start.7
  332.4 2.5 copy-start.9
  332.4 2.5 copy-start.10
  332.5 2.5 copy-start.17
  332.5 2.5 copy-start.18
  332.5 3.4 %copy-start.22 = (f32[2,2048]{1,0:T(2,128)S(1)}, f32[2,2048]{1,0:T(2,128)}, u32[]{:S(2)}) copy-start(f32[2,2048]{1,0:T(2,128)} %get-tuple-element.35) | copy-start | bytes 49156
  332.5 3.8 %copy-start.21 = (f32[2,2048]{1,0:T(2,128)S(1)}, f32[2,2048]{1,0:T(2,128)}, u32[]{:S(2)}) copy-start(f32[2,2048]{1,0:T(2,128)} %get-tuple-element.38) | copy-start | bytes 49156
  332.5 4.2 %copy-start.11 = (f32[2,2048]{1,0:T(2,128)S(1)}, f32[2,2048]{1,0:T(2,128)}, u32[]{:S(2)}) copy-start(f32[2,2048]{1,0:T(2,128)} %proj_norm.1) | copy-start | bytes 49156
  332.6 4.2 %copy-start.12 = (f32[2,2048]{1,0:T(2,128)S(1)}, f32[2,2048]{1,0:T(2,128)}, u32[]{:S(2)}) copy-start(f32[2,2048]{1,0:T(2,128)} %pred_norm.1) | copy-start | bytes 49156
  332.6 4.2 %copy-start.13 = (f32[2,2048]{1,0:T(2,128)S(1)}, f32[2,2048]{1,0:T(2,128)}, u32[]{:S(2)}) copy-start(f32[2,2048]{1,0:T(2,128)} %target_norm.1) | copy-start | bytes 49156
  332.6 4.2 %copy-start.19 = (f32[2,2048]{1,0:T(2,128)S(1)}, f32[2,2048]{1,0:T(2,128)}, u32[]{:S(2)}) copy-start(f32[2,2048]{1,0:T(2,128)} %param.27) | copy-start | bytes 49156
  332.6 4.2 %copy-start.20 = (f32[2,2048]{1,0:T(2,128)S(1)}, f32[2,2048]{1,0:T(2,128)}, u32[]{:S(2)}) copy-start(f32[2,2048]{1,0:T(2,128)} %param.30) | copy-start | bytes 49156
  332.6 4.9 %copy-start.4 = (f32[16,2048]{1,0:T(8,128)S(1)}, f32[16,2048]{1,0:T(8,128)}, u32[]{:S(2)}) copy-start(f32[16,2048]{1,0:T(8,128)} %qu_hbm.1) | copy-start | bytes 393220
  332.6 4.9 %copy-start.8 = (f32[16,2048]{1,0:T(8,128)S(1)}, f32[16,2048]{1,0:T(8,128)}, u32[]{:S(2)}) copy-start(f32[16,2048]{1,0:T(8,128)} %param.28) | copy-start | bytes 393220
  332.6 4.9 %copy-start.16 = (bf16[16,2048]{1,0:T(8,128)(2,1)S(1)}, bf16[16,2048]{1,0:T(8,128)(2,1)}, u32[]{:S(2)}) copy-start(bf16[16,2048]{1,0:T(8,128)(2,1)} %get-tuple-element.36) | copy-start | bytes 196612
  336.3 2.0 copy-start.14
  336.8 1.5 copy-start.15

commit v5 on v4

--- a/solution.py
+++ b/solution.py
@@ -280,7 +280,7 @@
 TILE = 256
 GELU_A = math.sqrt(2.0 / math.pi)
 GELU_B = 0.044715
-LATE_PER_TICK = 2
+LATE_STEPS = (1, 2, 2, 2, 2, 2, 1)
 VMEM_LIMIT = 63 * 1024 * 1024
 
 
@@ -737,7 +737,7 @@
             if tick + ahead < main:
                 gather_line(tick + ahead, hop)
         if tick >= 1:
-            for _ in range(LATE_PER_TICK):
+            for _ in range(LATE_STEPS[tick - 1]):
                 late_next()
             gather_side(tick - 1, 1)
 
@@ -782,9 +782,9 @@
     forward(main - 1)
     after(main - 1)
     online_middle()
-    gather_side(main - 1, 1)
     gather_end(main - 3)
     hidden(4)
+    gather_side(main - 1, 1)
     gather_end(main)
     hidden(6)
     sum_middle(half_sum, 0)
@@ -795,14 +795,14 @@
     gather_end(main + 1)
     online_query()
     act_target(0)
+    gather_end(main - 1)
     sum_middle(narrow_sum, 6)
     sum_middle(narrow_sum, 5)
-    gather_end(main - 1)
     hidden(7)
     swap_end(1)
     act_target(1)
+    sum_middle(narrow_sum, 7)
     act_target(2)
-    sum_middle(narrow_sum, 7)
     act_target(3)
     ex[2] = acc[...].astype(jnp.bfloat16)
     swap(2).start()
@@ -1110,6 +1110,7 @@
     small_grad(1, 3, act1)
     pl.semaphore_signal(ready, inc=1, device_id=other, device_id_type=MESH)
     sum_middle(half_sum, 5)
+    reduce_step("small", 2, 0)
     sum_middle(scalar_sum, 1)
     proj_stat[:, pl.ds(0, half)] = sum_end(half_sum, 4)
 
@@ -1158,7 +1159,6 @@
 
     up_hidden(0)
     up_grad(0)
-    reduce_step("small", 2, 0)
     up_hidden(1)
     up_grad(1)
     proj_stat[:, pl.ds(half, half)] = sum_end(half_sum, 5)
@@ -1207,7 +1207,7 @@
     out_copy.start()
     reduce_step("up", 4, 2)
     reduce_step("small", 2, 3)
-    loss_out[...] = sum_end(scalar_sum, 1) / count[0]
+    loss_out[...] = (sum_end(scalar_sum, 1) / count[0])[0:1, 0:1]
     for g in range(5):
         reduce_step("up", g, 3)
     out_copy.wait()
@@ -1239,7 +1239,7 @@
             jax.ShapeDtypeStruct((small_rows, width), low),
             jax.ShapeDtypeStruct((2, width), full),
             jax.ShapeDtypeStruct((2, width), full),
-            jax.ShapeDtypeStruct((8, 128), full),
+            jax.ShapeDtypeStruct((1, 1), full),
         ),
         in_specs=[anywhere] * 7 + [inside] * 4,
         out_specs=(anywhere,) + (inside,) * 7,
@@ -1336,7 +1336,7 @@
     return finish(
         total_views,
         args,
-        loss[0, 0],
+        loss.reshape(()),
         input_grad,
         shard_proj_up,
         shard_proj_down,

time: 339 us -> 324 us (0.956)
  Pallas kernels: 325 us -> 310 us
    pallas_call x1, Pallas kernels: 325 us -> 310 us  [kernel_step(): pl.pallas_call(functools.partial(step_kernel, grid, total_views), out_sha...]
where the time goes in v5:
time: 324 us
  Pallas kernels  310 us (96%)
  other arithmetic  9.6 us (3%)
    pallas_call x1, Pallas kernels, kernel_step(): pl.pallas_call(functools.partial(step_kernel, grid, total_views), out_sha...  310 us

profile of v5, /device:TPU:0, one launch (start us, length us, event | category | flops | bytes accessed | tf_op | source)
XLA Modules:
  0.0 323.9 jit_solution(3500070902364617257)
XLA Ops:
  0.7 0.7 convert_bitcast_fusion
  1.3 0.7 copy.40
  2.1 309.9 %shard_map.344 = (bf16[4,2,128,1024]{3,2,1,0:T(8,128)(2,1)}, bf16[128,2048]{1,0:T(8,128)(2,1)}, bf16[16,2048]{1,0:T(8,128)(2,1)}, bf16[16,2048]{1,0:T(8,128)(2,1...) custom-call(bf16[1024,2048]{1,0:T(8,128)(2,1)} %x_hbm.1, ...), custom_call_target="tpu_custom_call" | custom-call | tf_op jit(solution)/shard_map/pallas_call | solution.py:1232
  312.0 0.0 copy-start
  312.0 0.0 copy-start.1
  312.0 0.0 copy-start.2
  312.1 0.0 copy-start.3
  312.1 4.2 %bitcast_convert_fusion = f32[1024,1024]{1,0:T(8,128)} fusion(bf16[4,2,128,1024]{3,2,1,0:T(8,128)(2,1)} %get-tuple-element.32), kind=kLoop, calls=%fused_computation | loop fusion | flops 1048576 | bytes 6291456 | tf_op jit(solution)/shard_map/reshape | solution.py:1333
  316.3 0.0 copy-start.10
  316.3 0.0 copy-start.17
  316.3 0.0 copy-start.18
  316.3 0.0 copy-done
  316.3 0.0 copy-done.1
  316.4 0.0 copy-done.2
  316.4 0.0 copy-done.3
  316.4 0.0 copy-start.22
  316.4 0.0 copy-start.21
  316.4 0.0 copy-start.11
  316.4 0.0 copy-start.12
  316.4 0.0 copy-start.13
  316.4 0.0 copy-start.19
  316.4 0.0 copy-start.20
  316.5 0.0 copy-start.4
  316.5 0.0 copy-start.8
  316.5 0.0 copy-start.16
  316.5 2.3 add_multiply_fusion
  318.8 0.0 copy-done.5
  318.8 0.0 copy-done.6
  318.8 0.0 copy-done.7
  318.8 0.0 copy-done.9
  318.8 0.0 copy-done.10
  318.8 0.0 copy-done.17
  318.8 0.0 copy-done.18
  318.9 0.9 add_multiply_fusion.1
  319.8 0.0 copy-done.22
  319.8 0.4 rev.6
  320.2 0.0 copy-start.14
  320.2 0.0 copy-done.21
  320.2 0.4 rev.7
  320.6 0.0 copy-done.11
  320.6 0.0 copy-done.12
  320.6 0.0 copy-done.13
  320.7 0.0 copy-done.19
  320.7 0.0 copy-done.20
  320.7 0.0 copy-start.15
  320.7 0.7 add_multiply_fusion.2
  321.4 0.0 copy-done.8
  321.4 0.8 multiply_subtract_fusion.2
  (8 shorter events, 0.0 us)
Async XLA Ops:
  312.0 4.3 %copy-start = (f32[128,2048]{1,0:T(8,128)S(1)}, f32[128,2048]{1,0:T(8,128)}, u32[]{:S(2)}) copy-start(f32[128,2048]{1,0:T(8,128)} %pu_hbm.1) | copy-start | bytes 3145732
  312.0 4.3 %copy-start.1 = (f32[128,2048]{1,0:T(8,128)S(1)}, f32[128,2048]{1,0:T(8,128)}, u32[]{:S(2)}) copy-start(f32[128,2048]{1,0:T(8,128)} %tu_hbm.1) | copy-start | bytes 3145732
  312.0 4.3 %copy-start.2 = (f32[128,2048]{1,0:T(8,128)S(1)}, f32[128,2048]{1,0:T(8,128)}, u32[]{:S(2)}) copy-start(f32[128,2048]{1,0:T(8,128)} %param.25) | copy-start | bytes 3145732
  312.1 4.3 %copy-start.3 = (bf16[128,2048]{1,0:T(8,128)(2,1)S(1)}, bf16[128,2048]{1,0:T(8,128)(2,1)}, u32[]{:S(2)}) copy-start(bf16[128,2048]{1,0:T(8,128)(2,1)} %get-tuple-element.33) | copy-start | bytes 1572868
  316.3 2.5 copy-start.5
  316.3 2.5 copy-start.6
  316.3 2.5 copy-start.7
  316.3 2.5 copy-start.9
  316.3 2.5 copy-start.10
  316.3 2.5 copy-start.17
  316.3 2.5 copy-start.18
  316.4 3.4 %copy-start.22 = (f32[2,2048]{1,0:T(2,128)S(1)}, f32[2,2048]{1,0:T(2,128)}, u32[]{:S(2)}) copy-start(f32[2,2048]{1,0:T(2,128)} %get-tuple-element.35) | copy-start | bytes 49156
  316.4 3.8 %copy-start.21 = (f32[2,2048]{1,0:T(2,128)S(1)}, f32[2,2048]{1,0:T(2,128)}, u32[]{:S(2)}) copy-start(f32[2,2048]{1,0:T(2,128)} %get-tuple-element.38) | copy-start | bytes 49156
  316.4 4.2 %copy-start.11 = (f32[2,2048]{1,0:T(2,128)S(1)}, f32[2,2048]{1,0:T(2,128)}, u32[]{:S(2)}) copy-start(f32[2,2048]{1,0:T(2,128)} %proj_norm.1) | copy-start | bytes 49156
  316.4 4.2 %copy-start.12 = (f32[2,2048]{1,0:T(2,128)S(1)}, f32[2,2048]{1,0:T(2,128)}, u32[]{:S(2)}) copy-start(f32[2,2048]{1,0:T(2,128)} %pred_norm.1) | copy-start | bytes 49156
  316.4 4.2 %copy-start.13 = (f32[2,2048]{1,0:T(2,128)S(1)}, f32[2,2048]{1,0:T(2,128)}, u32[]{:S(2)}) copy-start(f32[2,2048]{1,0:T(2,128)} %target_norm.1) | copy-start | bytes 49156
  316.4 4.2 %copy-start.19 = (f32[2,2048]{1,0:T(2,128)S(1)}, f32[2,2048]{1,0:T(2,128)}, u32[]{:S(2)}) copy-start(f32[2,2048]{1,0:T(2,128)} %param.27) | copy-start | bytes 49156
  316.4 4.2 %copy-start.20 = (f32[2,2048]{1,0:T(2,128)S(1)}, f32[2,2048]{1,0:T(2,128)}, u32[]{:S(2)}) copy-start(f32[2,2048]{1,0:T(2,128)} %param.30) | copy-start | bytes 49156
  316.5 4.9 %copy-start.4 = (f32[16,2048]{1,0:T(8,128)S(1)}, f32[16,2048]{1,0:T(8,128)}, u32[]{:S(2)}) copy-start(f32[16,2048]{1,0:T(8,128)} %qu_hbm.1) | copy-start | bytes 393220
  316.5 4.9 %copy-start.8 = (f32[16,2048]{1,0:T(8,128)S(1)}, f32[16,2048]{1,0:T(8,128)}, u32[]{:S(2)}) copy-start(f32[16,2048]{1,0:T(8,128)} %param.28) | copy-start | bytes 393220
  316.5 4.9 %copy-start.16 = (bf16[16,2048]{1,0:T(8,128)(2,1)S(1)}, bf16[16,2048]{1,0:T(8,128)(2,1)}, u32[]{:S(2)}) copy-start(bf16[16,2048]{1,0:T(8,128)(2,1)} %get-tuple-element.36) | copy-start | bytes 196612
  320.2 2.6 copy-start.14
  320.7 2.1 copy-start.15

commit v6 on v5

--- a/solution.py
+++ b/solution.py
@@ -643,13 +643,12 @@
             part = pl.ds(pl.multiple_of(b * rows, rows), rows)
             hat = (wide[part, columns] - mean) * inverse
             value = hat * gain + shift
+            value = value.astype(jnp.bfloat16)
             gate, square = gelu_parts(value)
-            act_ref[b // 2, b % 2, :, targets] = (value * gate).astype(jnp.bfloat16)
+            act_ref[b // 2, b % 2, :, targets] = value * gate
             if hat_ref is not None:
                 hat_ref[b // 2, b % 2, :, targets] = hat.astype(jnp.bfloat16)
-                slope1[b // 2, b % 2, :, targets] = gelu_slope(value, gate, square).astype(
-                    jnp.bfloat16
-                )
+                slope1[b // 2, b % 2, :, targets] = gelu_slope(value, gate, square)
 
         loop(blocks, one)
 
@@ -719,8 +718,9 @@
                 part = pl.ds(pl.multiple_of(b * rows, rows), rows)
                 hat = (wide[part, spare] - mean_n) * inverse_n
                 value = hat * gain + shift
+                value = value.astype(jnp.bfloat16)
                 gate, _ = gelu_parts(value)
-                act2[b // 2, b % 2, :, columns] = (value * gate).astype(jnp.bfloat16)
+                act2[b // 2, b % 2, :, columns] = value * gate
                 hat2[b // 2, b % 2, :, columns] = hat.astype(jnp.bfloat16)
 
             loop(blocks, tile)
@@ -1165,13 +1165,13 @@
     for g in (2, 3, 4):
         up_hidden(g)
     up_grad(2)
+    reduce_step("small", 2, 1)
     reduce_step("small", 1, 2)
     reduce_step("small", 0, 3)
     pl.semaphore_wait(ready, 1)
     send_part(0)
     reduce_step("up", 1, 1)
     up_grad(3)
-    reduce_step("small", 2, 1)
     send_part(1)
     send_part(2)
     reduce_step("up", 0, 1)

time: 324 us -> 321 us (level)
  no operation moved by 1% of the time
where the time goes in v6:
time: 321 us
  Pallas kernels  307 us (96%)
  other arithmetic  9.6 us (3%)
    pallas_call x1, Pallas kernels, kernel_step(): pl.pallas_call(functools.partial(step_kernel, grid, total_views), out_sha...  307 us

profile of v6, /device:TPU:0, one launch (start us, length us, event | category | flops | bytes accessed | tf_op | source)
XLA Modules:
  0.0 321.0 jit_solution(15943698362288166190)
XLA Ops:
  0.7 0.7 convert_bitcast_fusion
  1.3 0.7 copy.40
  2.1 307.0 %shard_map.344 = (bf16[4,2,128,1024]{3,2,1,0:T(8,128)(2,1)}, bf16[128,2048]{1,0:T(8,128)(2,1)}, bf16[16,2048]{1,0:T(8,128)(2,1)}, bf16[16,2048]{1,0:T(8,128)(2,1...) custom-call(bf16[1024,2048]{1,0:T(8,128)(2,1)} %x_hbm.1, ...), custom_call_target="tpu_custom_call" | custom-call | tf_op jit(solution)/shard_map/pallas_call | solution.py:1232
  309.1 0.0 copy-start
  309.1 0.0 copy-start.1
  309.1 0.0 copy-start.2
  309.1 0.0 copy-start.3
  309.1 4.2 %bitcast_convert_fusion = f32[1024,1024]{1,0:T(8,128)} fusion(bf16[4,2,128,1024]{3,2,1,0:T(8,128)(2,1)} %get-tuple-element.32), kind=kLoop, calls=%fused_computation | loop fusion | flops 1048576 | bytes 6291456 | tf_op jit(solution)/shard_map/reshape | solution.py:1333
  313.4 0.0 copy-start.10
  313.4 0.0 copy-start.17
  313.4 0.0 copy-start.18
  313.4 0.0 copy-done
  313.4 0.0 copy-done.1
  313.4 0.0 copy-done.2
  313.4 0.0 copy-done.3
  313.4 0.0 copy-start.22
  313.4 0.0 copy-start.21
  313.4 0.0 copy-start.11
  313.5 0.0 copy-start.12
  313.5 0.0 copy-start.13
  313.5 0.0 copy-start.19
  313.5 0.0 copy-start.20
  313.5 0.0 copy-start.4
  313.5 0.0 copy-start.8
  313.5 0.0 copy-start.16
  313.5 2.3 add_multiply_fusion
  315.9 0.0 copy-done.5
  315.9 0.0 copy-done.6
  315.9 0.0 copy-done.7
  315.9 0.0 copy-done.9
  315.9 0.0 copy-done.10
  315.9 0.0 copy-done.17
  315.9 0.0 copy-done.18
  315.9 0.9 add_multiply_fusion.1
  316.8 0.0 copy-done.22
  316.8 0.4 rev.6
  317.2 0.0 copy-start.14
  317.2 0.0 copy-done.21
  317.3 0.4 rev.7
  317.7 0.0 copy-done.11
  317.7 0.0 copy-done.12
  317.7 0.0 copy-done.13
  317.7 0.0 copy-done.19
  317.7 0.0 copy-start.15
  317.7 0.7 add_multiply_fusion.2
  318.4 0.8 multiply_subtract_fusion.2
  319.8 0.0 copy-done.14
  319.8 0.0 copy-done.15
  (8 shorter events, 0.0 us)
Async XLA Ops:
  309.1 4.3 %copy-start = (f32[128,2048]{1,0:T(8,128)S(1)}, f32[128,2048]{1,0:T(8,128)}, u32[]{:S(2)}) copy-start(f32[128,2048]{1,0:T(8,128)} %pu_hbm.1) | copy-start | bytes 3145732
  309.1 4.3 %copy-start.1 = (f32[128,2048]{1,0:T(8,128)S(1)}, f32[128,2048]{1,0:T(8,128)}, u32[]{:S(2)}) copy-start(f32[128,2048]{1,0:T(8,128)} %tu_hbm.1) | copy-start | bytes 3145732
  309.1 4.3 %copy-start.2 = (f32[128,2048]{1,0:T(8,128)S(1)}, f32[128,2048]{1,0:T(8,128)}, u32[]{:S(2)}) copy-start(f32[128,2048]{1,0:T(8,128)} %param.25) | copy-start | bytes 3145732
  309.1 4.3 %copy-start.3 = (bf16[128,2048]{1,0:T(8,128)(2,1)S(1)}, bf16[128,2048]{1,0:T(8,128)(2,1)}, u32[]{:S(2)}) copy-start(bf16[128,2048]{1,0:T(8,128)(2,1)} %get-tuple-element.33) | copy-start | bytes 1572868
  313.3 2.5 copy-start.5
  313.3 2.5 copy-start.6
  313.3 2.5 copy-start.7
  313.3 2.5 copy-start.9
  313.4 2.5 copy-start.10
  313.4 2.5 copy-start.17
  313.4 2.5 copy-start.18
  313.4 3.4 %copy-start.22 = (f32[2,2048]{1,0:T(2,128)S(1)}, f32[2,2048]{1,0:T(2,128)}, u32[]{:S(2)}) copy-start(f32[2,2048]{1,0:T(2,128)} %get-tuple-element.35) | copy-start | bytes 49156
  313.4 3.8 %copy-start.21 = (f32[2,2048]{1,0:T(2,128)S(1)}, f32[2,2048]{1,0:T(2,128)}, u32[]{:S(2)}) copy-start(f32[2,2048]{1,0:T(2,128)} %get-tuple-element.38) | copy-start | bytes 49156
  313.4 4.2 %copy-start.11 = (f32[2,2048]{1,0:T(2,128)S(1)}, f32[2,2048]{1,0:T(2,128)}, u32[]{:S(2)}) copy-start(f32[2,2048]{1,0:T(2,128)} %proj_norm.1) | copy-start | bytes 49156
  313.5 4.2 %copy-start.12 = (f32[2,2048]{1,0:T(2,128)S(1)}, f32[2,2048]{1,0:T(2,128)}, u32[]{:S(2)}) copy-start(f32[2,2048]{1,0:T(2,128)} %pred_norm.1) | copy-start | bytes 49156
  313.5 4.2 %copy-start.13 = (f32[2,2048]{1,0:T(2,128)S(1)}, f32[2,2048]{1,0:T(2,128)}, u32[]{:S(2)}) copy-start(f32[2,2048]{1,0:T(2,128)} %target_norm.1) | copy-start | bytes 49156
  313.5 4.2 %copy-start.19 = (f32[2,2048]{1,0:T(2,128)S(1)}, f32[2,2048]{1,0:T(2,128)}, u32[]{:S(2)}) copy-start(f32[2,2048]{1,0:T(2,128)} %param.27) | copy-start | bytes 49156
  313.5 4.2 %copy-start.20 = (f32[2,2048]{1,0:T(2,128)S(1)}, f32[2,2048]{1,0:T(2,128)}, u32[]{:S(2)}) copy-start(f32[2,2048]{1,0:T(2,128)} %param.30) | copy-start | bytes 49156
  313.5 4.9 %copy-start.4 = (f32[16,2048]{1,0:T(8,128)S(1)}, f32[16,2048]{1,0:T(8,128)}, u32[]{:S(2)}) copy-start(f32[16,2048]{1,0:T(8,128)} %qu_hbm.1) | copy-start | bytes 393220
  313.5 4.9 %copy-start.8 = (f32[16,2048]{1,0:T(8,128)S(1)}, f32[16,2048]{1,0:T(8,128)}, u32[]{:S(2)}) copy-start(f32[16,2048]{1,0:T(8,128)} %param.28) | copy-start | bytes 393220
  313.5 4.9 %copy-start.16 = (bf16[16,2048]{1,0:T(8,128)(2,1)S(1)}, bf16[16,2048]{1,0:T(8,128)(2,1)}, u32[]{:S(2)}) copy-start(bf16[16,2048]{1,0:T(8,128)(2,1)} %get-tuple-element.36) | copy-start | bytes 196612
  317.2 2.6 copy-start.14
  317.7 2.1 copy-start.15

commit v7 on v6

--- a/solution.py
+++ b/solution.py
@@ -1173,10 +1173,10 @@
     reduce_step("up", 1, 1)
     up_grad(3)
     send_part(1)
-    send_part(2)
-    reduce_step("up", 0, 1)
     reduce_step("up", 2, 1)
     up_grad(4)
+    reduce_step("up", 0, 1)
+    send_part(2)
     reduce_step("up", 1, 2)
     reduce_step("small", 2, 2)
     reduce_step("small", 1, 3)

time: 321 us -> 326 us (1.016)
  Pallas kernels: 307 us -> 312 us
    pallas_call x1, Pallas kernels: 307 us -> 312 us  [kernel_step(): pl.pallas_call(functools.partial(step_kernel, grid, total_views), out_sha...]
where the time goes in v7:
time: 326 us; the launch traced here: 325 us
  Pallas kernels  312 us (96%)
  other arithmetic  9.6 us (3%)
    pallas_call x1, Pallas kernels, kernel_step(): pl.pallas_call(functools.partial(step_kernel, grid, total_views), out_sha...  312 us

profile of v7, /device:TPU:0, one launch (start us, length us, event | category | flops | bytes accessed | tf_op | source)
XLA Modules:
  0.0 325.5 jit_solution(17047718758098470219)
XLA Ops:
  0.7 0.7 convert_bitcast_fusion
  1.3 0.7 copy.40
  2.1 311.5 %shard_map.344 = (bf16[4,2,128,1024]{3,2,1,0:T(8,128)(2,1)}, bf16[128,2048]{1,0:T(8,128)(2,1)}, bf16[16,2048]{1,0:T(8,128)(2,1)}, bf16[16,2048]{1,0:T(8,128)(2,1...) custom-call(bf16[1024,2048]{1,0:T(8,128)(2,1)} %x_hbm.1, ...), custom_call_target="tpu_custom_call" | custom-call | tf_op jit(solution)/shard_map/pallas_call | solution.py:1232
  313.6 0.0 copy-start
  313.6 0.0 copy-start.1
  313.6 0.0 copy-start.2
  313.6 0.0 copy-start.3
  313.6 4.2 %bitcast_convert_fusion = f32[1024,1024]{1,0:T(8,128)} fusion(bf16[4,2,128,1024]{3,2,1,0:T(8,128)(2,1)} %get-tuple-element.32), kind=kLoop, calls=%fused_computation | loop fusion | flops 1048576 | bytes 6291456 | tf_op jit(solution)/shard_map/reshape | solution.py:1333
  317.9 0.0 copy-start.10
  317.9 0.0 copy-start.17
  317.9 0.0 copy-start.18
  317.9 0.0 copy-done
  317.9 0.0 copy-done.1
  317.9 0.0 copy-done.2
  317.9 0.0 copy-done.3
  317.9 0.0 copy-start.22
  318.0 0.0 copy-start.21
  318.0 0.0 copy-start.11
  318.0 0.0 copy-start.12
  318.0 0.0 copy-start.13
  318.0 0.0 copy-start.19
  318.0 0.0 copy-start.20
  318.0 0.0 copy-start.4
  318.0 0.0 copy-start.8
  318.1 0.0 copy-start.16
  318.1 2.3 add_multiply_fusion
  320.4 0.0 copy-done.5
  320.4 0.0 copy-done.6
  320.4 0.0 copy-done.7
  320.4 0.0 copy-done.9
  320.4 0.0 copy-done.10
  320.4 0.0 copy-done.17
  320.4 0.0 copy-done.18
  320.4 0.9 add_multiply_fusion.1
  321.4 0.0 copy-done.22
  321.4 0.4 rev.6
  321.8 0.0 copy-start.14
  321.8 0.0 copy-done.21
  321.8 0.4 rev.7
  322.2 0.0 copy-done.11
  322.2 0.0 copy-done.12
  322.2 0.0 copy-done.13
  322.2 0.0 copy-start.15
  322.3 0.7 add_multiply_fusion.2
  322.9 0.0 copy-done.4
  322.9 0.8 multiply_subtract_fusion.2
  324.3 0.0 copy-done.14
  324.3 0.0 copy-done.15
  (8 shorter events, 0.0 us)
Async XLA Ops:
  313.6 4.3 %copy-start = (f32[128,2048]{1,0:T(8,128)S(1)}, f32[128,2048]{1,0:T(8,128)}, u32[]{:S(2)}) copy-start(f32[128,2048]{1,0:T(8,128)} %pu_hbm.1) | copy-start | bytes 3145732
  313.6 4.3 %copy-start.1 = (f32[128,2048]{1,0:T(8,128)S(1)}, f32[128,2048]{1,0:T(8,128)}, u32[]{:S(2)}) copy-start(f32[128,2048]{1,0:T(8,128)} %tu_hbm.1) | copy-start | bytes 3145732
  313.6 4.3 %copy-start.2 = (f32[128,2048]{1,0:T(8,128)S(1)}, f32[128,2048]{1,0:T(8,128)}, u32[]{:S(2)}) copy-start(f32[128,2048]{1,0:T(8,128)} %param.25) | copy-start | bytes 3145732
  313.6 4.3 %copy-start.3 = (bf16[128,2048]{1,0:T(8,128)(2,1)S(1)}, bf16[128,2048]{1,0:T(8,128)(2,1)}, u32[]{:S(2)}) copy-start(bf16[128,2048]{1,0:T(8,128)(2,1)} %get-tuple-element.33) | copy-start | bytes 1572868
  317.9 2.5 copy-start.5
  317.9 2.5 copy-start.6
  317.9 2.5 copy-start.7
  317.9 2.5 copy-start.9
  317.9 2.5 copy-start.10
  317.9 2.5 copy-start.17
  317.9 2.5 copy-start.18
  317.9 3.4 %copy-start.22 = (f32[2,2048]{1,0:T(2,128)S(1)}, f32[2,2048]{1,0:T(2,128)}, u32[]{:S(2)}) copy-start(f32[2,2048]{1,0:T(2,128)} %get-tuple-element.35) | copy-start | bytes 49156
  318.0 3.8 %copy-start.21 = (f32[2,2048]{1,0:T(2,128)S(1)}, f32[2,2048]{1,0:T(2,128)}, u32[]{:S(2)}) copy-start(f32[2,2048]{1,0:T(2,128)} %get-tuple-element.38) | copy-start | bytes 49156
  318.0 4.2 %copy-start.11 = (f32[2,2048]{1,0:T(2,128)S(1)}, f32[2,2048]{1,0:T(2,128)}, u32[]{:S(2)}) copy-start(f32[2,2048]{1,0:T(2,128)} %proj_norm.1) | copy-start | bytes 49156
  318.0 4.2 %copy-start.12 = (f32[2,2048]{1,0:T(2,128)S(1)}, f32[2,2048]{1,0:T(2,128)}, u32[]{:S(2)}) copy-start(f32[2,2048]{1,0:T(2,128)} %pred_norm.1) | copy-start | bytes 49156
  318.0 4.2 %copy-start.13 = (f32[2,2048]{1,0:T(2,128)S(1)}, f32[2,2048]{1,0:T(2,128)}, u32[]{:S(2)}) copy-start(f32[2,2048]{1,0:T(2,128)} %target_norm.1) | copy-start | bytes 49156
  318.0 4.2 %copy-start.19 = (f32[2,2048]{1,0:T(2,128)S(1)}, f32[2,2048]{1,0:T(2,128)}, u32[]{:S(2)}) copy-start(f32[2,2048]{1,0:T(2,128)} %param.27) | copy-start | bytes 49156
  318.0 4.2 %copy-start.20 = (f32[2,2048]{1,0:T(2,128)S(1)}, f32[2,2048]{1,0:T(2,128)}, u32[]{:S(2)}) copy-start(f32[2,2048]{1,0:T(2,128)} %param.30) | copy-start | bytes 49156
  318.0 4.9 %copy-start.4 = (f32[16,2048]{1,0:T(8,128)S(1)}, f32[16,2048]{1,0:T(8,128)}, u32[]{:S(2)}) copy-start(f32[16,2048]{1,0:T(8,128)} %qu_hbm.1) | copy-start | bytes 393220
  318.0 4.9 %copy-start.8 = (f32[16,2048]{1,0:T(8,128)S(1)}, f32[16,2048]{1,0:T(8,128)}, u32[]{:S(2)}) copy-start(f32[16,2048]{1,0:T(8,128)} %param.28) | copy-start | bytes 393220
  318.1 4.9 %copy-start.16 = (bf16[16,2048]{1,0:T(8,128)(2,1)S(1)}, bf16[16,2048]{1,0:T(8,128)(2,1)}, u32[]{:S(2)}) copy-start(bf16[16,2048]{1,0:T(8,128)(2,1)} %get-tuple-element.36) | copy-start | bytes 196612
  321.8 2.6 copy-start.14
  322.2 2.1 copy-start.15
